TPU v7x, 32 devices: a whole 2x2x4 slice. The times are simulated.
32 devices in a mesh: section: 2 (over core), dp: 4 (over z), tensor: 4 (over y, x).
Axes of the slice: x: 2, y: 2, z: 4, core: 2. Of those that a mesh axis runs over, the one named last changes fastest.
Arguments:
- activations: bfloat16 [2, 2, 4096, 1024], P('section', None, ('dp', 'tensor')), may hold values from -6 to 6
- starts: int32 [2, 4, 4], P(None, 'dp'), may hold values from 0 to 1023, as said below
- attention_weights: bfloat16 [2, 3, 1024, 1024], P('section', None, None, 'tensor'), may hold values from -0.1875 to 0.1875
- projection_weight: bfloat16 [2, 1024, 1024], P('section', 'tensor'), may hold values from -0.75 to 0.75
- feedforward_weight: bfloat16 [2, 1024, 4096], P('section', None, 'tensor'), may hold values from -0.1875 to 0.1875
- output_weight: bfloat16 [2, 4096, 1024], P('section', 'tensor'), may hold values from -0.09375 to 0.09375
- norm_gains: float32 [2, 2, 1024], P('section'), may hold values from 0.1 to 1.9
- norm_biases: float32 [2, 2, 1024], P('section'), may hold values from -3 to 3
- output_biases: float32 [2, 2, 1024], P('section'), may hold values from -3 to 3
- query_value_bias: float32 [2, 2, 1024], P('section', None, 'tensor'), may hold values from -3 to 3
- feedforward_bias: float32 [2, 4096], P('section', 'tensor'), may hold values from -3 to 3
- adapter_down_weight: bfloat16 [2, 2, 1024, 4], P('section'), may hold values from -0.1875 to 0.1875
- adapter_up_weight: bfloat16 [2, 2, 4, 1024], P('section', None, None, 'tensor'), may hold values from -0.1875 to 0.1875
Outputs:
- combined: float32 [2, 2, 4096, 1024], P('section', None, ('dp', 'tensor'))
- grad_lora_a: float32 [2, 2, 1024, 4], P('section')
- grad_lora_b: float32 [2, 2, 4, 1024], P('section', None, None, 'tensor')
Inputs may be any that keep to these rules, and one draw needn't show every extreme that they name: In each slot the first start is 0 and the 4 starts rise strictly, all below 1024.
All inputs are finite; a program needn't handle non-finite values.
Results may differ from a plain program's by a relative error of at most 0.0173.
Values may be sent and summed in bfloat16 or wider, within the bound.
No kernel may reach another device: no remote copies, remote signals or barrier semaphores. Data moves between devices by JAX's collectives and lax.ppermute only.
A program may use at most 192 MiB of HBM per device.

v0:
```python
import jax
import jax.numpy as jnp
from jax import lax
from jax.sharding import PartitionSpec as P

HEAD = 64
ADAPTER_RANK = 4
SEQ_LEN = 1024


adapter_scale = 8.0


def from_behind(block, axis, distance):
    devices = range(lax.axis_size(axis))
    route = [(i - distance, i) for i in devices if i - distance in devices]
    return lax.ppermute(block, axis, route)


def contract_axes(left, right, left_dim, right_dim):
    return lax.dot_general(
        left, right, (((left_dim,), (right_dim,)), ((), ())), preferred_element_type=jnp.float32
    )


def layer_norm(rows, gain, shift):
    mean = jnp.mean(rows, axis=-1, keepdims=True)
    centered = rows - mean
    spread = jnp.mean(centered * centered, axis=-1, keepdims=True)
    return centered * lax.rsqrt(spread + 1e-05) * gain + shift


def gelu_tanh(value):
    return (
        0.5
        * value
        * (1.0 + jnp.tanh(0.7978845608028654 * (value + 0.044715 * value * value * value)))
    )


def doc_mask(doc_starts):
    positions = jnp.arange(SEQ_LEN, dtype=jnp.int32)
    labels = jnp.sum((doc_starts[None, :] <= positions[:, None]).astype(jnp.int32), axis=1)
    return (positions[None, :] <= positions[:, None]) & (labels[:, None] == labels[None, :])


def masked_scores(query_rows, keys, doc_starts):
    scores = jnp.einsum(
        "qhd,khd->hqk", query_rows, keys, preferred_element_type=jnp.float32
    ) * HEAD ** (-0.5)
    return jnp.where(doc_mask(doc_starts)[None], scores, -1e30)


def attend(items):
    query_rows, keys, value_rows, doc_starts = items
    scores = masked_scores(query_rows, keys, doc_starts)
    top = jnp.max(scores, axis=-1, keepdims=True)
    weights = jnp.exp(scores - top)
    total = jnp.sum(weights, axis=-1, keepdims=True)
    mixed = jnp.einsum(
        "hqk,khd->qhd",
        (weights / total).astype(jnp.bfloat16),
        value_rows,
        preferred_element_type=jnp.float32,
    )
    return (mixed.astype(jnp.bfloat16), (top + jnp.log(total))[:, :, 0])


def attend_back(items):
    query_rows, keys, value_rows, doc_starts, log_totals, grad_mixed = items
    scores = masked_scores(query_rows, keys, doc_starts)
    probs = jnp.exp(scores - log_totals[:, :, None])
    grad_probs = jnp.einsum(
        "qhd,khd->hqk", grad_mixed, value_rows, preferred_element_type=jnp.float32
    )
    inner = jnp.sum(probs * grad_probs, axis=-1, keepdims=True)
    grad_scores = (probs * (grad_probs - inner)).astype(jnp.bfloat16)
    query_gradient = jnp.einsum(
        "hqk,khd->qhd", grad_scores, keys, preferred_element_type=jnp.float32
    ) * HEAD ** (-0.5)
    grad_k = jnp.einsum(
        "hqk,qhd->khd", grad_scores, query_rows, preferred_element_type=jnp.float32
    ) * HEAD ** (-0.5)
    value_gradient = jnp.einsum(
        "hqk,qhd->khd", probs.astype(jnp.bfloat16), grad_mixed, preferred_element_type=jnp.float32
    )
    return (
        query_gradient.astype(jnp.bfloat16),
        grad_k.astype(jnp.bfloat16),
        value_gradient.astype(jnp.bfloat16),
    )


def reduce_adapters(part_a, second_portion):
    return (lax.psum(part_a, ("dp", "tensor")), lax.psum(second_portion, "dp"))


def body(
    activations,
    starts,
    attention_weights,
    projection_weight,
    feedforward_weight,
    output_weight,
    norm_gains,
    norm_biases,
    output_biases,
    query_value_bias,
    feedforward_bias,
    adapter_down_weight,
    adapter_up_weight,
):
    section = lax.axis_index("section")
    first = section == 0
    batches = activations.shape[1]
    own_rows = activations.shape[2]
    width = activations.shape[3]
    head_cols = projection_weight.shape[1]
    local_heads = head_cols // HEAD
    shaped = (-1, SEQ_LEN, local_heads, HEAD)
    w_cat = jnp.concatenate(
        [attention_weights[0, 0], attention_weights[0, 1], attention_weights[0, 2]], axis=1
    )
    stacked_down_maps = jnp.concatenate(
        [adapter_down_weight[0, 0], adapter_down_weight[0, 1]], axis=1
    )

    def forward_relay(rows, group_starts):
        normalized_rows = layer_norm(rows, norm_gains[0, 0], norm_biases[0, 0]).astype(jnp.bfloat16)
        gathered = lax.all_gather(normalized_rows, "tensor", axis=0, tiled=True)
        joined = jnp.dot(gathered, w_cat, preferred_element_type=jnp.float32)
        apply_adapter = jnp.dot(
            gathered, stacked_down_maps, preferred_element_type=jnp.float32
        ).astype(jnp.bfloat16)
        query_rows = (
            joined[:, :head_cols]
            + query_value_bias[0, 0]
            + adapter_scale
            * jnp.dot(
                apply_adapter[:, :ADAPTER_RANK],
                adapter_up_weight[0, 0],
                preferred_element_type=jnp.float32,
            )
        ).astype(jnp.bfloat16)
        keys = joined[:, head_cols : 2 * head_cols].astype(jnp.bfloat16)
        value_rows = (
            joined[:, 2 * head_cols :]
            + query_value_bias[0, 1]
            + adapter_scale
            * jnp.dot(
                apply_adapter[:, ADAPTER_RANK:],
                adapter_up_weight[0, 1],
                preferred_element_type=jnp.float32,
            )
        ).astype(jnp.bfloat16)
        mixed, log_totals = lax.map(
            attend,
            (
                query_rows.reshape(shaped),
                keys.reshape(shaped),
                value_rows.reshape(shaped),
                group_starts,
            ),
        )
        mixed = mixed.reshape(-1, head_cols)
        middle = (
            rows
            + lax.psum_scatter(
                jnp.dot(mixed, projection_weight[0], preferred_element_type=jnp.float32),
                "tensor",
                scatter_dimension=0,
                tiled=True,
            )
            + output_biases[0, 0]
        )
        normed_two = layer_norm(middle, norm_gains[0, 1], norm_biases[0, 1]).astype(jnp.bfloat16)
        hidden = (
            jnp.dot(
                lax.all_gather(normed_two, "tensor", axis=0, tiled=True),
                feedforward_weight[0],
                preferred_element_type=jnp.float32,
            )
            + feedforward_bias[0]
        )
        active = gelu_tanh(hidden).astype(jnp.bfloat16)
        output = (
            middle
            + lax.psum_scatter(
                jnp.dot(active, output_weight[0], preferred_element_type=jnp.float32).astype(
                    jnp.bfloat16
                ),
                "tensor",
                scatter_dimension=0,
                tiled=True,
            ).astype(jnp.float32)
            + output_biases[0, 1]
        )
        return (
            output,
            (
                rows,
                middle,
                gathered,
                apply_adapter,
                query_rows,
                keys,
                value_rows,
                log_totals,
                hidden,
            ),
        )

    def backward_relay(grad_rows, cache, group_starts):
        rows, middle, gathered, apply_adapter, query_rows, keys, value_rows, log_totals, hidden = (
            cache
        )
        grad_active = contract_axes(
            lax.all_gather(grad_rows.astype(jnp.bfloat16), "tensor", axis=0, tiled=True),
            output_weight[0],
            1,
            1,
        )
        _, gelu_back = jax.vjp(gelu_tanh, hidden)
        grad_hidden = gelu_back(grad_active)[0].astype(jnp.bfloat16)
        grad_normed_two = lax.psum_scatter(
            contract_axes(grad_hidden, feedforward_weight[0], 1, 1).astype(jnp.bfloat16),
            "tensor",
            scatter_dimension=0,
            tiled=True,
        ).astype(jnp.float32)
        _, norm_two_back = jax.vjp(
            lambda inner_rows: layer_norm(inner_rows, norm_gains[0, 1], norm_biases[0, 1]), middle
        )
        grad_middle = grad_rows + norm_two_back(grad_normed_two)[0]
        grad_mixed = contract_axes(
            lax.all_gather(grad_middle.astype(jnp.bfloat16), "tensor", axis=0, tiled=True),
            projection_weight[0],
            1,
            1,
        ).astype(jnp.bfloat16)
        query_gradient, grad_k, value_gradient = lax.map(
            attend_back,
            (
                query_rows.reshape(shaped),
                keys.reshape(shaped),
                value_rows.reshape(shaped),
                group_starts,
                log_totals,
                grad_mixed.reshape(shaped),
            ),
        )
        query_gradient = query_gradient.reshape(-1, head_cols)
        grad_k = grad_k.reshape(-1, head_cols)
        value_gradient = value_gradient.reshape(-1, head_cols)
        grad_low = jnp.concatenate(
            [
                adapter_scale * contract_axes(query_gradient, adapter_up_weight[0, 0], 1, 1),
                adapter_scale * contract_axes(value_gradient, adapter_up_weight[0, 1], 1, 1),
            ],
            axis=1,
        ).astype(jnp.bfloat16)
        grad_joined = jnp.concatenate([query_gradient, grad_k, value_gradient], axis=1)
        grad_normed = lax.psum_scatter(
            (
                contract_axes(grad_joined, w_cat, 1, 1)
                + contract_axes(grad_low, stacked_down_maps, 1, 1)
            ).astype(jnp.bfloat16),
            "tensor",
            scatter_dimension=0,
            tiled=True,
        ).astype(jnp.float32)
        _, norm_back = jax.vjp(
            lambda inner_rows: layer_norm(inner_rows, norm_gains[0, 0], norm_biases[0, 0]), rows
        )
        grad_in = grad_middle + norm_back(grad_normed)[0]
        grad_down = contract_axes(gathered, grad_low, 0, 0)
        part_a = jnp.stack([grad_down[:, :ADAPTER_RANK], grad_down[:, ADAPTER_RANK:]])
        second_portion = adapter_scale * jnp.stack(
            [
                contract_axes(apply_adapter[:, :ADAPTER_RANK], query_gradient, 0, 0),
                contract_axes(apply_adapter[:, ADAPTER_RANK:], value_gradient, 0, 0),
            ]
        )
        return (grad_in, part_a, second_portion)

    received = jnp.zeros((own_rows, width), jnp.bfloat16)
    finals = []
    stored = []
    for tick in range(batches + 1):
        batch_index = jnp.clip(tick - section, 0, batches - 1)
        own = lax.dynamic_index_in_dim(activations[0], batch_index, 0, keepdims=False)
        rows = jnp.where(first, own, received).astype(jnp.float32)
        group_starts = lax.dynamic_index_in_dim(starts, batch_index, 0, keepdims=False)
        output, cache = forward_relay(rows, group_starts)
        finals.append(output)
        stored.append(rows)
        if tick < batches:
            received = from_behind(output.astype(jnp.bfloat16), "section", 1)
    stacked = jax.tree.map(lambda *items: jnp.stack(items), *stored)
    returned = jnp.zeros((own_rows, width), jnp.bfloat16)
    totals_a = jnp.zeros((2, width, ADAPTER_RANK), jnp.float32)
    totals_b = jnp.zeros((2, ADAPTER_RANK, head_cols), jnp.float32)
    grads_in = []
    for tick in range(batches + 1):
        position = tick - 1 + section
        batch_index = jnp.clip(position, 0, batches - 1)
        valid = ((position >= 0) & (position < batches)).astype(jnp.float32)
        own = lax.dynamic_index_in_dim(activations[0], batch_index, 0, keepdims=False)
        grad_rows = jnp.where(first, returned, own).astype(jnp.float32) * valid
        group_starts = lax.dynamic_index_in_dim(starts, batch_index, 0, keepdims=False)
        slot_index = jnp.clip(tick - 1 + 2 * section, 0, batches)
        picked = lax.dynamic_index_in_dim(stacked, slot_index, 0, keepdims=False)
        _, cache = forward_relay(picked, group_starts)
        grad_in, part_a, second_portion = backward_relay(grad_rows, cache, group_starts)
        grads_in.append(grad_in)
        if tick < batches:
            returned = from_behind(grad_in.astype(jnp.bfloat16), "section", -1)
        part_a, second_portion = reduce_adapters(part_a, second_portion)
        totals_a = totals_a + part_a
        totals_b = totals_b + second_portion
    combined = jnp.stack(
        [jnp.where(first, grads_in[index + 1], finals[index + 1]) for index in range(batches)]
    )
    return (combined[None], totals_a[None], totals_b[None])


def solution(mesh):
    placed = (
        P("section", None, ("dp", "tensor"), None),
        P(None, "dp", None),
        P("section", None, None, "tensor"),
        P("section", "tensor", None),
        P("section", None, "tensor"),
        P("section", "tensor", None),
        P("section", None, None),
        P("section", None, None),
        P("section", None, None),
        P("section", None, "tensor"),
        P("section", "tensor"),
        P("section", None, None, None),
        P("section", None, None, "tensor"),
    )
    return jax.shard_map(
        body,
        mesh=mesh,
        in_specs=placed,
        out_specs=(
            P("section", None, ("dp", "tensor"), None),
            P("section", None, None, None),
            P("section", None, None, "tensor"),
        ),
        check_vma=False,
    )
```

profile of v0, /device:TPU:0, one launch (start us, length us, event | category | flops | bytes accessed | tf_op | source)
XLA Modules:
  0.0 1687.8 jit_solution(10173065813340421367)
XLA Ops:
  20.8 32.0 %all-gather.19.cloned.1.call-done = bf16[1024,1024]{1,0:T(8,128)(2,1)} async-done(((bf16[256,1024]{1,0:T(8,128)(2,1)}), bf16[1024,1024]{1,0:T(8,128)(2,1)}) %all-gather.19.cloned.1.call-update) | async-done | bytes 2097168 | tf_op jit(solution)/shard_map/all_gather | solution.py:130
  82.7 52.2 %reduce-scatter.16.cloned.1.call-done = f32[256,1024]{1,0:T(8,128)} async-done(((f32[1024,1024]{1,0:T(8,128)}), f32[256,1024]{1,0:T(8,128)}) %reduce-scatter.16.cloned.1.call-update) | async-done | bytes 1048592 | tf_op jit(solution)/shard_map/reduce_scatter | solution.py:168
  140.6 35.1 %all-gather.21.cloned.1.call-done = bf16[1024,1024]{1,0:T(8,128)(2,1)} async-done(((bf16[256,1024]{1,0:T(8,128)(2,1)}), bf16[1024,1024]{1,0:T(8,128)(2,1)}) %all-gather.21.cloned.1.call-update) | async-done | bytes 2097168 | tf_op jit(solution)/shard_map/all_gather | solution.py:179
  184.1 35.3 %reduce-scatter.18.cloned.1.call-done = bf16[256,1024]{1,0:T(8,128)(2,1)} async-done(((bf16[1024,1024]{1,0:T(8,128)(2,1)}), bf16[256,1024]{1,0:T(8,128)(2,1)}) %reduce-scatter.18.cloned.1.call-update) | async-done | bytes 524304 | tf_op jit(solution)/shard_map/reduce_scatter | solution.py:188
  229.0 33.8 %all-gather.23.cloned.1.call-done = bf16[1024,1024]{1,0:T(8,128)(2,1)} async-done(((bf16[256,1024]{1,0:T(8,128)(2,1)}), bf16[1024,1024]{1,0:T(8,128)(2,1)}) %all-gather.23.cloned.1.call-update) | async-done | bytes 2097168 | tf_op jit(solution)/shard_map/all_gather | solution.py:130
  292.4 52.8 %reduce-scatter.20.cloned.1.call-done = f32[256,1024]{1,0:T(8,128)} async-done(((f32[1024,1024]{1,0:T(8,128)}), f32[256,1024]{1,0:T(8,128)}) %reduce-scatter.20.cloned.1.call-update) | async-done | bytes 1048592 | tf_op jit(solution)/shard_map/reduce_scatter | solution.py:168
  392.5 35.3 %reduce-scatter.22.cloned.1.call-done = bf16[256,1024]{1,0:T(8,128)(2,1)} async-done(((bf16[1024,1024]{1,0:T(8,128)(2,1)}), bf16[256,1024]{1,0:T(8,128)(2,1)}) %reduce-scatter.22.cloned.1.call-update) | async-done | bytes 524304 | tf_op jit(solution)/shard_map/reduce_scatter | solution.py:188
  439.5 34.8 %all-gather.27.cloned.1.call-done = bf16[1024,1024]{1,0:T(8,128)(2,1)} async-done(((bf16[256,1024]{1,0:T(8,128)(2,1)}), bf16[1024,1024]{1,0:T(8,128)(2,1)}) %all-gather.27.cloned.1.call-update) | async-done | bytes 2097168 | tf_op jit(solution)/shard_map/all_gather | solution.py:130
  505.7 52.8 %reduce-scatter.24.cloned.1.call-done = f32[256,1024]{1,0:T(8,128)} async-done(((f32[1024,1024]{1,0:T(8,128)}), f32[256,1024]{1,0:T(8,128)}) %reduce-scatter.24.cloned.1.call-update) | async-done | bytes 1048592 | tf_op jit(solution)/shard_map/reduce_scatter | solution.py:168
  563.3 34.4 %all-gather.29.cloned.1.call-done = bf16[1024,1024]{1,0:T(8,128)(2,1)} async-done(((bf16[256,1024]{1,0:T(8,128)(2,1)}), bf16[1024,1024]{1,0:T(8,128)(2,1)}) %all-gather.29.cloned.1.call-update) | async-done | bytes 2097168 | tf_op jit(solution)/shard_map/all_gather | solution.py:179
  603.6 31.3 %all-gather.31.cloned.1.call-done = bf16[1024,1024]{1,0:T(8,128)(2,1)} async-done(((bf16[256,1024]{1,0:T(8,128)(2,1)}), bf16[1024,1024]{1,0:T(8,128)(2,1)}) %all-gather.31.cloned.1.call-update) | async-done | bytes 2097168 | tf_op jit(solution)/shard_map/all_gather | solution.py:218
  645.2 35.3 %reduce-scatter.26.cloned.1.call-done = bf16[256,1024]{1,0:T(8,128)(2,1)} async-done(((bf16[1024,1024]{1,0:T(8,128)(2,1)}), bf16[256,1024]{1,0:T(8,128)(2,1)}) %reduce-scatter.26.cloned.1.call-update) | async-done | bytes 524304 | tf_op jit(solution)/shard_map/reduce_scatter | solution.py:225
  686.0 35.4 %all-gather.33.cloned.1.call-done = bf16[1024,1024]{1,0:T(8,128)(2,1)} async-done(((bf16[256,1024]{1,0:T(8,128)(2,1)}), bf16[1024,1024]{1,0:T(8,128)(2,1)}) %all-gather.33.cloned.1.call-update) | async-done | bytes 2097168 | tf_op jit(solution)/shard_map/all_gather | solution.py:236
  765.9 35.3 %reduce-scatter.28.cloned.1.call-done = bf16[256,1024]{1,0:T(8,128)(2,1)} async-done(((bf16[1024,1024]{1,0:T(8,128)(2,1)}), bf16[256,1024]{1,0:T(8,128)(2,1)}) %reduce-scatter.28.cloned.1.call-update) | async-done | bytes 524304 | tf_op jit(solution)/shard_map/reduce_scatter | solution.py:263
  809.9 33.7 %all-gather.35.cloned.1.call-done = bf16[1024,1024]{1,0:T(8,128)(2,1)} async-done(((bf16[256,1024]{1,0:T(8,128)(2,1)}), bf16[1024,1024]{1,0:T(8,128)(2,1)}) %all-gather.35.cloned.1.call-update) | async-done | bytes 2097168 | tf_op jit(solution)/shard_map/all_gather | solution.py:130
  875.1 52.8 %reduce-scatter.30.cloned.1.call-done = f32[256,1024]{1,0:T(8,128)} async-done(((f32[1024,1024]{1,0:T(8,128)}), f32[256,1024]{1,0:T(8,128)}) %reduce-scatter.30.cloned.1.call-update) | async-done | bytes 1048592 | tf_op jit(solution)/shard_map/reduce_scatter | solution.py:168
  1015.1 34.9 %reduce-scatter.32.cloned.1.call-done = bf16[256,1024]{1,0:T(8,128)(2,1)} async-done(((bf16[1024,1024]{1,0:T(8,128)(2,1)}), bf16[256,1024]{1,0:T(8,128)(2,1)}) %reduce-scatter.32.cloned.1.call-update) | async-done | bytes 524304 | tf_op jit(solution)/shard_map/reduce_scatter | solution.py:225
  1055.0 35.4 %all-gather.41.cloned.1.call-done = bf16[1024,1024]{1,0:T(8,128)(2,1)} async-done(((bf16[256,1024]{1,0:T(8,128)(2,1)}), bf16[1024,1024]{1,0:T(8,128)(2,1)}) %all-gather.41.cloned.1.call-update) | async-done | bytes 2097168 | tf_op jit(solution)/shard_map/all_gather | solution.py:236
  1135.4 34.8 %reduce-scatter.34.cloned.1.call-done = bf16[256,1024]{1,0:T(8,128)(2,1)} async-done(((bf16[1024,1024]{1,0:T(8,128)(2,1)}), bf16[256,1024]{1,0:T(8,128)(2,1)}) %reduce-scatter.34.cloned.1.call-update) | async-done | bytes 524304 | tf_op jit(solution)/shard_map/reduce_scatter | solution.py:263
  1178.5 33.6 %all-gather.51.cloned.1.call-done = bf16[1024,1024]{1,0:T(8,128)(2,1)} async-done(((bf16[256,1024]{1,0:T(8,128)(2,1)}), bf16[1024,1024]{1,0:T(8,128)(2,1)}) %all-gather.51.cloned.1.call-update) | async-done | bytes 2097168 | tf_op jit(solution)/shard_map/all_gather | solution.py:130
  1306.4 54.4 %reduce-scatter.36.cloned.1.call-done = f32[256,1024]{1,0:T(8,128)} async-done(((f32[1024,1024]{1,0:T(8,128)}), f32[256,1024]{1,0:T(8,128)}) %reduce-scatter.36.cloned.1.call-update) | async-done | bytes 1048592 | tf_op jit(solution)/shard_map/reduce_scatter | solution.py:168
  1448.0 35.3 %reduce-scatter.38.cloned.1.call-done = bf16[256,1024]{1,0:T(8,128)(2,1)} async-done(((bf16[1024,1024]{1,0:T(8,128)(2,1)}), bf16[256,1024]{1,0:T(8,128)(2,1)}) %reduce-scatter.38.cloned.1.call-update) | async-done | bytes 524304 | tf_op jit(solution)/shard_map/reduce_scatter | solution.py:225
  1488.9 34.7 %all-gather.49.cloned.1.call-done = bf16[1024,1024]{1,0:T(8,128)(2,1)} async-done(((bf16[256,1024]{1,0:T(8,128)(2,1)}), bf16[1024,1024]{1,0:T(8,128)(2,1)}) %all-gather.49.cloned.1.call-update) | async-done | bytes 2097168 | tf_op jit(solution)/shard_map/all_gather | solution.py:236
  1598.9 73.8 %psum.49 = f32[2,1024,4]{1,2,0:T(4,128)} all-reduce(f32[2,1024,4]{1,2,0:T(4,128)S(1)} %fusion.293), channel_id=1, replica_groups=mesh['section'=2,'dp'=4,'tensor'=4] {'dp','tensor'}, use_global_device_ids=true, to_apply=%region_72.73 | all-reduce | flops 8192 | bytes 65536 | tf_op jit(solution)/shard_map/psum | solution.py:95
  (648 shorter events, 711.4 us)
Async XLA Ops:
  14.7 120.2 %reduce-scatter.16.cloned.1.call-start = ((), (), s32[]{:S(2)}) async-start(), calls=%async_computation.16 | async-start | bytes 5242880 | tf_op jit(solution)/shard_map/reduce_scatter | solution.py:168
  82.0 93.7 %all-gather.21.cloned.1.call-start = ((), (), s32[]{:S(2)}) async-start(), calls=%async_computation.17 | async-start | bytes 2621440 | tf_op jit(solution)/shard_map/all_gather | solution.py:179
  140.3 79.0 %reduce-scatter.18.cloned.1.call-start = ((), (), s32[]{:S(2)}) async-start(), calls=%async_computation.18 | async-start | bytes 2621440 | tf_op jit(solution)/shard_map/reduce_scatter | solution.py:188
  184.0 78.8 %all-gather.23.cloned.1.call-start = ((), (), s32[]{:S(2)}) async-start(), calls=%async_computation.19 | async-start | bytes 2621440 | tf_op jit(solution)/shard_map/all_gather | solution.py:130
  227.3 117.9 %reduce-scatter.20.cloned.1.call-start = ((), (), s32[]{:S(2)}) async-start(), calls=%async_computation.20 | async-start | bytes 5242880 | tf_op jit(solution)/shard_map/reduce_scatter | solution.py:168
  292.3 91.9 %all-gather.25.cloned.1.call-start = ((), (), s32[]{:S(2)}) async-start(), calls=%async_computation.21 | async-start | bytes 2621440 | tf_op jit(solution)/shard_map/all_gather | solution.py:179
  348.7 79.1 %reduce-scatter.22.cloned.1.call-start = ((), (), s32[]{:S(2)}) async-start(), calls=%async_computation.22 | async-start | bytes 2621440 | tf_op jit(solution)/shard_map/reduce_scatter | solution.py:188
  392.5 81.8 %all-gather.27.cloned.1.call-start = ((), (), s32[]{:S(2)}) async-start(), calls=%async_computation.23 | async-start | bytes 2621440 | tf_op jit(solution)/shard_map/all_gather | solution.py:130
  437.8 120.7 %reduce-scatter.24.cloned.1.call-start = ((), (), s32[]{:S(2)}) async-start(), calls=%async_computation.24 | async-start | bytes 5242880 | tf_op jit(solution)/shard_map/reduce_scatter | solution.py:168
  505.6 92.1 %all-gather.29.cloned.1.call-start = ((), (), s32[]{:S(2)}) async-start(), calls=%async_computation.25 | async-start | bytes 2621440 | tf_op jit(solution)/shard_map/all_gather | solution.py:179
  562.8 117.7 %reduce-scatter.26.cloned.1.call-start = ((), (), s32[]{:S(2)}) async-start(), calls=%async_computation.27 | async-start | bytes 2621440 | tf_op jit(solution)/shard_map/reduce_scatter | solution.py:225
  685.9 115.2 %reduce-scatter.28.cloned.1.call-start = ((), (), s32[]{:S(2)}) async-start(), calls=%async_computation.29 | async-start | bytes 2621440 | tf_op jit(solution)/shard_map/reduce_scatter | solution.py:263
  765.8 77.8 %all-gather.35.cloned.1.call-start = ((), (), s32[]{:S(2)}) async-start(), calls=%async_computation.30 | async-start | bytes 2621440 | tf_op jit(solution)/shard_map/all_gather | solution.py:130
  808.1 119.8 %reduce-scatter.30.cloned.1.call-start = ((), (), s32[]{:S(2)}) async-start(), calls=%async_computation.31 | async-start | bytes 5242880 | tf_op jit(solution)/shard_map/reduce_scatter | solution.py:168
  875.1 92.1 %all-gather.37.cloned.1.call-start = ((), (), s32[]{:S(2)}) async-start(), calls=%async_computation.32 | async-start | bytes 2621440 | tf_op jit(solution)/shard_map/all_gather | solution.py:179
  938.2 111.8 %reduce-scatter.32.cloned.1.call-start = ((), (), s32[]{:S(2)}) async-start(), calls=%async_computation.34 | async-start | bytes 2621440 | tf_op jit(solution)/shard_map/reduce_scatter | solution.py:225
  1054.9 115.3 %reduce-scatter.34.cloned.1.call-start = ((), (), s32[]{:S(2)}) async-start(), calls=%async_computation.36 | async-start | bytes 2621440 | tf_op jit(solution)/shard_map/reduce_scatter | solution.py:263
  1178.5 126.4 %reduce-scatter.42.cloned.1.call-start = ((), (), s32[]{:S(2)}) async-start(), calls=%async_computation.45 | async-start | bytes 5242880 | tf_op jit(solution)/shard_map/reduce_scatter | solution.py:168
  1241.0 119.8 %reduce-scatter.36.cloned.1.call-start = ((), (), s32[]{:S(2)}) async-start(), calls=%async_computation.38 | async-start | bytes 5242880 | tf_op jit(solution)/shard_map/reduce_scatter | solution.py:168
  1282.0 118.4 %all-gather.45.cloned.1.call-start = ((), (), s32[]{:S(2)}) async-start(), calls=%async_computation.39 | async-start | bytes 2621440 | tf_op jit(solution)/shard_map/all_gather | solution.py:179
  1375.6 107.7 %reduce-scatter.38.cloned.1.call-start = ((), (), s32[]{:S(2)}) async-start(), calls=%async_computation.41 | async-start | bytes 2621440 | tf_op jit(solution)/shard_map/reduce_scatter | solution.py:225
  1488.1 81.6 %all-gather.53.cloned.1.call-start = ((), (), s32[]{:S(2)}) async-start(), calls=%async_computation.46 | async-start | bytes 2621440 | tf_op jit(solution)/shard_map/all_gather | solution.py:179
  1488.9 183.8 %reduce-scatter.40.cloned.1.call-start = ((), (), s32[]{:S(2)}) async-start(), calls=%async_computation.43 | async-start | bytes 2621440 | tf_op jit(solution)/shard_map/reduce_scatter | solution.py:263
  1569.4 106.8 %reduce-scatter.44.cloned.1.call-start = ((), (), s32[]{:S(2)}) async-start(), calls=%async_computation.47 | async-start | bytes 2621440 | tf_op jit(solution)/shard_map/reduce_scatter | solution.py:188
  (185 other events, 6974.9 us)
Sparse Core Ops, SparseCore 0:
  14.8 38.0 all-gather.18
  82.2 52.6 reduce-scatter.15
  227.4 35.3 all-gather.22
  292.4 52.6 reduce-scatter.19
  348.9 35.2 all-gather.24
  437.9 36.3 all-gather.26
  505.7 52.6 reduce-scatter.23
  562.4 35.2 all-gather.28
  599.5 35.2 all-gather.30
  686.1 35.2 all-gather.32
  808.3 35.3 all-gather.34
  875.2 52.6 reduce-scatter.29
  931.9 35.2 all-gather.36
  969.1 35.2 all-gather.38
  1055.0 35.2 all-gather.40
  1176.8 35.2 all-gather.50
  1213.9 35.2 all-gather.42
  1252.2 52.6 reduce-scatter.41
  1308.0 52.6 reduce-scatter.35
  1365.0 35.2 all-gather.44
  1402.2 35.3 all-gather.46
  1488.3 35.2 all-gather.48
  1525.6 35.2 all-gather.52
  1608.1 36.1 reduce-scatter.43
  (9 shorter events, 316.4 us)
where the time goes:
time: 1700 us; the launch traced here: 1690 us
  waiting for transfers between devices  1060 us (62%)
  matrix products  339 us (20%)
  other arithmetic  139 us (8%)
  blocking collectives  86.2 us (5%)
  local copies, waits for them, and re-layouts  21.4 us (1%)
  starting transfers between devices  20.4 us (1%)
  between operations  17.2 us (1%)
    reduce_scatter x6, waiting for transfers between devices, forward_relay(): lax.psum_scatter(jnp.dot(mixed, projection_weight[0], preferred_element_t...  288 us
    all_gather x6, waiting for transfers between devices, forward_relay(): gathered = lax.all_gather(normalized_rows, 'tensor', axis=0, tiled=True)  174 us
    all_gather x6, waiting for transfers between devices, forward_relay(): lax.all_gather(normed_two, 'tensor', axis=0, tiled=True)  148 us
    reduce_scatter x3, waiting for transfers between devices, backward_relay(): lax.psum_scatter(contract_axes(grad_hidden, feedforward_weight[0], 1, 1)....  106 us
    all_gather x3, waiting for transfers between devices, backward_relay(): lax.all_gather(grad_middle.astype(jnp.bfloat16), 'tensor', axis=0, tiled=...  105 us
    all_gather x3, waiting for transfers between devices, backward_relay(): lax.all_gather(grad_rows.astype(jnp.bfloat16), 'tensor', axis=0, tiled=True)  93.8 us
    psum x2, blocking collectives, reduce_adapters(): return (lax.psum(part_a, ('dp', 'tensor')), lax.psum(second_portion, 'dp'))  86.2 us
    reduce_scatter x3, waiting for transfers between devices, forward_relay(): lax.psum_scatter(jnp.dot(active, output_weight[0], preferred_element_type...  70.6 us
  transfers between devices with their start and end apart: 37, of which 34 were waited for; matrix products, arithmetic and copies ran while one was open for 10% of the time, Pallas kernels for 0%

commit v1 on v0

--- a/solution.py
+++ b/solution.py
@@ -1,6 +1,10 @@
+import functools
+
 import jax
 import jax.numpy as jnp
 from jax import lax
+from jax.experimental import pallas as pl
+from jax.experimental.pallas import tpu as pltpu
 from jax.sharding import PartitionSpec as P
 
 HEAD = 64
@@ -95,7 +99,7 @@
     return (lax.psum(part_a, ("dp", "tensor")), lax.psum(second_portion, "dp"))
 
 
-def body(
+def plain_body(
     activations,
     starts,
     attention_weights,
@@ -324,6 +328,707 @@
     return (combined[None], totals_a[None], totals_b[None])
 
 
+LOW = 2 * ADAPTER_RANK
+VMEM_SPACE = pl.BlockSpec(memory_space=pltpu.VMEM)
+SMEM_SPACE = pl.BlockSpec(memory_space=pltpu.SMEM)
+HBM_SPACE = pl.BlockSpec(memory_space=pl.ANY)
+BLOCK = 256
+
+
+def send(block, route):
+    pairs = []
+    for s in range(2):
+        for t in range(4):
+            to = route(s, t)
+            if to is not None:
+                pairs.append((s * 4 + t, to[0] * 4 + to[1]))
+    return lax.ppermute(block, ("section", "tensor"), pairs)
+
+
+def other_core(block):
+    return send(block, lambda s, t: (1 - s, t))
+
+
+def x_swap(block):
+    return send(block, lambda s, t: (s, t ^ 1))
+
+
+def y_swap(block):
+    return send(block, lambda s, t: (s, t ^ 2))
+
+
+def deal(source, same_chip, cross_chip):
+    return (
+        send(same_chip, lambda s, t: (t >> 1, t) if s == source else None),
+        send(cross_chip, lambda s, t: (t >> 1, t ^ 2) if s == source else None),
+    )
+
+
+def collect(target, same_chip, cross_chip):
+    return (
+        send(same_chip, lambda s, t: (target, t) if s == t >> 1 else None),
+        send(cross_chip, lambda s, t: (target, t ^ 2) if s != t >> 1 else None),
+    )
+
+
+def mm(left, right):
+    return jnp.dot(left, right, preferred_element_type=jnp.float32)
+
+
+def mm_nt(left, right):
+    return contract_axes(left, right, 1, 1)
+
+
+def norm_back(rows, gain, grad):
+    mean = jnp.mean(rows, axis=-1, keepdims=True)
+    centered = rows - mean
+    scale = lax.rsqrt(jnp.mean(centered * centered, axis=-1, keepdims=True) + 1e-05)
+    unit = centered * scale
+    scaled = grad * gain
+    return scale * (
+        scaled
+        - jnp.mean(scaled, axis=-1, keepdims=True)
+        - unit * jnp.mean(scaled * unit, axis=-1, keepdims=True)
+    )
+
+
+def gelu_both(value):
+    square = value * value
+    bent = jnp.tanh(0.7978845608028654 * value * (1.0 + 0.044715 * square))
+    half = 0.5 * (1.0 + bent)
+    slope = half + 0.5 * value * (1.0 - bent * bent) * (
+        0.7978845608028654 * (1.0 + 3.0 * 0.044715 * square)
+    )
+    return value * half, slope
+
+
+def cost(flops, read):
+    return pl.CostEstimate(flops=int(flops), bytes_accessed=int(read), transcendentals=0)
+
+
+def kernel_params(mib):
+    return pltpu.CompilerParams(vmem_limit_bytes=mib * 1024 * 1024)
+
+
+def position_mask(meta, query_block, key_block):
+    shape = (BLOCK, BLOCK)
+    key_pos = key_block * BLOCK + lax.broadcasted_iota(jnp.int32, shape, 0)
+    query_pos = query_block * BLOCK + lax.broadcasted_iota(jnp.int32, (1, BLOCK), 1)
+    low = jnp.zeros((1, BLOCK), jnp.int32)
+    for c in range(4):
+        first = meta[4 + c]
+        low = jnp.where(first <= query_pos, jnp.maximum(low, first), low)
+    valid = key_pos >= low
+    if query_block == key_block:
+        valid = valid & (key_pos <= query_pos)
+    return valid
+
+
+def head_lanes(half):
+    return (lax.broadcasted_iota(jnp.int32, (1, 2 * HEAD), 1) // HEAD) == half
+
+
+def load_qkv_weight(meta, w_same, w_cross, w_buf, sem):
+    home = meta[0] == meta[2]
+
+    @pl.when(home)
+    def _():
+        pltpu.make_async_copy(w_same, w_buf, sem).start()
+
+    @pl.when(jnp.logical_not(home))
+    def _():
+        pltpu.make_async_copy(w_cross, w_buf, sem).start()
+
+
+def block_places(meta):
+    s, x = meta[0], meta[1]
+    return (x + 2 * s, x + 2 * (1 - s), (1 - x) + 2 * s, (1 - x) + 2 * (1 - s))
+
+
+def attend_kernel(
+    layer, meta, n0, n1, n2, n3, shared, varied, w_same, w_cross,
+    q_ref, k_ref, v_ref, lse_ref, mixed_ref, o0, o1, o2, o3,
+    w_buf, score_buf, vt_buf, sem,
+):
+    load_qkv_weight(meta, w_same, w_cross, w_buf, sem)
+    s, x = meta[0], meta[1]
+    quarter = x + 2 * s
+    down = shared[layer, 8:16, :].astype(jnp.bfloat16)
+    bias = varied[quarter, layer, 1:2, :]
+    up = varied[quarter, layer, 8:16, 0:512].astype(jnp.bfloat16)
+    places = block_places(meta)
+    pltpu.make_async_copy(w_same, w_buf, sem).wait()
+    for place, block in zip(places, (n0, n1, n2, n3)):
+        rows = pl.ds(pl.multiple_of(place * BLOCK, BLOCK), BLOCK)
+        normed = block[...]
+        low = mm_nt(normed, down).astype(jnp.bfloat16)
+        lifted = adapter_scale * mm(low, up)
+        q_ref[rows, :] = (mm(normed, w_buf[0]) + bias[:, 0:256] + lifted[:, 0:256]).astype(
+            jnp.bfloat16
+        )
+        k_ref[rows, :] = mm(normed, w_buf[1]).astype(jnp.bfloat16)
+        v_ref[rows, :] = (mm(normed, w_buf[2]) + bias[:, 256:512] + lifted[:, 256:512]).astype(
+            jnp.bfloat16
+        )
+    for b in range(4):
+        vt_buf[:, b * BLOCK : (b + 1) * BLOCK] = v_ref[b * BLOCK : (b + 1) * BLOCK, :].T
+
+    def one_head(head, carry):
+        lanes = pl.ds(pl.multiple_of((head // 2) * 128, 128), 128)
+        chosen = head_lanes(head % 2)
+        deep = pl.ds(pl.multiple_of(head * HEAD, HEAD), HEAD)
+        for i in range(4):
+            part = q_ref[i * BLOCK : (i + 1) * BLOCK, lanes]
+            query = jnp.where(chosen, part * HEAD ** (-0.5), 0.0).astype(jnp.bfloat16)
+            top = jnp.full((1, BLOCK), -1e30, jnp.float32)
+            for j in range(i + 1):
+                scores = mm_nt(k_ref[j * BLOCK : (j + 1) * BLOCK, lanes], query)
+                scores = jnp.where(position_mask(meta, i, j), scores, -1e30)
+                score_buf[j] = scores
+                top = jnp.maximum(top, jnp.max(scores, axis=0, keepdims=True))
+            total = jnp.zeros((1, BLOCK), jnp.float32)
+            mixed = jnp.zeros((HEAD, BLOCK), jnp.float32)
+            for j in range(i + 1):
+                weights = jnp.exp(score_buf[j] - top)
+                total = total + jnp.sum(weights, axis=0, keepdims=True)
+                mixed = mixed + mm(
+                    vt_buf[deep, j * BLOCK : (j + 1) * BLOCK], weights.astype(jnp.bfloat16)
+                )
+            mixed_ref[deep, i * BLOCK : (i + 1) * BLOCK] = mixed / total
+            lse_ref[pl.ds(head, 1), i * BLOCK : (i + 1) * BLOCK] = top + jnp.log(total)
+        return carry
+
+    lax.fori_loop(0, 4, one_head, 0)
+    for place, out in zip(places, (o0, o1, o2, o3)):
+        columns = pl.ds(pl.multiple_of(place * BLOCK, BLOCK), BLOCK)
+        out[...] = mixed_ref[:, columns].T.astype(jnp.bfloat16)
+
+
+def attend_call(layer, meta, blocks, shared, varied, w_same, w_cross):
+    bf, f32 = jnp.bfloat16, jnp.float32
+    wide = jax.ShapeDtypeStruct((SEQ_LEN, 256), bf)
+    piece = jax.ShapeDtypeStruct((BLOCK, 256), bf)
+    return pl.pallas_call(
+        functools.partial(attend_kernel, layer),
+        in_specs=[SMEM_SPACE] + [VMEM_SPACE] * 6 + [HBM_SPACE] * 2,
+        out_specs=[VMEM_SPACE] * 9,
+        out_shape=[wide, wide, wide, jax.ShapeDtypeStruct((8, SEQ_LEN), f32),
+                   jax.ShapeDtypeStruct((256, SEQ_LEN), f32)] + [piece] * 4,
+        scratch_shapes=[
+            pltpu.VMEM((3, 1024, 256), bf),
+            pltpu.VMEM((4, BLOCK, BLOCK), f32),
+            pltpu.VMEM((256, SEQ_LEN), bf),
+            pltpu.SemaphoreType.DMA,
+        ],
+        compiler_params=kernel_params(40),
+        cost_estimate=cost(3.5e9, 8e6),
+        name="attention_forward",
+    )(meta, *blocks, shared, varied, w_same, w_cross)
+
+
+def attend_back_kernel(
+    layer, meta, n0, n1, n2, n3, g0, g1, g2, g3, q_ref, k_ref, v_ref, lse_ref, mixed_ref,
+    shared, varied, w_same, w_cross,
+    keep_ref, give_ref, down_ref, up_ref,
+    w_buf, kt_buf, do_buf, delta_buf, dqt_buf, dk_buf, dv_buf, dq_buf, sem,
+):
+    load_qkv_weight(meta, w_same, w_cross, w_buf, sem)
+    s, x = meta[0], meta[1]
+    quarter = x + 2 * s
+    places = block_places(meta)
+    for place, block in zip(places, (g0, g1, g2, g3)):
+        do_buf[pl.ds(pl.multiple_of(place * BLOCK, BLOCK), BLOCK), :] = block[...]
+    for b in range(4):
+        span = slice(b * BLOCK, (b + 1) * BLOCK)
+        kt_buf[:, span] = k_ref[span, :].T
+        product = do_buf[span, :].astype(jnp.float32).T * mixed_ref[:, span]
+        for head in range(4):
+            delta_buf[head : head + 1, span] = jnp.sum(
+                product[head * HEAD : (head + 1) * HEAD], axis=0, keepdims=True
+            )
+    dk_buf[...] = jnp.zeros_like(dk_buf)
+    dv_buf[...] = jnp.zeros_like(dv_buf)
+
+    def one_head(head, carry):
+        lanes = pl.ds(pl.multiple_of((head // 2) * 128, 128), 128)
+        chosen = head_lanes(head % 2)
+        deep = pl.ds(pl.multiple_of(head * HEAD, HEAD), HEAD)
+        for i in range(4):
+            span = slice(i * BLOCK, (i + 1) * BLOCK)
+            query = jnp.where(chosen, q_ref[span, lanes] * HEAD ** (-0.5), 0.0).astype(jnp.bfloat16)
+            grad_mixed = jnp.where(chosen, do_buf[span, lanes], 0.0).astype(jnp.bfloat16)
+            lse = lse_ref[pl.ds(head, 1), span]
+            delta = delta_buf[pl.ds(head, 1), span]
+            grad_query = jnp.zeros((HEAD, BLOCK), jnp.float32)
+            for j in range(i + 1):
+                keys = slice(j * BLOCK, (j + 1) * BLOCK)
+                scores = mm_nt(k_ref[keys, lanes], query)
+                probs = jnp.where(position_mask(meta, i, j), jnp.exp(scores - lse), 0.0)
+                grad_probs = mm_nt(v_ref[keys, lanes], grad_mixed)
+                grad_scores = (probs * (grad_probs - delta)).astype(jnp.bfloat16)
+                dv_buf[keys, lanes] += mm(probs.astype(jnp.bfloat16), grad_mixed)
+                dk_buf[keys, lanes] += mm(grad_scores, query)
+                grad_query = grad_query + mm(kt_buf[deep, keys], grad_scores)
+            dqt_buf[deep, span] = grad_query * HEAD ** (-0.5)
+        return carry
+
+    lax.fori_loop(0, 4, one_head, 0)
+    down = shared[layer, 8:16, :].astype(jnp.bfloat16)
+    up = varied[quarter, layer, 8:16, 0:512].astype(jnp.bfloat16)
+    for b in range(4):
+        span = slice(b * BLOCK, (b + 1) * BLOCK)
+        dq_buf[span, :] = dqt_buf[:, span].T.astype(jnp.bfloat16)
+    pltpu.make_async_copy(w_same, w_buf, sem).wait()
+    total_down = jnp.zeros((LOW, 1024), jnp.float32)
+    total_up = jnp.zeros((LOW, 512), jnp.float32)
+    targets = ((keep_ref, 0), (give_ref, 0), (keep_ref, 1), (give_ref, 1))
+    for place, block, (target, slot) in zip(places, (n0, n1, n2, n3), targets):
+        rows = pl.ds(pl.multiple_of(place * BLOCK, BLOCK), BLOCK)
+        normed = block[...]
+        grad_q = dq_buf[rows, :]
+        grad_k = dk_buf[rows, :].astype(jnp.bfloat16)
+        grad_v = dv_buf[rows, :].astype(jnp.bfloat16)
+        both = jnp.concatenate([grad_q, grad_v], axis=1)
+        low_grad = (adapter_scale * mm_nt(both, up)).astype(jnp.bfloat16)
+        low_grad_t = (adapter_scale * mm_nt(up, both)).astype(jnp.bfloat16)
+        low_t = mm_nt(down, normed).astype(jnp.bfloat16)
+        grad_normed = (
+            mm_nt(grad_q, w_buf[0]) + mm_nt(grad_k, w_buf[1]) + mm_nt(grad_v, w_buf[2])
+            + mm(low_grad, down)
+        )
+        target[slot] = grad_normed.astype(jnp.bfloat16)
+        total_down = total_down + mm(low_grad_t, normed)
+        total_up = total_up + adapter_scale * mm(low_t, both)
+    down_ref[...] = total_down
+    up_ref[...] = total_up
+
+
+def attend_back_call(layer, meta, blocks, grads, saved, shared, varied, w_same, w_cross):
+    bf, f32 = jnp.bfloat16, jnp.float32
+    pair = jax.ShapeDtypeStruct((2, BLOCK, 1024), bf)
+    return pl.pallas_call(
+        functools.partial(attend_back_kernel, layer),
+        in_specs=[SMEM_SPACE] + [VMEM_SPACE] * 15 + [HBM_SPACE] * 2,
+        out_specs=[VMEM_SPACE] * 4,
+        out_shape=[pair, pair, jax.ShapeDtypeStruct((LOW, 1024), f32),
+                   jax.ShapeDtypeStruct((LOW, 512), f32)],
+        scratch_shapes=[
+            pltpu.VMEM((3, 1024, 256), bf),
+            pltpu.VMEM((256, SEQ_LEN), bf),
+            pltpu.VMEM((SEQ_LEN, 256), bf),
+            pltpu.VMEM((8, SEQ_LEN), f32),
+            pltpu.VMEM((256, SEQ_LEN), f32),
+            pltpu.VMEM((SEQ_LEN, 256), f32),
+            pltpu.VMEM((SEQ_LEN, 256), f32),
+            pltpu.VMEM((SEQ_LEN, 256), bf),
+            pltpu.SemaphoreType.DMA,
+        ],
+        compiler_params=kernel_params(48),
+        cost_estimate=cost(6e9, 12e6),
+        name="attention_backward",
+    )(meta, *blocks, *grads, *saved, shared, varied, w_same, w_cross)
+
+
+N_WEIGHTS = 18
+
+
+def weight_plan(layer, meta, refs, wp, w1, w2, sems):
+    s = meta[0]
+    own, dup, parts = refs[0:3], refs[3:6], refs[6:18]
+    plan = {"p": [[] for _ in range(4)], "a": [[] for _ in range(4)], "b": [[] for _ in range(4)]}
+    count = 0
+
+    def add(kind, slot, source, target, alternative=None):
+        nonlocal count
+        plan[kind][slot].append((source, target, sems.at[count], alternative))
+        count += 1
+
+    half_p = [pl.ds(pl.multiple_of(h * 128, 128), 128) for h in (s, 1 - s)]
+    half_w = [pl.ds(pl.multiple_of(h * 512, 512), 512) for h in (s, 1 - s)]
+    add("p", 0, own[0], wp.at[0], dup[0])
+    add("a", 0, own[1], w1.at[0], dup[1])
+    add("b", 0, own[2], w2.at[0], dup[2])
+    for slot in (1, 2, 3):
+        for h in range(2):
+            first, second = parts[(slot - 1) * 4 + 2 * h : (slot - 1) * 4 + 2 * h + 2]
+            add("p", slot, first.at[0:128], wp.at[slot, half_p[h]])
+            add("a", slot, first.at[128:640], w1.at[slot, half_w[h]])
+            add("b", slot, second, w2.at[slot, half_w[h]])
+    return plan
+
+
+def start_copies(layer, meta, copies):
+    for source, target, sem, alternative in copies:
+        if alternative is None:
+            pltpu.make_async_copy(source, target, sem).start()
+        else:
+            mine = meta[0] == layer
+
+            @pl.when(mine)
+            def _():
+                pltpu.make_async_copy(source, target, sem).start()
+
+            @pl.when(jnp.logical_not(mine))
+            def _():
+                pltpu.make_async_copy(alternative, target, sem).start()
+
+
+def wait_copies(copies):
+    for source, target, sem, _ in copies:
+        pltpu.make_async_copy(source, target, sem).wait()
+
+
+def project(meta, pieces, wp):
+    apart = jnp.where(meta[0] == meta[2], 0, 1)
+    slots = (2 * apart, 2 * (1 - apart), 2 * apart + 1, 2 * (1 - apart) + 1)
+    total = mm(pieces[0][...], wp[slots[0]])
+    for piece, slot in zip(pieces[1:], slots[1:]):
+        total = total + mm(piece[...], wp[slot])
+    return total
+
+
+def back_to_heads(meta, grad, wp, outs):
+    apart = jnp.where(meta[0] == meta[2], 0, 1)
+    slots = (2 * apart, 2 * (1 - apart), 2 * apart + 1, 2 * (1 - apart) + 1)
+    for out, slot in zip(outs, slots):
+        out[...] = mm_nt(grad, wp[slot]).astype(jnp.bfloat16)
+
+
+def unit_bias(meta, varied, layer, slot):
+    return varied[jnp.bitwise_xor(meta[3], slot), layer, 0:1, :]
+
+
+def rows_forward_kernel(meta, p0, p1, p2, p3, h_ref, shared, varied, *rest):
+    refs = rest[:N_WEIGHTS]
+    middle_ref, slope_ref, between_ref, normed_ref = rest[N_WEIGHTS : N_WEIGHTS + 4]
+    wp, w1, w2, total, sems = rest[N_WEIGHTS + 4 :]
+    plan = weight_plan(0, meta, refs, wp, w1, w2, sems)
+    for kind in "pab":
+        for slot in range(4):
+            start_copies(0, meta, plan[kind][slot])
+    for slot in range(4):
+        wait_copies(plan["p"][slot])
+    middle = h_ref[...].astype(jnp.float32) + project(meta, (p0, p1, p2, p3), wp) + shared[0, 4:5, :]
+    middle_ref[...] = middle
+    normed = layer_norm(middle, shared[0, 1:2, :], shared[0, 3:4, :]).astype(jnp.bfloat16)
+    total[...] = middle + shared[0, 5:6, :]
+    for slot in range(4):
+        wait_copies(plan["a"][slot])
+        active, slope = gelu_both(mm(normed, w1[slot]) + unit_bias(meta, varied, 0, slot))
+        slope_ref[slot] = slope.astype(jnp.bfloat16)
+        wait_copies(plan["b"][slot])
+        total[...] += mm(active.astype(jnp.bfloat16), w2[slot])
+    between = total[...].astype(jnp.bfloat16)
+    between_ref[...] = between
+    normed_ref[...] = layer_norm(
+        between.astype(jnp.float32), shared[1, 0:1, :], shared[1, 2:3, :]
+    ).astype(jnp.bfloat16)
+
+
+def rows_turn_kernel(meta, p0, p1, p2, p3, h_ref, g_ref, shared, varied, *rest):
+    refs = rest[:N_WEIGHTS]
+    middle_ref, active_ref, grad_ref, o0, o1, o2, o3 = rest[N_WEIGHTS : N_WEIGHTS + 7]
+    wp, w1, w2, total, sems = rest[N_WEIGHTS + 7 :]
+    plan = weight_plan(1, meta, refs, wp, w1, w2, sems)
+    for kind in "pab":
+        for slot in range(4):
+            start_copies(1, meta, plan[kind][slot])
+    for slot in range(4):
+        wait_copies(plan["p"][slot])
+    middle = h_ref[...].astype(jnp.float32) + project(meta, (p0, p1, p2, p3), wp) + shared[1, 4:5, :]
+    middle_ref[...] = middle
+    normed = layer_norm(middle, shared[1, 1:2, :], shared[1, 3:4, :]).astype(jnp.bfloat16)
+    grad = g_ref[...]
+    for slot in range(4):
+        wait_copies(plan["a"][slot])
+        active, slope = gelu_both(mm(normed, w1[slot]) + unit_bias(meta, varied, 1, slot))
+        active_ref[slot] = active.astype(jnp.bfloat16)
+        wait_copies(plan["b"][slot])
+        grad_hidden = (mm_nt(grad, w2[slot]) * slope).astype(jnp.bfloat16)
+        part = mm_nt(grad_hidden, w1[slot])
+        if slot == 0:
+            total[...] = part
+        else:
+            total[...] += part
+    grad_middle = grad.astype(jnp.float32) + norm_back(middle, shared[1, 1:2, :], total[...])
+    grad_ref[...] = grad_middle
+    back_to_heads(meta, grad_middle.astype(jnp.bfloat16), wp, (o0, o1, o2, o3))
+
+
+def rows_backward_kernel(meta, gm_ref, keep, take, far, between_ref, middle_ref, slope_ref, shared, *rest):
+    refs = rest[:N_WEIGHTS]
+    grad_ref, o0, o1, o2, o3 = rest[N_WEIGHTS : N_WEIGHTS + 5]
+    wp, w1, w2, total, sems = rest[N_WEIGHTS + 5 :]
+    plan = weight_plan(0, meta, refs, wp, w1, w2, sems)
+    for kind in "bap":
+        for slot in range(4):
+            start_copies(0, meta, plan[kind][slot])
+    grad_normed = (
+        keep[0].astype(jnp.float32) + take[0].astype(jnp.float32) + far[...].astype(jnp.float32)
+    )
+    grad_rows = gm_ref[...] + norm_back(
+        between_ref[...].astype(jnp.float32), shared[1, 0:1, :], grad_normed
+    )
+    grad = grad_rows.astype(jnp.bfloat16)
+    for slot in range(4):
+        wait_copies(plan["b"][slot])
+        grad_active = mm_nt(grad, w2[slot])
+        grad_hidden = (grad_active * slope_ref[slot].astype(jnp.float32)).astype(jnp.bfloat16)
+        wait_copies(plan["a"][slot])
+        part = mm_nt(grad_hidden, w1[slot])
+        if slot == 0:
+            total[...] = part
+        else:
+            total[...] += part
+    grad_middle = grad.astype(jnp.float32) + norm_back(middle_ref[...], shared[0, 1:2, :], total[...])
+    grad_ref[...] = grad_middle
+    for slot in range(4):
+        wait_copies(plan["p"][slot])
+    back_to_heads(meta, grad_middle.astype(jnp.bfloat16), wp, (o0, o1, o2, o3))
+
+
+def rows_output_kernel(meta, active_ref, middle_ref, shared, *rest):
+    refs = rest[:N_WEIGHTS]
+    wide_ref, narrow_ref = rest[N_WEIGHTS : N_WEIGHTS + 2]
+    wp, w1, w2, sems = rest[N_WEIGHTS + 2 :]
+    plan = weight_plan(1, meta, refs, wp, w1, w2, sems)
+    for slot in range(4):
+        start_copies(1, meta, plan["b"][slot])
+    total = middle_ref[...] + shared[1, 5:6, :]
+    for slot in range(4):
+        wait_copies(plan["b"][slot])
+        total = total + mm(active_ref[slot], w2[slot])
+    wide_ref[...] = total
+    narrow_ref[...] = total.astype(jnp.bfloat16)
+
+
+def rows_final_kernel(gm_ref, keep, take, far, h_ref, shared, wide_ref, narrow_ref):
+    grad_normed = (
+        keep[0].astype(jnp.float32) + take[0].astype(jnp.float32) + far[...].astype(jnp.float32)
+    )
+    grad_in = gm_ref[...] + norm_back(
+        h_ref[...].astype(jnp.float32), shared[0, 0:1, :], grad_normed
+    )
+    wide_ref[...] = grad_in
+    narrow_ref[...] = grad_in.astype(jnp.bfloat16)
+
+
+def rows_call(kernel, small, weights, outs, scratch, flops, name):
+    return pl.pallas_call(
+        kernel,
+        in_specs=[SMEM_SPACE] + [VMEM_SPACE] * (len(small) - 1) + [HBM_SPACE] * len(weights),
+        out_specs=[VMEM_SPACE] * len(outs),
+        out_shape=outs,
+        scratch_shapes=scratch,
+        compiler_params=kernel_params(52),
+        cost_estimate=cost(flops, 2e7),
+        name=name,
+    )(*small, *weights)
+
+
+def weight_scratch(total):
+    bf = jnp.bfloat16
+    found = [
+        pltpu.VMEM((4, 256, 1024), bf),
+        pltpu.VMEM((4, 1024, 1024), bf),
+        pltpu.VMEM((4, 1024, 1024), bf),
+    ]
+    if total:
+        found.append(pltpu.VMEM((BLOCK, 1024), jnp.float32))
+    found.append(pltpu.SemaphoreType.DMA((21,)))
+    return found
+
+
+def spread_weights(layer, section, wp, w1, w2):
+    own = (wp, w1, w2)
+    dup = tuple(
+        send(w, lambda s, t: (1 - layer, t) if s == layer else None) for w in own
+    )
+
+    def halves(group, half):
+        return (
+            jnp.concatenate(
+                [group[0][half * 128 : half * 128 + 128], group[1][half * 512 : half * 512 + 512]]
+            ),
+            group[2][half * 512 : half * 512 + 512],
+        )
+
+    mine = section == layer
+    first, second = jax.tree.map(
+        lambda a, b: jnp.where(mine, a, b), halves(own, layer), halves(dup, 1 - layer)
+    )
+    x1, x2 = x_swap(first), x_swap(second)
+    y1, y2 = y_swap(first), y_swap(second)
+    d1, d2 = y_swap(x1), x_swap(y2)
+    parts = (
+        x1, x2, other_core(x1), other_core(x2),
+        y1, y2, other_core(y1), other_core(y2),
+        d1, d2, other_core(d1), other_core(d2),
+    )
+    return own + dup + parts
+
+
+def gather_rows(own):
+    near = other_core(own)
+    far = x_swap(own)
+    return (own, near, far, other_core(far))
+
+
+def exchange_heads(o0, o1, o2, o3):
+    return (
+        o0,
+        other_core(o1),
+        x_swap(o2),
+        send(o3, lambda s, t: (1 - s, t ^ 1)),
+    )
+
+
+def reduce_rows(keep, give):
+    take = other_core(give)
+    far = x_swap((keep[1].astype(jnp.float32) + take[1].astype(jnp.float32)).astype(jnp.bfloat16))
+    return keep, take, far
+
+
+def total_adapters(layer, part_down, part_up):
+    part_down = part_down + other_core(part_down)
+    part_down = part_down + x_swap(part_down)
+    both = jnp.concatenate([part_down, part_up], axis=1)
+    both = both + y_swap(both)
+    size = lax.axis_size("dp")
+    step = 1
+    while step < size:
+        both = both + lax.ppermute(both, "dp", [(i, i ^ step) for i in range(size)])
+        step *= 2
+    up = send(both[:, 1024:], lambda s, t: (layer, t) if s == t >> 1 else None)
+    return both[:, :1024], up
+
+
+def relay_body(
+    activations, starts, attention_weights, projection_weight, feedforward_weight, output_weight,
+    norm_gains, norm_biases, output_biases, query_value_bias, feedforward_bias,
+    adapter_down_weight, adapter_up_weight,
+):
+    bf, f32 = jnp.bfloat16, jnp.float32
+    section = lax.axis_index("section")
+    place = lax.axis_index("tensor")
+    y, x = place // 2, place % 2
+    first = section == 0
+    home = section == y
+
+    meta = jnp.concatenate(
+        [
+            jnp.stack([section, x, y, place]).astype(jnp.int32),
+            lax.dynamic_index_in_dim(starts, y, 0, keepdims=False).reshape(4),
+        ]
+    )
+    slots = activations[0]
+    same = lax.dynamic_index_in_dim(slots, y, 0, keepdims=False)
+    cross = lax.dynamic_index_in_dim(slots, 1 - y, 0, keepdims=False)
+    rows = jnp.where(home, *deal(0, same, cross))
+
+    down_rows = adapter_down_weight[0].astype(f32).transpose(0, 2, 1).reshape(LOW, 1024)
+    up0 = adapter_up_weight[0, 0].astype(f32)
+    up1 = adapter_up_weight[0, 1].astype(f32)
+    zero = jnp.zeros((ADAPTER_RANK, 256), f32)
+    packed = jnp.concatenate(
+        [
+            norm_gains[0], norm_biases[0], output_biases[0], jnp.zeros((2, 1024), f32), down_rows,
+            feedforward_bias,
+            jnp.pad(query_value_bias[0].reshape(1, 512), ((0, 0), (0, 512))),
+            jnp.zeros((6, 1024), f32),
+            jnp.concatenate([up0, zero, jnp.zeros((ADAPTER_RANK, 512), f32)], axis=1),
+            jnp.concatenate([zero, up1, jnp.zeros((ADAPTER_RANK, 512), f32)], axis=1),
+        ]
+    )
+    partner = other_core(packed)
+    both = jnp.where(first, jnp.stack([packed, partner]), jnp.stack([partner, packed]))
+    shared = both[:, :16]
+    varied = lax.all_gather(both[:, 16:], "tensor", axis=0)
+
+    qkv = [deal(layer, attention_weights[0], attention_weights[0]) for layer in range(2)]
+    weights = [
+        spread_weights(layer, section, projection_weight[0], feedforward_weight[0], output_weight[0])
+        for layer in range(2)
+    ]
+    grad_out = jnp.where(home, *deal(1, same, cross))
+
+    sheet = jax.ShapeDtypeStruct((BLOCK, 1024), f32)
+    thin = jax.ShapeDtypeStruct((BLOCK, 1024), bf)
+    stack4 = jax.ShapeDtypeStruct((4, BLOCK, 1024), bf)
+    piece = jax.ShapeDtypeStruct((BLOCK, 256), bf)
+
+    normed = layer_norm(rows.astype(f32), shared[0, 0], shared[0, 2]).astype(bf)
+    blocks0 = gather_rows(normed)
+    *saved0, o0, o1, o2, o3 = attend_call(0, meta, blocks0, shared, varied, *qkv[0])
+    heads = exchange_heads(o0, o1, o2, o3)
+    middle0, slope0, between, normed = rows_call(
+        rows_forward_kernel, (meta, *heads, rows, shared, varied), weights[0],
+        [sheet, stack4, thin, thin], weight_scratch(True), 5e9, "rows_forward",
+    )
+    blocks1 = gather_rows(normed)
+    *saved1, o0, o1, o2, o3 = attend_call(1, meta, blocks1, shared, varied, *qkv[1])
+    heads = exchange_heads(o0, o1, o2, o3)
+    middle1, active1, grad_middle1, o0, o1, o2, o3 = rows_call(
+        rows_turn_kernel, (meta, *heads, between, grad_out, shared, varied), weights[1],
+        [sheet, stack4, sheet, piece, piece, piece, piece], weight_scratch(True), 8e9, "rows_turn",
+    )
+    grads = exchange_heads(o0, o1, o2, o3)
+    wide, narrow = rows_call(
+        rows_output_kernel, (meta, active1, middle1, shared), weights[1],
+        [sheet, thin], weight_scratch(False), 2.1e9, "rows_output",
+    )
+    out_same, out_cross = collect(1, wide, narrow)
+    keep, give, down1, up1 = attend_back_call(
+        1, meta, blocks1, grads, saved1, shared, varied, *qkv[1]
+    )
+    keep, take, far = reduce_rows(keep, give)
+    grad_middle0, o0, o1, o2, o3 = rows_call(
+        rows_backward_kernel,
+        (meta, grad_middle1, keep, take, far, between, middle0, slope0, shared), weights[0],
+        [sheet, piece, piece, piece, piece], weight_scratch(True), 5e9, "rows_backward",
+    )
+    total1 = total_adapters(1, down1, up1)
+    grads = exchange_heads(o0, o1, o2, o3)
+    keep, give, down0, up0 = attend_back_call(
+        0, meta, blocks0, grads, saved0, shared, varied, *qkv[0]
+    )
+    keep, take, far = reduce_rows(keep, give)
+    wide, narrow = pl.pallas_call(
+        rows_final_kernel,
+        in_specs=[VMEM_SPACE] * 6,
+        out_specs=[VMEM_SPACE] * 2,
+        out_shape=[sheet, thin],
+        compiler_params=kernel_params(32),
+        cost_estimate=cost(1e7, 6e6),
+        name="rows_final",
+    )(grad_middle0, keep, take, far, rows, shared)
+    total0 = total_adapters(0, down0, up0)
+    in_same, in_cross = collect(0, wide, narrow)
+    same = jnp.where(first, in_same, out_same)
+    cross = jnp.where(first, in_cross, out_cross).astype(f32)
+    combined = jnp.where(y == 0, jnp.stack([same, cross]), jnp.stack([cross, same]))
+    grad_down = jnp.where(first, total0[0], total1[0])
+    grad_up = jnp.where(first, total0[1], total1[1])
+    return (
+        combined[None],
+        grad_down.reshape(1, 2, ADAPTER_RANK, 1024).transpose(0, 1, 3, 2),
+        jnp.stack([grad_up[:ADAPTER_RANK, :256], grad_up[ADAPTER_RANK:, 256:]])[None],
+    )
+
+
+def body(*arrays):
+    dp = lax.axis_size("dp")
+    known = (
+        arrays[0].shape == (1, 2, BLOCK, 1024)
+        and lax.axis_size("tensor") == 4
+        and lax.axis_size("section") == 2
+        and arrays[3].shape == (1, 256, 1024)
+        and arrays[5].shape == (1, 1024, 1024)
+        and dp & (dp - 1) == 0
+    )
+    return relay_body(*arrays) if known else plain_body(*arrays)
+
+
 def solution(mesh):
     placed = (
         P("section", None, ("dp", "tensor"), None),

time: 1700 us -> 461 us (0.27)
  waiting for transfers between devices: 1060 us -> 178 us
  matrix products: 339 us -> 0 us
  other arithmetic: 139 us -> 10.5 us
  Pallas kernels: 0 us -> 114 us
  starting transfers between devices: 20.4 us -> 102 us
  blocking collectives: 86.2 us -> 34.2 us
    reduce_scatter x15 -> x0, waiting for transfers between devices: 534 us -> none  [the longest x6 288 us: forward_relay(): lax.psum_scatter(jnp.dot(mixed, projection_weight[0], preferred_element_t...]
    all_gather x18 -> x0, waiting for transfers between devices: 521 us -> none  [the longest x6 174 us: forward_relay(): gathered = lax.all_gather(normalized_rows, 'tensor', axis=0, tiled=True)]
    dot_general x84 -> x0, matrix products: 306 us -> none  [the longest x27 59 us: contract_axes(): lax.dot_general(left, right, (((left_dim,), (right_dim,)), ((), ())), pre...]
    ppermute x4 -> x77, waiting for transfers between devices: 8.18 us -> 178 us  [the longest x73 178 us: send(): return lax.ppermute(block, ('section', 'tensor'), pairs)]
    pallas_call x0 -> x9, Pallas kernels: none -> 114 us  [the longest x4 52.6 us: rows_call(): pl.pallas_call(kernel, in_specs=[SMEM_SPACE] + [VMEM_SPACE] * (len(small)...]
    ppermute x4 -> x77, starting transfers between devices: 6.86 us -> 102 us  [the longest x73 93.4 us: send(): return lax.ppermute(block, ('section', 'tensor'), pairs)]
    psum x2 -> x0, blocking collectives: 86.2 us -> none  [reduce_adapters(): return (lax.psum(part_a, ('dp', 'tensor')), lax.psum(second_portion, 'dp'))]
    convert_element_type x22 -> x4, other arithmetic: 57.2 us -> 1.47 us  [the longest x2 1.18 us: reduce_rows(): (keep[1].astype(jnp.float32) + take[1].astype(jnp.float32)).astype(jnp.bf...]
  transfers between devices with their start and end apart: 37 -> 77, of which waited for: 34 -> 32; matrix products, arithmetic and copies ran while one was open for 10% -> 3% of each run, Pallas kernels for 0% -> 11%
where the time goes in v1:
time: 461 us; the launch traced here: 454 us
  waiting for transfers between devices  178 us (39%)
  Pallas kernels  114 us (25%)
  starting transfers between devices  102 us (22%)
  blocking collectives  34.2 us (7%)
  local copies, waits for them, and re-layouts  12.6 us (3%)
  other arithmetic  10.5 us (2%)
    ppermute x73, waiting for transfers between devices, send(): return lax.ppermute(block, ('section', 'tensor'), pairs)  178 us
    ppermute x73, starting transfers between devices, send(): return lax.ppermute(block, ('section', 'tensor'), pairs)  93.4 us
    pallas_call x4, Pallas kernels, rows_call(): pl.pallas_call(kernel, in_specs=[SMEM_SPACE] + [VMEM_SPACE] * (len(small)...  52.6 us
    pallas_call x2, Pallas kernels, attend_back_call(): pl.pallas_call(functools.partial(attend_back_kernel, layer), in_specs=[SM...  34.6 us
    all_gather x1, blocking collectives, relay_body(): varied = lax.all_gather(both[:, 16:], 'tensor', axis=0)  34.2 us
    pallas_call x2, Pallas kernels, attend_call(): pl.pallas_call(functools.partial(attend_kernel, layer), in_specs=[SMEM_SP...  24.3 us
  transfers between devices with their start and end apart: 77, of which 32 were waited for; matrix products, arithmetic and copies ran while one was open for 3% of the time, Pallas kernels for 11%

profile of v1, /device:TPU:0, one launch (start us, length us, event | category | flops | bytes accessed | tf_op | source)
XLA Modules:
  0.0 454.2 jit_solution(15196029029320817995)
XLA Ops:
  21.1 5.7 %collective-permute-start.13 = (bf16[1024,1024]{1,0:T(8,128)(2,1)}, bf16[1024,1024]{1,0:T(8,128)(2,1)}, u32[]{:S(2)}, u32[]{:S(2)}) collective-permute-start(bf16[1024,1024]{1,0:T(8,128)(2,1)} %bitcast.82), channel_id=1, source_target_pairs={{0,16},{1,17},{2,18},{3,19},{4,20},{5,21},{6,22},{7,23},{8,24},{9,... | collective-permute-start | bytes 6291464 | tf_op jit(solution)/shard_map/ppermute | solution.py:345
  31.3 12.1 %collective-permute-done.4.n2 = bf16[256,1024]{1,0:T(8,128)(2,1)S(1)} collective-permute-done((bf16[256,1024]{1,0:T(8,128)(2,1)S(1)}, bf16[256,1024]{1,0:T(8,128)(2,1)S(1)}, u32[]{:S(2)}, u32[]{:S(2)}) %collective-permute-start.4) | collective-permute-done | bytes 524320 | tf_op jit(solution)/shard_map/ppermute | solution.py:345
  46.8 13.3 %collective-permute-start.6 = (bf16[3,1024,256]{2,1,0:T(8,128)(2,1)}, bf16[3,1024,256]{2,1,0:T(8,128)(2,1)}, u32[]{:S(2)}, u32[]{:S(2)}) collective-permute-start(bf16[3,1024,256]{2,1,0:T(8,128)(2,1)} %bitcast.19), channel_id=1, source_target_pairs={{0,0},{1,1},{2,18},{3,19},{4,4},{5,5},{6,22},{7,23},{8,8},{9,9},{1... | collective-permute-start | bytes 4718600 | tf_op jit(solution)/shard_map/ppermute | solution.py:345
  74.6 34.2 %all-gather = f32[8,16,1024]{2,1,0:T(8,128)S(1)} all-gather(f32[2,16,1024]{2,1,0:T(8,128)S(1)} %get-tuple-element.105), channel_id=2, replica_groups=mesh['section'=2,'dp'=4,'tensor'=4] {'tensor'}, dimensions={0}, use_global_device_ids=true | all-gather | bytes 655360 | tf_op jit(solution)/shard_map/all_gather | solution.py:946
  108.8 12.7 %attention_forward.2 = (bf16[1024,256]{1,0:T(8,128)(2,1)S(1)}, bf16[1024,256]{1,0:T(8,128)(2,1)S(1)}, bf16[1024,256]{1,0:T(8,128)(2,1)S(1)}, f32[8,1024]{1,0:T(8...) custom-call(s32[8]{0:T(128)S(1)} %concatenate.44.meta, ...), custom_call_target="tpu_custom_call" | custom-call | flops 3500000000 | bytes 8000000 | tf_op jit(solution)/shard_map/attention_forward/pallas_call | solution.py:511
  121.6 6.1 %collective-permute-start.8 = (bf16[256,256]{1,0:T(8,128)(2,1)S(1)}, bf16[256,256]{1,0:T(8,128)(2,1)S(1)}, u32[]{:S(2)}, u32[]{:S(2)}) collective-permute-start(bf16[256,256]{1,0:T(8,128)(2,1)S(1)} %get-tuple-element.50), channel_id=1, source_target_pairs={{0,16},{1,17},{2,18},{3,19},{16,0},{17,1},{18,2},{19,3},{4,20},{5,... | collective-permute-start | bytes 393224 | tf_op jit(solution)/shard_map/ppermute | solution.py:345
  133.2 5.2 %collective-permute-done.10.p3 = bf16[256,256]{1,0:T(8,128)(2,1)S(1)} collective-permute-done((bf16[256,256]{1,0:T(8,128)(2,1)S(1)}, bf16[256,256]{1,0:T(8,128)(2,1)S(1)}, u32[]{:S(2)}, u32[]{:S(2)}) %collective-permute-start.10) | collective-permute-done | bytes 131104 | tf_op jit(solution)/shard_map/ppermute | solution.py:345
  145.5 9.2 %collective-permute-done.19.rest_11_ = bf16[512,1024]{1,0:T(8,128)(2,1)S(1)} collective-permute-done((bf16[512,1024]{1,0:T(8,128)(2,1)S(1)}, bf16[512,1024]{1,0:T(8,128)(2,1)S(1)}, u32[]{:S(2)}, u32[]{:S(2)}) %collective-permute-start.19) | collective-permute-done | bytes 1048608 | tf_op jit(solution)/shard_map/ppermute | solution.py:345
  155.8 8.7 %collective-permute-done.15.rest_7_ = bf16[512,1024]{1,0:T(8,128)(2,1)S(1)} collective-permute-done((bf16[512,1024]{1,0:T(8,128)(2,1)S(1)}, bf16[512,1024]{1,0:T(8,128)(2,1)S(1)}, u32[]{:S(2)}, u32[]{:S(2)}) %collective-permute-start.15) | collective-permute-done | bytes 1048608 | tf_op jit(solution)/shard_map/ppermute | solution.py:345
  164.5 18.2 %collective-permute-done.18.rest_10_ = bf16[640,1024]{1,0:T(8,128)(2,1)S(1)} collective-permute-done((bf16[640,1024]{1,0:T(8,128)(2,1)S(1)}, bf16[640,1024]{1,0:T(8,128)(2,1)S(1)}, u32[]{:S(2)}, u32[]{:S(2)}) %collective-permute-start.18) | collective-permute-done | bytes 1310752 | tf_op jit(solution)/shard_map/ppermute | solution.py:345
  182.8 9.9 %collective-permute-done.39.rest_6_ = bf16[640,1024]{1,0:T(8,128)(2,1)} collective-permute-done((bf16[640,1024]{1,0:T(8,128)(2,1)}, bf16[640,1024]{1,0:T(8,128)(2,1)}, u32[]{:S(2)}, u32[]{:S(2)}) %collective-permute-start.39) | collective-permute-done | bytes 1310752 | tf_op jit(solution)/shard_map/ppermute | solution.py:345
  192.7 21.0 %collective-permute-done.23.rest_15_ = bf16[512,1024]{1,0:T(8,128)(2,1)S(1)} collective-permute-done((bf16[512,1024]{1,0:T(8,128)(2,1)S(1)}, bf16[512,1024]{1,0:T(8,128)(2,1)S(1)}, u32[]{:S(2)}, u32[]{:S(2)}) %collective-permute-start.23) | collective-permute-done | bytes 1048608 | tf_op jit(solution)/shard_map/ppermute | solution.py:345
  222.8 13.6 %rows_forward.1 = (f32[256,1024]{1,0:T(8,128)}, bf16[4,256,1024]{2,1,0:T(8,128)(2,1)}, bf16[256,1024]{1,0:T(8,128)(2,1)S(1)}, bf16[256,1024]{1,0:T(8,128)(2,1)S(1)}) custom-call(s32[8]{0:T(128)S(1)} %concatenate.44.meta, bf16[256,256]{1,0:T(8,128)(2,1)S(1)} %get-tuple-element.49.p0, bf16[256,256]{1,0:T(8,128)(2,1)S(1)} %collective-permute-done.8.p1, ...), custom_call_target="tpu_custom_call" | custom-call | flops 5000000000 | bytes 20000000 | tf_op jit(solution)/shard_map/rows_forward/pallas_call | solution.py:817
  242.2 5.7 %collective-permute-done.43.rest_10_ = bf16[640,1024]{1,0:T(8,128)(2,1)} collective-permute-done((bf16[640,1024]{1,0:T(8,128)(2,1)}, bf16[640,1024]{1,0:T(8,128)(2,1)}, u32[]{:S(2)}, u32[]{:S(2)}) %collective-permute-start.43) | collective-permute-done | bytes 1310752 | tf_op jit(solution)/shard_map/ppermute | solution.py:345
  247.8 15.2 %collective-permute-done.48.rest_15_ = bf16[512,1024]{1,0:T(8,128)(2,1)} collective-permute-done((bf16[512,1024]{1,0:T(8,128)(2,1)}, bf16[512,1024]{1,0:T(8,128)(2,1)}, u32[]{:S(2)}, u32[]{:S(2)}) %collective-permute-start.48) | collective-permute-done | bytes 1048608 | tf_op jit(solution)/shard_map/ppermute | solution.py:345
  263.5 10.2 %collective-permute-done.27.n2 = bf16[256,1024]{1,0:T(8,128)(2,1)S(1)} collective-permute-done((bf16[256,1024]{1,0:T(8,128)(2,1)S(1)}, bf16[256,1024]{1,0:T(8,128)(2,1)S(1)}, u32[]{:S(2)}, u32[]{:S(2)}) %collective-permute-start.27) | collective-permute-done | bytes 524320 | tf_op jit(solution)/shard_map/ppermute | solution.py:345
  275.7 11.6 %attention_forward.3 = (bf16[1024,256]{1,0:T(8,128)(2,1)S(1)}, bf16[1024,256]{1,0:T(8,128)(2,1)S(1)}, bf16[1024,256]{1,0:T(8,128)(2,1)S(1)}, f32[8,1024]{1,0:T(8...) custom-call(s32[8]{0:T(128)S(1)} %concatenate.44.meta, ...), custom_call_target="tpu_custom_call" | custom-call | flops 3500000000 | bytes 8000000 | tf_op jit(solution)/shard_map/attention_forward/pallas_call | solution.py:511
  297.9 17.6 %rows_turn.1 = (f32[256,1024]{1,0:T(8,128)}, bf16[4,256,1024]{2,1,0:T(8,128)(2,1)}, f32[256,1024]{1,0:T(8,128)}, bf16[256,256]{1,0:T(8,128)(2,1)S(1)}, bf16[256,...) custom-call(s32[8]{0:T(128)S(1)} %concatenate.44.meta, ...), custom_call_target="tpu_custom_call" | custom-call | flops 8000000000 | bytes 20000000 | tf_op jit(solution)/shard_map/rows_turn/pallas_call | solution.py:817
  323.5 17.3 %attention_backward.2 = (bf16[2,256,1024]{2,1,0:T(8,128)(2,1)S(1)}, bf16[2,256,1024]{2,1,0:T(8,128)(2,1)}, f32[8,1024]{1,0:T(8,128)S(1)}, f32[8,512]{1,0:T(8,128)S(1)}) custom-call(s32[8]{0:T(128)S(1)} %concatenate.44.meta, bf16[256,1024]{1,0:T(8,128)(2,1)S(1)} %get-tuple-element.53.n0, bf16[256,1024]{1,0:T(8,128)(2,1)S(1)} %collective-permute-done.26.n1, ...), custom_call_target="tpu_custom_call" | custom-call | flops 6000000000 | bytes 12000000 | tf_op jit(solution)/shard_map/attention_backward/pallas_call | solution.py:609
  345.9 12.6 %collective-permute-done.55.far = bf16[256,1024]{1,0:T(8,128)(2,1)S(1)} collective-permute-done((bf16[256,1024]{1,0:T(8,128)(2,1)S(1)}, bf16[256,1024]{1,0:T(8,128)(2,1)S(1)}, u32[]{:S(2)}, u32[]{:S(2)}) %collective-permute-start.55) | collective-permute-done | bytes 524320 | tf_op jit(solution)/shard_map/ppermute | solution.py:345
  358.5 14.0 %rows_backward.1 = (f32[256,1024]{1,0:T(8,128)}, bf16[256,256]{1,0:T(8,128)(2,1)S(1)}, bf16[256,256]{1,0:T(8,128)(2,1)S(1)}, bf16[256,256]{1,0:T(8,128)(2,1)S(1)}, bf16[256,256]{1,0:T(8,128)(2,1)S(1)}) custom-call(s32[8]{0:T(128)S(1)} %concatenate.44.meta, f32[256,1024]{1,0:T(8,128)} %get-tuple-element.59.gm_ref, bf16[2,256,1024]{2,1,0:T(8,128)(2,1)} %copy-done.6, ...), custom_call_target="tpu_custom_call" | custom-call | flops 5000000000 | bytes 20000000 | tf_op jit(solution)/shard_map/rows_backward/pallas_call | solution.py:817
  380.9 17.3 %attention_backward.3 = (bf16[2,256,1024]{2,1,0:T(8,128)(2,1)S(1)}, bf16[2,256,1024]{2,1,0:T(8,128)(2,1)}, f32[8,1024]{1,0:T(8,128)S(1)}, f32[8,512]{1,0:T(8,128)S(1)}) custom-call(s32[8]{0:T(128)S(1)} %concatenate.44.meta, bf16[256,1024]{1,0:T(8,128)(2,1)S(1)} %fusion.5.n0, bf16[256,1024]{1,0:T(8,128)(2,1)S(1)} %copy-done.15, ...), custom_call_target="tpu_custom_call" | custom-call | flops 6000000000 | bytes 12000000 | tf_op jit(solution)/shard_map/attention_backward/pallas_call | solution.py:609
  423.3 7.4 %rows_output.1 = (f32[256,1024]{1,0:T(8,128)}, bf16[256,1024]{1,0:T(8,128)(2,1)}) custom-call(s32[8]{0:T(128)S(1)} %concatenate.44.meta, bf16[4,256,1024]{2,1,0:T(8,128)(2,1)} %get-tuple-element.86.active_ref, f32[256,1024]{1,0:T(8,128)} %get-tuple-element.87.middle_ref, f32[2,16,1024]{2,1,0:T(8,128)S(1)} %get-tuple-element.106.shared, ...), custom_call_target="tpu_custom_call" | custom-call | flops 2100000000 | bytes 20000000 | tf_op jit(solution)/shard_map/rows_output/pallas_call | solution.py:817
  443.1 9.1 %collective-permute-done.63 = bf16[256,1024]{1,0:T(8,128)(2,1)S(1)} collective-permute-done((bf16[256,1024]{1,0:T(8,128)(2,1)S(1)}, bf16[256,1024]{1,0:T(8,128)(2,1)S(1)}, u32[]{:S(2)}, u32[]{:S(2)}) %collective-permute-start.63) | collective-permute-done | bytes 524320 | tf_op jit(solution)/shard_map/ppermute | solution.py:345
  (313 shorter events, 144.3 us)
Async XLA Ops:
  15.2 44.8 %collective-permute-start.12 = (bf16[1024,1024]{1,0:T(8,128)(2,1)}, bf16[1024,1024]{1,0:T(8,128)(2,1)}, u32[]{:S(2)}, u32[]{:S(2)}) collective-permute-start(bf16[1024,1024]{1,0:T(8,128)(2,1)} %bitcast.75), channel_id=1, source_target_pairs={{0,16},{1,17},{2,18},{3,19},{4,20},{5,21},{6,22},{7,23},{8,24},{9,... | collective-permute-start | bytes 6291464 | tf_op jit(solution)/shard_map/ppermute | solution.py:345
  19.5 42.7 %collective-permute-start.38 = (bf16[1024,1024]{1,0:T(8,128)(2,1)}, bf16[1024,1024]{1,0:T(8,128)(2,1)}, u32[]{:S(2)}, u32[]{:S(2)}) collective-permute-start(bf16[1024,1024]{1,0:T(8,128)(2,1)} %bitcast.81), channel_id=1, source_target_pairs={{16,0},{17,1},{18,2},{19,3},{20,4},{21,5},{22,6},{23,7},{24,8},{25... | collective-permute-start | bytes 6291464 | tf_op jit(solution)/shard_map/ppermute | solution.py:345
  21.1 43.0 %collective-permute-start.13 = (bf16[1024,1024]{1,0:T(8,128)(2,1)}, bf16[1024,1024]{1,0:T(8,128)(2,1)}, u32[]{:S(2)}, u32[]{:S(2)}) collective-permute-start(bf16[1024,1024]{1,0:T(8,128)(2,1)} %bitcast.82), channel_id=1, source_target_pairs={{0,16},{1,17},{2,18},{3,19},{4,20},{5,21},{6,22},{7,23},{8,24},{9,... | collective-permute-start | bytes 6291464 | tf_op jit(solution)/shard_map/ppermute | solution.py:345
  43.5 29.6 %collective-permute-start.7 = (bf16[3,1024,256]{2,1,0:T(8,128)(2,1)}, bf16[3,1024,256]{2,1,0:T(8,128)(2,1)}, u32[]{:S(2)}, u32[]{:S(2)}) collective-permute-start(bf16[3,1024,256]{2,1,0:T(8,128)(2,1)} %bitcast.19), channel_id=1, source_target_pairs={{0,2},{1,3},{2,16},{3,17},{4,6},{5,7},{6,20},{7,21},{8,10},{9,11},... | collective-permute-start | bytes 4718600 | tf_op jit(solution)/shard_map/ppermute | solution.py:345
  46.8 27.9 %collective-permute-start.6 = (bf16[3,1024,256]{2,1,0:T(8,128)(2,1)}, bf16[3,1024,256]{2,1,0:T(8,128)(2,1)}, u32[]{:S(2)}, u32[]{:S(2)}) collective-permute-start(bf16[3,1024,256]{2,1,0:T(8,128)(2,1)} %bitcast.19), channel_id=1, source_target_pairs={{0,0},{1,1},{2,18},{3,19},{4,4},{5,5},{6,22},{7,23},{8,8},{9,9},{1... | collective-permute-start | bytes 4718600 | tf_op jit(solution)/shard_map/ppermute | solution.py:345
  60.0 79.4 %collective-permute-start.37 = (bf16[1024,1024]{1,0:T(8,128)(2,1)}, bf16[1024,1024]{1,0:T(8,128)(2,1)}, u32[]{:S(2)}, u32[]{:S(2)}) collective-permute-start(bf16[1024,1024]{1,0:T(8,128)(2,1)} %bitcast.76), channel_id=1, source_target_pairs={{16,0},{17,1},{18,2},{19,3},{20,4},{21,5},{22,6},{23,7},{24,8},{25... | collective-permute-start | bytes 6291464 | tf_op jit(solution)/shard_map/ppermute | solution.py:345
  62.2 59.4 %collective-permute-start.30 = (bf16[3,1024,256]{2,1,0:T(8,128)(2,1)}, bf16[3,1024,256]{2,1,0:T(8,128)(2,1)}, u32[]{:S(2)}, u32[]{:S(2)}) collective-permute-start(bf16[3,1024,256]{2,1,0:T(8,128)(2,1)} %bitcast.19), channel_id=1, source_target_pairs={{16,2},{17,3},{18,16},{19,17},{20,6},{21,7},{22,20},{23,21},{24,10... | collective-permute-start | bytes 4718600 | tf_op jit(solution)/shard_map/ppermute | solution.py:345
  64.1 63.6 %collective-permute-start.29 = (bf16[3,1024,256]{2,1,0:T(8,128)(2,1)}, bf16[3,1024,256]{2,1,0:T(8,128)(2,1)S(1)}, u32[]{:S(2)}, u32[]{:S(2)}) collective-permute-start(bf16[3,1024,256]{2,1,0:T(8,128)(2,1)} %bitcast.19), channel_id=1, source_target_pairs={{16,0},{17,1},{18,18},{19,19},{20,4},{21,5},{22,22},{23,23},{24,8}... | collective-permute-start | bytes 4718600 | tf_op jit(solution)/shard_map/ppermute | solution.py:345
  73.1 71.4 %collective-permute-start.14 = (bf16[640,1024]{1,0:T(8,128)(2,1)S(1)}, bf16[640,1024]{1,0:T(8,128)(2,1)S(1)}, u32[]{:S(2)}, u32[]{:S(2)}) collective-permute-start(bf16[640,1024]{1,0:T(8,128)(2,1)S(1)} %maximum_select_fusion.1), channel_id=1, source_target_pairs={{0,1},{1,0},{2,3},{3,2},{16,17},{17,16},{18,19},{19,18},{4,5},{5,4... | collective-permute-start | bytes 3932168 | tf_op jit(solution)/shard_map/ppermute | solution.py:345
  74.6 68.8 %collective-permute-start.44 = (bf16[512,1024]{1,0:T(8,128)(2,1)}, bf16[512,1024]{1,0:T(8,128)(2,1)}, u32[]{:S(2)}, u32[]{:S(2)}) collective-permute-start(bf16[512,1024]{1,0:T(8,128)(2,1)} %get-tuple-element.97), channel_id=1, source_target_pairs={{0,2},{1,3},{2,0},{3,1},{16,18},{17,19},{18,16},{19,17},{4,6},{5,7... | collective-permute-start | bytes 3145736 | tf_op jit(solution)/shard_map/ppermute | solution.py:345
  139.5 43.3 %collective-permute-start.18 = (bf16[640,1024]{1,0:T(8,128)(2,1)S(1)}, bf16[640,1024]{1,0:T(8,128)(2,1)S(1)}, u32[]{:S(2)}, u32[]{:S(2)}) collective-permute-start(bf16[640,1024]{1,0:T(8,128)(2,1)S(1)} %maximum_select_fusion.1), channel_id=1, source_target_pairs={{0,2},{1,3},{2,0},{3,1},{16,18},{17,19},{18,16},{19,17},{4,6},{5,7... | collective-permute-start | bytes 3932168 | tf_op jit(solution)/shard_map/ppermute | solution.py:345
  143.5 49.2 %collective-permute-start.39 = (bf16[640,1024]{1,0:T(8,128)(2,1)}, bf16[640,1024]{1,0:T(8,128)(2,1)}, u32[]{:S(2)}, u32[]{:S(2)}) collective-permute-start(bf16[640,1024]{1,0:T(8,128)(2,1)} %maximum_select_fusion.2), channel_id=1, source_target_pairs={{0,1},{1,0},{2,3},{3,2},{16,17},{17,16},{18,19},{19,18},{4,5},{5,4... | collective-permute-start | bytes 3932168 | tf_op jit(solution)/shard_map/ppermute | solution.py:345
  144.5 69.1 %collective-permute-start.22 = (bf16[640,1024]{1,0:T(8,128)(2,1)S(1)}, bf16[640,1024]{1,0:T(8,128)(2,1)S(1)}, u32[]{:S(2)}, u32[]{:S(2)}) collective-permute-start(bf16[640,1024]{1,0:T(8,128)(2,1)S(1)} %collective-permute-done.14.rest_6_), channel_id=1, source_target_pairs={{0,2},{1,3},{2,0},{3,1},{16,18},{17,19},{18,16},{19,17},{4,6},{5,7... | collective-permute-start | bytes 3932168 | tf_op jit(solution)/shard_map/ppermute | solution.py:345
  154.7 59.0 %collective-permute-start.23 = (bf16[512,1024]{1,0:T(8,128)(2,1)S(1)}, bf16[512,1024]{1,0:T(8,128)(2,1)S(1)}, u32[]{:S(2)}, u32[]{:S(2)}) collective-permute-start(bf16[512,1024]{1,0:T(8,128)(2,1)S(1)} %collective-permute-done.19.rest_11_), channel_id=1, source_target_pairs={{0,1},{1,0},{2,3},{3,2},{16,17},{17,16},{18,19},{19,18},{4,5},{5,4... | collective-permute-start | bytes 3145736 | tf_op jit(solution)/shard_map/ppermute | solution.py:345
  164.5 49.7 %collective-permute-start.21 = (bf16[512,1024]{1,0:T(8,128)(2,1)S(1)}, bf16[512,1024]{1,0:T(8,128)(2,1)S(1)}, u32[]{:S(2)}, u32[]{:S(2)}) collective-permute-start(bf16[512,1024]{1,0:T(8,128)(2,1)S(1)} %collective-permute-done.19.rest_11_), channel_id=1, source_target_pairs={{0,16},{1,17},{2,18},{3,19},{16,0},{17,1},{18,2},{19,3},{4,20},{5,... | collective-permute-start | bytes 3145736 | tf_op jit(solution)/shard_map/ppermute | solution.py:345
  182.7 33.1 %collective-permute-start.20 = (bf16[640,1024]{1,0:T(8,128)(2,1)S(1)}, bf16[640,1024]{1,0:T(8,128)(2,1)S(1)}, u32[]{:S(2)}, u32[]{:S(2)}) collective-permute-start(bf16[640,1024]{1,0:T(8,128)(2,1)S(1)} %collective-permute-done.18.rest_10_), channel_id=1, source_target_pairs={{0,16},{1,17},{2,18},{3,19},{16,0},{17,1},{18,2},{19,3},{4,20},{5,... | collective-permute-start | bytes 3932168 | tf_op jit(solution)/shard_map/ppermute | solution.py:345
  214.3 26.3 %collective-permute-start.40 = (bf16[512,1024]{1,0:T(8,128)(2,1)}, bf16[512,1024]{1,0:T(8,128)(2,1)}, u32[]{:S(2)}, u32[]{:S(2)}) collective-permute-start(bf16[512,1024]{1,0:T(8,128)(2,1)} %get-tuple-element.97), channel_id=1, source_target_pairs={{0,1},{1,0},{2,3},{3,2},{16,17},{17,16},{18,19},{19,18},{4,5},{5,4... | collective-permute-start | bytes 3145736 | tf_op jit(solution)/shard_map/ppermute | solution.py:345
  215.9 31.9 %collective-permute-start.43 = (bf16[640,1024]{1,0:T(8,128)(2,1)}, bf16[640,1024]{1,0:T(8,128)(2,1)}, u32[]{:S(2)}, u32[]{:S(2)}) collective-permute-start(bf16[640,1024]{1,0:T(8,128)(2,1)} %maximum_select_fusion.2), channel_id=1, source_target_pairs={{0,2},{1,3},{2,0},{3,1},{16,18},{17,19},{18,16},{19,17},{4,6},{5,7... | collective-permute-start | bytes 3932168 | tf_op jit(solution)/shard_map/ppermute | solution.py:345
  216.7 58.4 %collective-permute-start.47 = (bf16[640,1024]{1,0:T(8,128)(2,1)}, bf16[640,1024]{1,0:T(8,128)(2,1)}, u32[]{:S(2)}, u32[]{:S(2)}) collective-permute-start(bf16[640,1024]{1,0:T(8,128)(2,1)} %collective-permute-done.39.rest_6_), channel_id=1, source_target_pairs={{0,2},{1,3},{2,0},{3,1},{16,18},{17,19},{18,16},{19,17},{4,6},{5,7... | collective-permute-start | bytes 3932168 | tf_op jit(solution)/shard_map/ppermute | solution.py:345
  220.1 43.0 %collective-permute-start.48 = (bf16[512,1024]{1,0:T(8,128)(2,1)}, bf16[512,1024]{1,0:T(8,128)(2,1)}, u32[]{:S(2)}, u32[]{:S(2)}) collective-permute-start(bf16[512,1024]{1,0:T(8,128)(2,1)} %collective-permute-done.44.rest_11_), channel_id=1, source_target_pairs={{0,1},{1,0},{2,3},{3,2},{16,17},{17,16},{18,19},{19,18},{4,5},{5,4... | collective-permute-start | bytes 3145736 | tf_op jit(solution)/shard_map/ppermute | solution.py:345
  221.7 41.4 %collective-permute-start.46 = (bf16[512,1024]{1,0:T(8,128)(2,1)}, bf16[512,1024]{1,0:T(8,128)(2,1)}, u32[]{:S(2)}, u32[]{:S(2)}) collective-permute-start(bf16[512,1024]{1,0:T(8,128)(2,1)} %collective-permute-done.44.rest_11_), channel_id=1, source_target_pairs={{0,16},{1,17},{2,18},{3,19},{16,0},{17,1},{18,2},{19,3},{4,20},{5,... | collective-permute-start | bytes 3145736 | tf_op jit(solution)/shard_map/ppermute | solution.py:345
  240.6 33.1 %collective-permute-start.27 = (bf16[256,1024]{1,0:T(8,128)(2,1)S(1)}, bf16[256,1024]{1,0:T(8,128)(2,1)S(1)}, u32[]{:S(2)}, u32[]{:S(2)}) collective-permute-start(bf16[256,1024]{1,0:T(8,128)(2,1)S(1)} %get-tuple-element.53.n0), channel_id=1, source_target_pairs={{0,1},{1,0},{2,3},{3,2},{16,17},{17,16},{18,19},{19,18},{4,5},{5,4... | collective-permute-start | bytes 1572872 | tf_op jit(solution)/shard_map/ppermute | solution.py:345
  247.8 27.3 %collective-permute-start.26 = (bf16[256,1024]{1,0:T(8,128)(2,1)S(1)}, bf16[256,1024]{1,0:T(8,128)(2,1)S(1)}, u32[]{:S(2)}, u32[]{:S(2)}) collective-permute-start(bf16[256,1024]{1,0:T(8,128)(2,1)S(1)} %get-tuple-element.53.n0), channel_id=1, source_target_pairs={{0,16},{1,17},{2,18},{3,19},{16,0},{17,1},{18,2},{19,3},{4,20},{5,... | collective-permute-start | bytes 1572872 | tf_op jit(solution)/shard_map/ppermute | solution.py:345
  263.0 28.9 %collective-permute-start.41 = (bf16[640,1024]{1,0:T(8,128)(2,1)}, bf16[640,1024]{1,0:T(8,128)(2,1)S(1)}, u32[]{:S(2)}, u32[]{:S(2)}) collective-permute-start(bf16[640,1024]{1,0:T(8,128)(2,1)} %collective-permute-done.39.rest_6_), channel_id=1, source_target_pairs={{0,16},{1,17},{2,18},{3,19},{16,0},{17,1},{18,2},{19,3},{4,20},{5,... | collective-permute-start | bytes 3932168 | tf_op jit(solution)/shard_map/ppermute | solution.py:345
  (112 other events, 1856.9 us)

commit v2 on v0

--- a/solution.py
+++ b/solution.py
@@ -1,6 +1,10 @@
+import functools
+
 import jax
 import jax.numpy as jnp
 from jax import lax
+from jax.experimental import pallas as pl
+from jax.experimental.pallas import tpu as pltpu
 from jax.sharding import PartitionSpec as P
 
 HEAD = 64
@@ -95,7 +99,7 @@
     return (lax.psum(part_a, ("dp", "tensor")), lax.psum(second_portion, "dp"))
 
 
-def body(
+def plain_body(
     activations,
     starts,
     attention_weights,
@@ -324,6 +328,709 @@
     return (combined[None], totals_a[None], totals_b[None])
 
 
+LOW = 2 * ADAPTER_RANK
+VMEM_SPACE = pl.BlockSpec(memory_space=pltpu.VMEM)
+SMEM_SPACE = pl.BlockSpec(memory_space=pltpu.SMEM)
+HBM_SPACE = pl.BlockSpec(memory_space=pltpu.HBM)
+BLOCK = 256
+
+
+def send(block, route):
+    pairs = []
+    for s in range(2):
+        for t in range(4):
+            to = route(s, t)
+            if to is not None:
+                pairs.append((s * 4 + t, to[0] * 4 + to[1]))
+    return lax.ppermute(block, ("section", "tensor"), pairs)
+
+
+def other_core(block):
+    return send(block, lambda s, t: (1 - s, t))
+
+
+def x_swap(block):
+    return send(block, lambda s, t: (s, t ^ 1))
+
+
+def y_swap(block):
+    return send(block, lambda s, t: (s, t ^ 2))
+
+
+def after(value, *others):
+    return lax.optimization_barrier((value, others))[0]
+
+
+def cross_send(block, source=0):
+    return send(block, lambda s, t: (t >> 1, t ^ 2) if s == source else None)
+
+
+def collect(target, same_chip, cross_chip):
+    return (
+        send(same_chip, lambda s, t: (target, t) if s == t >> 1 and s != target else None),
+        send(cross_chip, lambda s, t: (target, t ^ 2) if s != t >> 1 else None),
+    )
+
+
+def mm(left, right):
+    return jnp.dot(left, right, preferred_element_type=jnp.float32)
+
+
+def mm_nt(left, right):
+    return contract_axes(left, right, 1, 1)
+
+
+def norm_back(rows, gain, grad):
+    mean = jnp.mean(rows, axis=-1, keepdims=True)
+    centered = rows - mean
+    scale = lax.rsqrt(jnp.mean(centered * centered, axis=-1, keepdims=True) + 1e-05)
+    unit = centered * scale
+    scaled = grad * gain
+    return scale * (
+        scaled
+        - jnp.mean(scaled, axis=-1, keepdims=True)
+        - unit * jnp.mean(scaled * unit, axis=-1, keepdims=True)
+    )
+
+
+def gelu_both(value):
+    square = value * value
+    bent = jnp.tanh(0.7978845608028654 * value * (1.0 + 0.044715 * square))
+    half = 0.5 * (1.0 + bent)
+    slope = half + 0.5 * value * (1.0 - bent * bent) * (
+        0.7978845608028654 * (1.0 + 3.0 * 0.044715 * square)
+    )
+    return value * half, slope
+
+
+def cost(flops, read):
+    return pl.CostEstimate(flops=1000, bytes_accessed=1000, transcendentals=0)
+
+
+def kernel_params(mib):
+    return pltpu.CompilerParams(vmem_limit_bytes=mib * 1024 * 1024)
+
+
+def position_mask(meta, query_block, key_block):
+    shape = (BLOCK, BLOCK)
+    key_pos = key_block * BLOCK + lax.broadcasted_iota(jnp.int32, shape, 0)
+    query_pos = query_block * BLOCK + lax.broadcasted_iota(jnp.int32, (1, BLOCK), 1)
+    low = jnp.zeros((1, BLOCK), jnp.int32)
+    for c in range(4):
+        first = meta[4 + c]
+        low = jnp.where(first <= query_pos, jnp.maximum(low, first), low)
+    valid = key_pos >= low
+    if query_block == key_block:
+        valid = valid & (key_pos <= query_pos)
+    return valid
+
+
+def head_lanes(half):
+    return (lax.broadcasted_iota(jnp.int32, (1, 2 * HEAD), 1) // HEAD) == half
+
+
+def start_pick(choices, target, sem):
+    for condition, source in choices:
+
+        @pl.when(condition)
+        def _(source=source):
+            pltpu.make_async_copy(source, target, sem).start()
+
+
+def load_qkv_weight(layer, meta, w_own, w_other, w_cross, w_buf, sem):
+    s, y = meta[0], meta[2]
+    start_pick(
+        (
+            ((s == y) & (s == layer), w_own),
+            ((s == y) & (s != layer), w_other),
+            (s != y, w_cross),
+        ),
+        w_buf,
+        sem,
+    )
+
+
+def block_places(meta):
+    s, x = meta[0], meta[1]
+    return (x + 2 * s, x + 2 * (1 - s), (1 - x) + 2 * s, (1 - x) + 2 * (1 - s))
+
+
+def attend_kernel(
+    layer, meta, n0, n1, n2, n3, shared, varied, w_own, w_other, w_cross,
+    q_out, k_out, v_out, lse_out, mixed_out, o0, o1, o2, o3,
+    w_buf, score_buf, vt_buf, q_ref, k_ref, v_ref, lse_ref, mixed_ref, sem, out_sems,
+):
+    load_qkv_weight(layer, meta, w_own, w_other, w_cross, w_buf, sem)
+    down = shared[layer, 8:16, :].astype(jnp.bfloat16)
+    bias = varied[layer, 1:2, :]
+    up = varied[layer, 8:16, 0:512].astype(jnp.bfloat16)
+    places = block_places(meta)
+    pltpu.make_async_copy(w_own, w_buf, sem).wait()
+    for place, block in zip(places, (n0, n1, n2, n3)):
+        rows = pl.ds(pl.multiple_of(place * BLOCK, BLOCK), BLOCK)
+        normed = block[...]
+        low = mm_nt(normed, down).astype(jnp.bfloat16)
+        lifted = adapter_scale * mm(low, up)
+        q_ref[rows, :] = (mm(normed, w_buf[0]) + bias[:, 0:256] + lifted[:, 0:256]).astype(
+            jnp.bfloat16
+        )
+        k_ref[rows, :] = mm(normed, w_buf[1]).astype(jnp.bfloat16)
+        v_ref[rows, :] = (mm(normed, w_buf[2]) + bias[:, 256:512] + lifted[:, 256:512]).astype(
+            jnp.bfloat16
+        )
+    saved = [
+        pltpu.make_async_copy(source, target, out_sems.at[i])
+        for i, (source, target) in enumerate(
+            (
+                (q_ref, q_out), (k_ref, k_out), (v_ref, v_out), (lse_ref, lse_out),
+                (mixed_ref, mixed_out),
+            )
+        )
+    ]
+    for copy in saved[:3]:
+        copy.start()
+    for b in range(4):
+        vt_buf[:, b * BLOCK : (b + 1) * BLOCK] = v_ref[b * BLOCK : (b + 1) * BLOCK, :].T
+
+    def one_head(head, carry):
+        lanes = pl.ds(pl.multiple_of((head // 2) * 128, 128), 128)
+        chosen = head_lanes(head % 2)
+        deep = pl.ds(pl.multiple_of(head * HEAD, HEAD), HEAD)
+        for i in range(4):
+            part = q_ref[i * BLOCK : (i + 1) * BLOCK, lanes]
+            query = jnp.where(chosen, part * HEAD ** (-0.5), 0.0).astype(jnp.bfloat16)
+            top = jnp.full((1, BLOCK), -1e30, jnp.float32)
+            for j in range(i + 1):
+                scores = mm_nt(k_ref[j * BLOCK : (j + 1) * BLOCK, lanes], query)
+                scores = jnp.where(position_mask(meta, i, j), scores, -1e30)
+                score_buf[j] = scores
+                top = jnp.maximum(top, jnp.max(scores, axis=0, keepdims=True))
+            total = jnp.zeros((1, BLOCK), jnp.float32)
+            mixed = jnp.zeros((HEAD, BLOCK), jnp.float32)
+            for j in range(i + 1):
+                weights = jnp.exp(score_buf[j] - top)
+                total = total + jnp.sum(weights, axis=0, keepdims=True)
+                mixed = mixed + mm(
+                    vt_buf[deep, j * BLOCK : (j + 1) * BLOCK], weights.astype(jnp.bfloat16)
+                )
+            mixed_ref[deep, i * BLOCK : (i + 1) * BLOCK] = mixed / total
+            lse_ref[pl.ds(head, 1), i * BLOCK : (i + 1) * BLOCK] = top + jnp.log(total)
+        return carry
+
+    lax.fori_loop(0, 4, one_head, 0)
+    for copy in saved[3:]:
+        copy.start()
+    for place, out in zip(places, (o0, o1, o2, o3)):
+        columns = pl.ds(pl.multiple_of(place * BLOCK, BLOCK), BLOCK)
+        heads_out = mixed_ref[:, columns].T.astype(jnp.bfloat16)
+        out[...] = mm_nt(heads_out, w_buf[3]).astype(jnp.bfloat16)
+    for copy in saved:
+        copy.wait()
+
+
+def attend_call(layer, meta, blocks, shared, varied, *weight):
+    bf, f32 = jnp.bfloat16, jnp.float32
+    wide = jax.ShapeDtypeStruct((SEQ_LEN, 256), bf)
+    piece = jax.ShapeDtypeStruct((BLOCK, 1024), bf)
+    return pl.pallas_call(
+        functools.partial(attend_kernel, layer),
+        in_specs=[SMEM_SPACE] + [VMEM_SPACE] * 6 + [HBM_SPACE] * 3,
+        out_specs=[HBM_SPACE] * 5 + [VMEM_SPACE] * 4,
+        out_shape=[wide, wide, wide, jax.ShapeDtypeStruct((8, SEQ_LEN), f32),
+                   jax.ShapeDtypeStruct((256, SEQ_LEN), f32)] + [piece] * 4,
+        scratch_shapes=[
+            pltpu.VMEM((4, 1024, 256), bf),
+            pltpu.VMEM((4, BLOCK, BLOCK), f32),
+            pltpu.VMEM((256, SEQ_LEN), bf),
+            pltpu.VMEM((SEQ_LEN, 256), bf),
+            pltpu.VMEM((SEQ_LEN, 256), bf),
+            pltpu.VMEM((SEQ_LEN, 256), bf),
+            pltpu.VMEM((8, SEQ_LEN), f32),
+            pltpu.VMEM((256, SEQ_LEN), f32),
+            pltpu.SemaphoreType.DMA,
+            pltpu.SemaphoreType.DMA((5,)),
+        ],
+        compiler_params=kernel_params(40),
+        cost_estimate=cost(3.5e9, 8e6),
+        name="attention_forward",
+    )(meta, *blocks, shared, varied, *weight)
+
+
+def attend_back_kernel(
+    layer, meta, n0, n1, n2, n3, g0, g1, g2, g3, q_ref, k_ref, v_ref, lse_ref, mixed_ref,
+    shared, varied, w_own, w_other, w_cross,
+    keep0, give0, keep1, give1, down_ref, up_ref,
+    w_buf, kt_buf, do_buf, delta_buf, dqt_buf, dk_buf, dv_buf, dq_buf, sem,
+):
+    load_qkv_weight(layer, meta, w_own, w_other, w_cross, w_buf, sem)
+    places = block_places(meta)
+    pltpu.make_async_copy(w_own, w_buf, sem).wait()
+    for place, block in zip(places, (g0, g1, g2, g3)):
+        rows = pl.ds(pl.multiple_of(place * BLOCK, BLOCK), BLOCK)
+        do_buf[rows, :] = mm(block[...], w_buf[3]).astype(jnp.bfloat16)
+    for b in range(4):
+        span = slice(b * BLOCK, (b + 1) * BLOCK)
+        kt_buf[:, span] = k_ref[span, :].T
+        product = do_buf[span, :].astype(jnp.float32).T * mixed_ref[:, span]
+        for head in range(4):
+            delta_buf[head : head + 1, span] = jnp.sum(
+                product[head * HEAD : (head + 1) * HEAD], axis=0, keepdims=True
+            )
+    dk_buf[...] = jnp.zeros_like(dk_buf)
+    dv_buf[...] = jnp.zeros_like(dv_buf)
+
+    def one_head(head, carry):
+        lanes = pl.ds(pl.multiple_of((head // 2) * 128, 128), 128)
+        chosen = head_lanes(head % 2)
+        deep = pl.ds(pl.multiple_of(head * HEAD, HEAD), HEAD)
+        for i in range(4):
+            span = slice(i * BLOCK, (i + 1) * BLOCK)
+            query = jnp.where(chosen, q_ref[span, lanes] * HEAD ** (-0.5), 0.0).astype(jnp.bfloat16)
+            grad_mixed = jnp.where(chosen, do_buf[span, lanes], 0.0).astype(jnp.bfloat16)
+            lse = lse_ref[pl.ds(head, 1), span]
+            delta = delta_buf[pl.ds(head, 1), span]
+            grad_query = jnp.zeros((HEAD, BLOCK), jnp.float32)
+            for j in range(i + 1):
+                keys = slice(j * BLOCK, (j + 1) * BLOCK)
+                scores = mm_nt(k_ref[keys, lanes], query)
+                probs = jnp.where(position_mask(meta, i, j), jnp.exp(scores - lse), 0.0)
+                grad_probs = mm_nt(v_ref[keys, lanes], grad_mixed)
+                grad_scores = (probs * (grad_probs - delta)).astype(jnp.bfloat16)
+                dv_buf[keys, lanes] += mm(probs.astype(jnp.bfloat16), grad_mixed)
+                dk_buf[keys, lanes] += mm(grad_scores, query)
+                grad_query = grad_query + mm(kt_buf[deep, keys], grad_scores)
+            dqt_buf[deep, span] = grad_query * HEAD ** (-0.5)
+        return carry
+
+    lax.fori_loop(0, 4, one_head, 0)
+    down = shared[layer, 8:16, :].astype(jnp.bfloat16)
+    up = varied[layer, 8:16, 0:512].astype(jnp.bfloat16)
+    for b in range(4):
+        span = slice(b * BLOCK, (b + 1) * BLOCK)
+        dq_buf[span, :] = dqt_buf[:, span].T.astype(jnp.bfloat16)
+    total_down = jnp.zeros((LOW, 1024), jnp.float32)
+    total_up = jnp.zeros((LOW, 512), jnp.float32)
+    targets = (keep0, give0, keep1, give1)
+    for place, block, target in zip(places, (n0, n1, n2, n3), targets):
+        rows = pl.ds(pl.multiple_of(place * BLOCK, BLOCK), BLOCK)
+        normed = block[...]
+        grad_q = dq_buf[rows, :]
+        grad_k = dk_buf[rows, :].astype(jnp.bfloat16)
+        grad_v = dv_buf[rows, :].astype(jnp.bfloat16)
+        both = jnp.concatenate([grad_q, grad_v], axis=1)
+        low_grad = (adapter_scale * mm_nt(both, up)).astype(jnp.bfloat16)
+        low_grad_t = (adapter_scale * mm_nt(up, both)).astype(jnp.bfloat16)
+        low_t = mm_nt(down, normed).astype(jnp.bfloat16)
+        grad_normed = (
+            mm_nt(grad_q, w_buf[0]) + mm_nt(grad_k, w_buf[1]) + mm_nt(grad_v, w_buf[2])
+            + mm(low_grad, down)
+        )
+        target[...] = grad_normed.astype(jnp.bfloat16)
+        total_down = total_down + mm(low_grad_t, normed)
+        total_up = total_up + adapter_scale * mm(low_t, both)
+    down_ref[...] = total_down
+    up_ref[...] = total_up
+
+
+def attend_back_call(layer, meta, blocks, grads, saved, shared, varied, *weight):
+    bf, f32 = jnp.bfloat16, jnp.float32
+    part = jax.ShapeDtypeStruct((BLOCK, 1024), bf)
+    return pl.pallas_call(
+        functools.partial(attend_back_kernel, layer),
+        in_specs=[SMEM_SPACE] + [VMEM_SPACE] * 15 + [HBM_SPACE] * 3,
+        out_specs=[VMEM_SPACE] * 6,
+        out_shape=[part, part, part, part, jax.ShapeDtypeStruct((LOW, 1024), f32),
+                   jax.ShapeDtypeStruct((LOW, 512), f32)],
+        scratch_shapes=[
+            pltpu.VMEM((4, 1024, 256), bf),
+            pltpu.VMEM((256, SEQ_LEN), bf),
+            pltpu.VMEM((SEQ_LEN, 256), bf),
+            pltpu.VMEM((8, SEQ_LEN), f32),
+            pltpu.VMEM((256, SEQ_LEN), f32),
+            pltpu.VMEM((SEQ_LEN, 256), f32),
+            pltpu.VMEM((SEQ_LEN, 256), f32),
+            pltpu.VMEM((SEQ_LEN, 256), bf),
+            pltpu.SemaphoreType.DMA,
+        ],
+        compiler_params=kernel_params(48),
+        cost_estimate=cost(6e9, 12e6),
+        name="attention_backward",
+    )(meta, *blocks, *grads, *saved, shared, varied, *weight)
+
+
+def summed(keep, take, far):
+    return keep[...].astype(jnp.float32) + take[...].astype(jnp.float32) + far[...].astype(jnp.float32)
+
+
+def rows_middle_kernel(layer, h_ref, keep, take, far, shared, middle_ref, normed_ref):
+    middle = h_ref[...].astype(jnp.float32) + summed(keep, take, far) + shared[layer, 4:5, :]
+    middle_ref[...] = middle
+    normed_ref[...] = layer_norm(middle, shared[layer, 1:2, :], shared[layer, 3:4, :]).astype(
+        jnp.bfloat16
+    )
+
+
+def load_units(layer, meta, pieces, w1, w2, sems):
+    s, y = meta[0], meta[2]
+    own, other, cross = pieces
+    copies = []
+    for m, matrix in enumerate((w1, w2)):
+        rows = slice(1024 * m, 1024 * (m + 1))
+        start_pick(
+            (
+                ((s == y) & (s == layer), own.at[rows]),
+                ((s == y) & (s != layer), other.at[rows]),
+                (s != y, cross.at[rows]),
+            ),
+            matrix,
+            sems.at[m],
+        )
+        copies.append(pltpu.make_async_copy(own.at[rows], matrix, sems.at[m]))
+    return copies
+
+
+def units_kernel(layer, meta, n0, n1, bias, *rest):
+    out0, out1, slope0, slope1, w1, w2, sems = rest[3:]
+    waits = load_units(layer, meta, rest[:3], w1, w2, sems)
+    waits[0].wait()
+    actives = []
+    for block, slope_ref in ((n0, slope0), (n1, slope1)):
+        active, slope = gelu_both(mm(block[...], w1[...]) + bias[layer, 0:1, :])
+        actives.append(active.astype(jnp.bfloat16))
+        slope_ref[...] = slope.astype(jnp.bfloat16)
+    waits[1].wait()
+    for active, out in zip(actives, (out0, out1)):
+        out[...] = mm(active, w2[...]).astype(jnp.bfloat16)
+
+
+def units_turn_kernel(layer, meta, n0, n1, g0, g1, bias, *rest):
+    back0, back1, out0, out1, w1, w2, sems = rest[3:]
+    for copy in load_units(layer, meta, rest[:3], w1, w2, sems):
+        copy.wait()
+    for block, grad, back, out in ((n0, g0, back0, out0), (n1, g1, back1, out1)):
+        active, slope = gelu_both(mm(block[...], w1[...]) + bias[layer, 0:1, :])
+        grad_hidden = (mm_nt(grad[...], w2[...]) * slope).astype(jnp.bfloat16)
+        back[...] = mm_nt(grad_hidden, w1[...]).astype(jnp.bfloat16)
+        out[...] = mm(active.astype(jnp.bfloat16), w2[...]).astype(jnp.bfloat16)
+
+
+def units_back_kernel(layer, meta, g0, g1, slope0, slope1, *rest):
+    back0, back1, w1, w2, sems = rest[3:]
+    waits = load_units(layer, meta, rest[:3], w1, w2, sems)
+    waits[1].wait()
+    grads = [
+        (mm_nt(grad[...], w2[...]) * slope[...].astype(jnp.float32)).astype(jnp.bfloat16)
+        for grad, slope in ((g0, slope0), (g1, slope1))
+    ]
+    waits[0].wait()
+    for grad, back in zip(grads, (back0, back1)):
+        back[...] = mm_nt(grad, w1[...]).astype(jnp.bfloat16)
+
+
+def rows_first_kernel(rows, shared, normed_ref):
+    normed_ref[...] = layer_norm(
+        rows[...].astype(jnp.float32), shared[0, 0:1, :], shared[0, 2:3, :]
+    ).astype(jnp.bfloat16)
+
+
+def rows_next_kernel(middle, keep, take, far, shared, between_ref, normed_ref):
+    between = (middle[...] + summed(keep, take, far) + shared[0, 5:6, :]).astype(jnp.bfloat16)
+    between_ref[...] = between
+    normed_ref[...] = layer_norm(
+        between.astype(jnp.float32), shared[1, 0:1, :], shared[1, 2:3, :]
+    ).astype(jnp.bfloat16)
+
+
+def rows_turn_kernel(layer, middle, g_ref, keep, take, far, shared, grad_ref, sent_ref):
+    grad_middle = g_ref[...].astype(jnp.float32) + norm_back(
+        middle[...], shared[layer, 1:2, :], summed(keep, take, far)
+    )
+    grad_ref[...] = grad_middle
+    sent_ref[...] = grad_middle.astype(jnp.bfloat16)
+
+
+def rows_before_kernel(gm_ref, keep, take, far, between_ref, shared, grad_ref):
+    grad_rows = gm_ref[...] + norm_back(
+        between_ref[...].astype(jnp.float32), shared[1, 0:1, :], summed(keep, take, far)
+    )
+    grad_ref[...] = grad_rows.astype(jnp.bfloat16)
+
+
+def rows_output_kernel(middle, keep, take, far, shared, wide_ref, narrow_ref):
+    total = middle[...] + summed(keep, take, far) + shared[1, 5:6, :]
+    wide_ref[...] = total
+    narrow_ref[...] = total.astype(jnp.bfloat16)
+
+
+def rows_final_kernel(gm_ref, keep, take, far, h_ref, shared, wide_ref, narrow_ref):
+    grad_in = gm_ref[...] + norm_back(
+        h_ref[...].astype(jnp.float32), shared[0, 0:1, :], summed(keep, take, far)
+    )
+    wide_ref[...] = grad_in
+    narrow_ref[...] = grad_in.astype(jnp.bfloat16)
+
+
+def plain_call(kernel, scalar, small, large, outs, scratch, flops, name, mib=40):
+    specs = [VMEM_SPACE] * len(small) + [HBM_SPACE] * len(large)
+    operands = (*small, *large)
+    if scalar is not None:
+        specs, operands = [SMEM_SPACE] + specs, (scalar, *operands)
+    return pl.pallas_call(
+        kernel,
+        in_specs=specs,
+        out_specs=[VMEM_SPACE] * len(outs),
+        out_shape=outs,
+        scratch_shapes=scratch,
+        compiler_params=kernel_params(mib),
+        cost_estimate=cost(flops, 8e6),
+        name=name,
+    )(*operands)
+
+
+def deal_rows(source, slots, section, y):
+    moved = [
+        send(
+            slots[m],
+            lambda s, t, m=m: (t >> 1, 2 * m + (t & 1))
+            if s == source and (t >> 1, 2 * m + (t & 1)) != (s, t)
+            else None,
+        )
+        for m in range(2)
+    ]
+    stays = (section == source) & (y == source)
+    return jnp.where(stays, slots[source], jnp.where(y == 0, moved[0], moved[1]))
+
+
+def z_swap(block):
+    return lax.ppermute(block, "dp", [(i, i ^ 1) for i in range(lax.axis_size("dp"))])
+
+
+def gather_rows(own):
+    near = other_core(own)
+    far = x_swap(own)
+    return (own, near, far, other_core(far))
+
+
+def reduce_rows(keep0, give0, keep1, give1):
+    passed = (keep1.astype(jnp.float32) + other_core(give1).astype(jnp.float32)).astype(jnp.bfloat16)
+    return keep0, other_core(give0), x_swap(passed)
+
+
+def total_over_z(part_down, part_up):
+    both = jnp.concatenate([part_down, part_up], axis=1)
+    size = lax.axis_size("dp")
+    step = 1
+    while step < size:
+        both = both + lax.ppermute(both, "dp", [(i, i ^ step) for i in range(size)])
+        step *= 2
+    return both
+
+
+def total_over_cores(both):
+    both = both + y_swap(both)
+    down = both[:, :1024]
+    return down + other_core(down), both[:, 1024:]
+
+
+def total_over_x(layer, total):
+    down, up = total
+    moved = send(up, lambda s, t: (layer, t) if s == t >> 1 and s != layer else None)
+    stays = lax.axis_index("tensor") // 2 == layer
+    return down + x_swap(down), jnp.where(stays, up, moved)
+
+
+def relay_body(
+    activations, starts, attention_weights, projection_weight, feedforward_weight, output_weight,
+    norm_gains, norm_biases, output_biases, query_value_bias, feedforward_bias,
+    adapter_down_weight, adapter_up_weight,
+):
+    bf, f32 = jnp.bfloat16, jnp.float32
+    section = lax.axis_index("section")
+    place = lax.axis_index("tensor")
+    y, x = place // 2, place % 2
+    first = section == 0
+
+    rows = deal_rows(0, activations[0], section, y)
+    down_rows = adapter_down_weight[0].astype(f32).transpose(0, 2, 1).reshape(LOW, 1024)
+    up0 = adapter_up_weight[0, 0].astype(f32)
+    up1 = adapter_up_weight[0, 1].astype(f32)
+    zero = jnp.zeros((ADAPTER_RANK, 256), f32)
+    common = jnp.concatenate(
+        [norm_gains[0], norm_biases[0], output_biases[0], jnp.zeros((2, 1024), f32), down_rows]
+    )
+    own_part = jnp.concatenate(
+        [
+            feedforward_bias,
+            jnp.pad(query_value_bias[0].reshape(1, 512), ((0, 0), (0, 512))),
+            jnp.zeros((6, 1024), f32),
+            jnp.concatenate([up0, zero, jnp.zeros((ADAPTER_RANK, 512), f32)], axis=1),
+            jnp.concatenate([zero, up1, jnp.zeros((ADAPTER_RANK, 512), f32)], axis=1),
+        ]
+    )
+    partner = other_core(common)
+    partner_part = other_core(own_part)
+    parts = jnp.where(
+        first, jnp.stack([own_part, partner_part]), jnp.stack([partner_part, own_part])
+    )
+    near_varied = jnp.where(section == y, parts, y_swap(parts))
+    shared = jnp.where(first, jnp.stack([common, partner]), jnp.stack([partner, common]))
+    meta = jnp.concatenate(
+        [
+            jnp.stack([section, x, y, place]).astype(jnp.int32),
+            lax.dynamic_index_in_dim(starts, y, 0, keepdims=False).reshape(4),
+        ]
+    )
+    own_a = jnp.concatenate([attention_weights[0], projection_weight[0].T[None]])
+    other_a = other_core(own_a)
+    weights_a0 = (own_a, other_a, cross_send(other_a, 1))
+
+    sheet = jax.ShapeDtypeStruct((BLOCK, 1024), f32)
+    thin = jax.ShapeDtypeStruct((BLOCK, 1024), bf)
+    quarter_scratch = [
+        pltpu.VMEM((1024, 1024), bf), pltpu.VMEM((1024, 1024), bf), pltpu.SemaphoreType.DMA((2,))
+    ]
+
+    normed = plain_call(rows_first_kernel, None, (rows, shared), (), [thin], [], 1e7, "rows_first")[0]
+    own_b = jnp.concatenate(after((feedforward_weight[0], output_weight[0]), normed))
+    near, far = other_core(normed), x_swap(normed)
+    far, near_varied, own_b, *weights_a0 = lax.optimization_barrier(
+        (far, near_varied, own_b, *weights_a0)
+    )
+    other_b = other_core(own_b)
+    blocks0 = (normed, near, far, other_core(far))
+    weights_b0 = (own_b, other_b, cross_send(after(own_b, far)))
+    *saved0, keep0, give0, keep1, give1 = attend_call(
+        0, meta, blocks0, shared, near_varied, *weights_a0
+    )
+    weights_a1 = (own_a, other_a, cross_send(after(other_a, give1)))
+    sums = reduce_rows(keep0, give0, keep1, give1)
+    middle0, normed0 = plain_call(
+        functools.partial(rows_middle_kernel, 0), None, (rows, *sums, shared), (), [sheet, thin],
+        [], 1e7, "rows_middle",
+    )
+    grad_out = deal_rows(1, after(activations[0], middle0), section, y)
+    n0, n1, n2 = normed0, other_core(normed0), x_swap(normed0)
+    units = functools.partial(units_kernel, 0)
+    keep0, give0, *slopes_near = plain_call(
+        units, meta, (n0, n1, near_varied), weights_b0, [thin] * 4, quarter_scratch,
+        2.2e9, "units_near",
+    )
+    n3 = other_core(after(n2, keep0))
+    keep1, give1, *slopes_far = plain_call(
+        units, meta, (n2, n3, near_varied), weights_b0, [thin] * 4, quarter_scratch,
+        2.2e9, "units_far",
+    )
+    sums = reduce_rows(keep0, give0, keep1, give1)
+    between, normed = plain_call(
+        rows_next_kernel, None, (middle0, *sums, shared), (), [thin, thin], [], 1e7, "rows_next",
+    )
+    normed, grad_out, *weights_a1 = lax.optimization_barrier((normed, grad_out, *weights_a1))
+    weights_b1 = (own_b, other_b, cross_send(after(other_b, normed)))
+    blocks1 = gather_rows(normed)
+    g0, g1, g2, g3 = gather_rows(after(grad_out, blocks1[2]))
+    *saved1, keep0, give0, keep1, give1 = attend_call(
+        1, meta, blocks1, shared, near_varied, *weights_a1
+    )
+    keep0, give0, keep1, give1 = after((keep0, give0, keep1, give1), g2)
+    sums = reduce_rows(keep0, give0, keep1, give1)
+    middle1, normed1 = plain_call(
+        functools.partial(rows_middle_kernel, 1), None, (between, *sums, shared), (),
+        [sheet, thin], [], 1e7, "rows_middle",
+    )
+    n0, n1, n2 = normed1, other_core(normed1), x_swap(normed1)
+    units = functools.partial(units_turn_kernel, 1)
+    keep0, give0, out_keep0, out_give0 = plain_call(
+        units, meta, (n0, n1, g0, g1, near_varied), weights_b1, [thin] * 4, quarter_scratch,
+        4.4e9, "units_turn_near",
+    )
+    n3 = other_core(after(n2, keep0))
+    keep1, give1, out_keep1, out_give1 = plain_call(
+        units, meta, (n2, n3, g2, g3, near_varied), weights_b1, [thin] * 4, quarter_scratch,
+        4.4e9, "units_turn_far",
+    )
+    sums = reduce_rows(keep0, give0, keep1, give1)
+    grad_middle1, sent = plain_call(
+        functools.partial(rows_turn_kernel, 1), None, (middle1, grad_out, *sums, shared), (),
+        [sheet, thin], [], 1e7, "rows_turn",
+    )
+    grads = gather_rows(sent)
+    out_parts = after((out_keep0, out_give0, out_keep1, out_give1), grads[2])
+    out_sums = reduce_rows(*out_parts)
+    keep0, give0, keep1, give1, down1, up1 = attend_back_call(
+        1, meta, blocks1, grads, saved1, shared, near_varied, *weights_a1
+    )
+    keep0, give0, keep1, give1 = after((keep0, give0, keep1, give1), out_sums)
+    sums = reduce_rows(keep0, give0, keep1, give1)
+    total1 = total_over_z(*after((down1, up1), sums[1]))
+    sums, total1 = lax.optimization_barrier((sums, total1))
+    grad_between = plain_call(
+        rows_before_kernel, None, (grad_middle1, *sums, between, shared), (), [thin], [], 1e7,
+        "rows_before",
+    )[0]
+    g0, g1, g2 = grad_between, other_core(grad_between), x_swap(grad_between)
+    out_wide, narrow = plain_call(
+        rows_output_kernel, None, (middle1, *after(out_sums, g1), shared), (),
+        [sheet, thin], [], 1e7, "rows_output",
+    )
+    out_same, out_cross = collect(1, out_wide, narrow)
+    units = functools.partial(units_back_kernel, 0)
+    keep0, give0 = plain_call(
+        units, meta, (g0, g1, *slopes_near), weights_b0, [thin] * 2, quarter_scratch,
+        2.2e9, "units_back_near",
+    )
+    g3 = other_core(after(g2, keep0))
+    keep1, give1 = plain_call(
+        units, meta, (g2, g3, *slopes_far), weights_b0, [thin] * 2, quarter_scratch,
+        2.2e9, "units_back_far",
+    )
+    sums = reduce_rows(keep0, give0, keep1, give1)
+    total1 = total_over_cores(after(total1, sums[1]))
+    sums, total1 = lax.optimization_barrier((sums, total1))
+    grad_middle0, sent = plain_call(
+        functools.partial(rows_turn_kernel, 0), None, (middle0, grad_between, *sums, shared), (),
+        [sheet, thin], [], 1e7, "rows_turn",
+    )
+    grads = after(gather_rows(sent), out_same, out_cross)
+    total1 = total_over_x(1, after(total1, grads))
+    keep0, give0, keep1, give1, down0, up0 = attend_back_call(
+        0, meta, blocks0, grads, saved0, shared, near_varied, *weights_a0
+    )
+    keep0, give0, keep1, give1 = after((keep0, give0, keep1, give1), total1)
+    sums = reduce_rows(keep0, give0, keep1, give1)
+    wide, narrow = plain_call(
+        rows_final_kernel, None, (grad_middle0, *sums, rows, shared), (), [sheet, thin], [], 1e7,
+        "rows_final",
+    )
+    in_same, in_cross = collect(0, wide, narrow)
+    total0 = total_over_z(*after((down0, up0), sums[1]))
+    total0 = total_over_x(0, total_over_cores(total0))
+    same = jnp.where(
+        first, jnp.where(y == 0, wide, in_same), jnp.where(y == 1, out_wide, out_same)
+    )
+    cross = jnp.where(first, in_cross, out_cross).astype(f32)
+    combined = jnp.where(y == 0, jnp.stack([same, cross]), jnp.stack([cross, same]))
+    grad_down = jnp.where(first, total0[0], total1[0])
+    grad_up = jnp.where(first, total0[1], total1[1])
+    return (
+        combined[None],
+        grad_down.reshape(1, 2, ADAPTER_RANK, 1024).transpose(0, 1, 3, 2),
+        jnp.stack([grad_up[:ADAPTER_RANK, :256], grad_up[ADAPTER_RANK:, 256:]])[None],
+    )
+
+
+def body(*arrays):
+    dp = lax.axis_size("dp")
+    known = (
+        arrays[0].shape == (1, 2, BLOCK, 1024)
+        and lax.axis_size("tensor") == 4
+        and lax.axis_size("section") == 2
+        and arrays[3].shape == (1, 256, 1024)
+        and arrays[5].shape == (1, 1024, 1024)
+        and dp & (dp - 1) == 0
+    )
+    return relay_body(*arrays) if known else plain_body(*arrays)
+
+
 def solution(mesh):
     placed = (
         P("section", None, ("dp", "tensor"), None),

time: 1700 us -> 406 us (0.24)
  waiting for transfers between devices: 1060 us -> 161 us
  matrix products: 339 us -> 0 us
  other arithmetic: 139 us -> 14.9 us
  Pallas kernels: 0 us -> 111 us
  blocking collectives: 86.2 us -> 0 us
  starting transfers between devices: 20.4 us -> 99.1 us
    reduce_scatter x15 -> x0, waiting for transfers between devices: 534 us -> none  [the longest x6 288 us: forward_relay(): lax.psum_scatter(jnp.dot(mixed, projection_weight[0], preferred_element_t...]
    all_gather x18 -> x0, waiting for transfers between devices: 521 us -> none  [the longest x6 174 us: forward_relay(): gathered = lax.all_gather(normalized_rows, 'tensor', axis=0, tiled=True)]
    dot_general x84 -> x0, matrix products: 306 us -> none  [the longest x27 59 us: contract_axes(): lax.dot_general(left, right, (((left_dim,), (right_dim,)), ((), ())), pre...]
    ppermute x4 -> x77, waiting for transfers between devices: 8.18 us -> 161 us  [the longest x73 151 us: send(): return lax.ppermute(block, ('section', 'tensor'), pairs)]
    pallas_call x0 -> x19, Pallas kernels: none -> 111 us  [the longest x15 45.6 us: plain_call(): pl.pallas_call(kernel, in_specs=specs, out_specs=[VMEM_SPACE] * len(outs)...]
    ppermute x4 -> x77, starting transfers between devices: 6.86 us -> 99.1 us  [the longest x73 90.3 us: send(): return lax.ppermute(block, ('section', 'tensor'), pairs)]
    psum x2 -> x0, blocking collectives: 86.2 us -> none  [reduce_adapters(): return (lax.psum(part_a, ('dp', 'tensor')), lax.psum(second_portion, 'dp'))]
    reduce_sum x39 -> x0, other arithmetic: 61.6 us -> none  [the longest x3 24.5 us: attend(): total = jnp.sum(weights, axis=-1, keepdims=True)]
  transfers between devices with their start and end apart: 37 -> 77, of which waited for: 34 -> 41; matrix products, arithmetic and copies ran while one was open for 10% -> 3% of each run, Pallas kernels for 0% -> 24%
where the time goes in v2:
time: 406 us; the launch traced here: 399 us
  waiting for transfers between devices  161 us (40%)
  Pallas kernels  111 us (27%)
  starting transfers between devices  99.1 us (24%)
  other arithmetic  14.9 us (4%)
  local copies, waits for them, and re-layouts  11.6 us (3%)
    ppermute x73, waiting for transfers between devices, send(): return lax.ppermute(block, ('section', 'tensor'), pairs)  151 us
    ppermute x73, starting transfers between devices, send(): return lax.ppermute(block, ('section', 'tensor'), pairs)  90.3 us
    pallas_call x15, Pallas kernels, plain_call(): pl.pallas_call(kernel, in_specs=specs, out_specs=[VMEM_SPACE] * len(outs)...  45.6 us
    pallas_call x2, Pallas kernels, attend_back_call(): pl.pallas_call(functools.partial(attend_back_kernel, layer), in_specs=[SM...  38.4 us
    pallas_call x2, Pallas kernels, attend_call(): pl.pallas_call(functools.partial(attend_kernel, layer), in_specs=[SMEM_SP...  26.7 us
    ppermute x4, waiting for transfers between devices, total_over_z(): both = both + lax.ppermute(both, 'dp', [(i, i ^ step) for i in range(size)])  9.56 us
    ppermute x4, starting transfers between devices, total_over_z(): both = both + lax.ppermute(both, 'dp', [(i, i ^ step) for i in range(size)])  8.78 us
    unnamed x76, local copies, waits for them, and re-layouts  8.78 us
  transfers between devices with their start and end apart: 77, of which 41 were waited for; matrix products, arithmetic and copies ran while one was open for 3% of the time, Pallas kernels for 24%

profile of v2, /device:TPU:0, one launch (start us, length us, event | category | flops | bytes accessed | tf_op | source)
XLA Modules:
  0.0 399.0 jit_solution(201761222452743026)
XLA Ops:
  21.1 6.6 %collective-permute-done.1 = bf16[256,1024]{1,0:T(8,128)(2,1)S(1)} collective-permute-done((bf16[256,1024]{1,0:T(8,128)(2,1)}, bf16[256,1024]{1,0:T(8,128)(2,1)S(1)}, u32[]{:S(2)}, u32[]{:S(2)}) %collective-permute-start.1) | collective-permute-done | bytes 524320 | tf_op jit(solution)/shard_map/ppermute | solution.py:345
  41.9 7.7 %collective-permute-start.15 = (bf16[2048,1024]{1,0:T(8,128)(2,1)}, bf16[2048,1024]{1,0:T(8,128)(2,1)}, u32[]{:S(2)}, u32[]{:S(2)}) collective-permute-start(bf16[2048,1024]{1,0:T(8,128)(2,1)} %pad_maximum_fusion.rest_0_), channel_id=1, source_target_pairs={{0,2},{1,3},{2,16},{3,17},{4,6},{5,7},{6,20},{7,21},{8,10},{9,11},... | collective-permute-start | bytes 12582920 | tf_op jit(solution)/shard_map/ppermute | solution.py:345
  52.3 6.7 %collective-permute-done.3.n1 = bf16[256,1024]{1,0:T(8,128)(2,1)} collective-permute-done((bf16[256,1024]{1,0:T(8,128)(2,1)S(1)}, bf16[256,1024]{1,0:T(8,128)(2,1)}, u32[]{:S(2)}, u32[]{:S(2)}) %collective-permute-start.3) | collective-permute-done | bytes 524320 | tf_op jit(solution)/shard_map/ppermute | solution.py:345
  60.4 12.8 %attention_forward.2 = (bf16[1024,256]{1,0:T(8,128)(2,1)S(1)}, bf16[1024,256]{1,0:T(8,128)(2,1)S(1)}, bf16[1024,256]{1,0:T(8,128)(2,1)S(1)}, f32[8,1024]{1,0:T(8...) custom-call(s32[8]{0:T(128)S(1)} %concatenate.41.meta, ...), custom_call_target="tpu_custom_call" | custom-call | flops 1000 | bytes 1000 | tf_op jit(solution)/shard_map/attention_forward/pallas_call | solution.py:535
  78.8 12.4 %collective-permute-done.12.far = bf16[256,1024]{1,0:T(8,128)(2,1)S(1)} collective-permute-done((bf16[256,1024]{1,0:T(8,128)(2,1)S(1)}, bf16[256,1024]{1,0:T(8,128)(2,1)S(1)}, u32[]{:S(2)}, u32[]{:S(2)}) %collective-permute-start.12) | collective-permute-done | bytes 524320 | tf_op jit(solution)/shard_map/ppermute | solution.py:345
  94.6 5.8 %collective-permute-start.23 = (bf16[4,1024,256]{2,1,0:T(8,128)(2,1)}, bf16[4,1024,256]{2,1,0:T(8,128)(2,1)}, u32[]{:S(2)}, u32[]{:S(2)}) collective-permute-start(bf16[4,1024,256]{2,1,0:T(8,128)(2,1)} %collective-permute-done.7.w_other), channel_id=1, source_target_pairs={{0,2},{1,3},{2,16},{3,17},{4,6},{5,7},{6,20},{7,21},{8,10},{9,11},... | collective-permute-start | bytes 6291464 | tf_op jit(solution)/shard_map/ppermute | solution.py:345
  100.5 6.7 %units_near.1 = (bf16[256,1024]{1,0:T(8,128)(2,1)S(1)}, bf16[256,1024]{1,0:T(8,128)(2,1)}, bf16[256,1024]{1,0:T(8,128)(2,1)S(1)}, bf16[256,1024]{1,0:T(8,128)(2,1)S(1)}) custom-call(s32[8]{0:T(128)S(1)} %concatenate.41.meta, bf16[256,1024]{1,0:T(8,128)(2,1)S(1)} %get-tuple-element.139.n0, bf16[256,1024]{1,0:T(8,128)(2,1)S(1)} %collective-permute-done.13.n1, ...), custom_call_target="tpu_custom_call" | custom-call | flops 1000 | bytes 1000 | tf_op jit(solution)/shard_map/units_near/pallas_call | solution.py:778
  111.4 5.9 %units_far.1 = (bf16[256,1024]{1,0:T(8,128)(2,1)S(1)}, bf16[256,1024]{1,0:T(8,128)(2,1)S(1)}, bf16[256,1024]{1,0:T(8,128)(2,1)S(1)}, bf16[256,1024]{1,0:T(8,128)(2,1)S(1)}) custom-call(s32[8]{0:T(128)S(1)} %concatenate.41.meta, bf16[256,1024]{1,0:T(8,128)(2,1)S(1)} %collective-permute-done.17.n0, bf16[256,1024]{1,0:T(8,128)(2,1)S(1)} %collective-permute-done.18.n1, ...), custom_call_target="tpu_custom_call" | custom-call | flops 1000 | bytes 1000 | tf_op jit(solution)/shard_map/units_far/pallas_call | solution.py:778
  129.2 11.1 %collective-permute-done.20.far = bf16[256,1024]{1,0:T(8,128)(2,1)} collective-permute-done((bf16[256,1024]{1,0:T(8,128)(2,1)}, bf16[256,1024]{1,0:T(8,128)(2,1)}, u32[]{:S(2)}, u32[]{:S(2)}) %collective-permute-start.20) | collective-permute-done | bytes 524320 | tf_op jit(solution)/shard_map/ppermute | solution.py:345
  142.1 6.3 %collective-permute-start.33 = (bf16[2048,1024]{1,0:T(8,128)(2,1)}, bf16[2048,1024]{1,0:T(8,128)(2,1)}, u32[]{:S(2)}, u32[]{:S(2)}) collective-permute-start(bf16[2048,1024]{1,0:T(8,128)(2,1)} %collective-permute-done.14.rest_1_), channel_id=1, source_target_pairs={{0,2},{1,3},{2,16},{3,17},{4,6},{5,7},{6,20},{7,21},{8,10},{9,11},... | collective-permute-start | bytes 12582920 | tf_op jit(solution)/shard_map/ppermute | solution.py:345
  150.1 7.5 %collective-permute-done.25.n2 = bf16[256,1024]{1,0:T(8,128)(2,1)S(1)} collective-permute-done((bf16[256,1024]{1,0:T(8,128)(2,1)S(1)}, bf16[256,1024]{1,0:T(8,128)(2,1)S(1)}, u32[]{:S(2)}, u32[]{:S(2)}) %collective-permute-start.25) | collective-permute-done | bytes 524320 | tf_op jit(solution)/shard_map/ppermute | solution.py:345
  159.6 13.8 %attention_forward.3 = (bf16[1024,256]{1,0:T(8,128)(2,1)S(1)}, bf16[1024,256]{1,0:T(8,128)(2,1)S(1)}, bf16[1024,256]{1,0:T(8,128)(2,1)S(1)}, f32[8,1024]{1,0:T(8...) custom-call(s32[8]{0:T(128)S(1)} %concatenate.41.meta, ...), custom_call_target="tpu_custom_call" | custom-call | flops 1000 | bytes 1000 | tf_op jit(solution)/shard_map/attention_forward/pallas_call | solution.py:535
  178.9 12.3 %collective-permute-done.30.far = bf16[256,1024]{1,0:T(8,128)(2,1)S(1)} collective-permute-done((bf16[256,1024]{1,0:T(8,128)(2,1)S(1)}, bf16[256,1024]{1,0:T(8,128)(2,1)S(1)}, u32[]{:S(2)}, u32[]{:S(2)}) %collective-permute-start.30) | collective-permute-done | bytes 524320 | tf_op jit(solution)/shard_map/ppermute | solution.py:345
  193.8 7.6 %units_turn_near.1 = (bf16[256,1024]{1,0:T(8,128)(2,1)S(1)}, bf16[256,1024]{1,0:T(8,128)(2,1)S(1)}, bf16[256,1024]{1,0:T(8,128)(2,1)S(1)}, bf16[256,1024]{1,0:T(8,128)(2,1)S(1)}) custom-call(s32[8]{0:T(128)S(1)} %concatenate.41.meta, bf16[256,1024]{1,0:T(8,128)(2,1)S(1)} %get-tuple-element.166.n0, bf16[256,1024]{1,0:T(8,128)(2,1)S(1)} %collective-permute-done.31.n1, ...), custom_call_target="tpu_custom_call" | custom-call | flops 1000 | bytes 1000 | tf_op jit(solution)/shard_map/units_turn_near/pallas_call | solution.py:778
  208.1 7.6 %units_turn_far.1 = (bf16[256,1024]{1,0:T(8,128)(2,1)S(1)}, bf16[256,1024]{1,0:T(8,128)(2,1)S(1)}, bf16[256,1024]{1,0:T(8,128)(2,1)S(1)}, bf16[256,1024]{1,0:T(8,128)(2,1)S(1)}) custom-call(s32[8]{0:T(128)S(1)} %concatenate.41.meta, bf16[256,1024]{1,0:T(8,128)(2,1)S(1)} %collective-permute-done.35.n0, bf16[256,1024]{1,0:T(8,128)(2,1)S(1)} %collective-permute-done.36.n1, ...), custom_call_target="tpu_custom_call" | custom-call | flops 1000 | bytes 1000 | tf_op jit(solution)/shard_map/units_turn_far/pallas_call | solution.py:778
  219.6 12.3 %collective-permute-done.39.far = bf16[256,1024]{1,0:T(8,128)(2,1)S(1)} collective-permute-done((bf16[256,1024]{1,0:T(8,128)(2,1)S(1)}, bf16[256,1024]{1,0:T(8,128)(2,1)S(1)}, u32[]{:S(2)}, u32[]{:S(2)}) %collective-permute-start.39) | collective-permute-done | bytes 524320 | tf_op jit(solution)/shard_map/ppermute | solution.py:345
  234.5 11.5 %collective-permute-done.41.g2 = bf16[256,1024]{1,0:T(8,128)(2,1)S(1)} collective-permute-done((bf16[256,1024]{1,0:T(8,128)(2,1)S(1)}, bf16[256,1024]{1,0:T(8,128)(2,1)S(1)}, u32[]{:S(2)}, u32[]{:S(2)}) %collective-permute-start.41) | collective-permute-done | bytes 524320 | tf_op jit(solution)/shard_map/ppermute | solution.py:345
  250.9 19.0 %attention_backward.2 = (bf16[256,1024]{1,0:T(8,128)(2,1)S(1)}, bf16[256,1024]{1,0:T(8,128)(2,1)S(1)}, bf16[256,1024]{1,0:T(8,128)(2,1)S(1)}, bf16[256,1024]{1,0...) custom-call(s32[8]{0:T(128)S(1)} %concatenate.41.meta, bf16[256,1024]{1,0:T(8,128)(2,1)S(1)} %get-tuple-element.151.n0, ...), custom_call_target="tpu_custom_call" | custom-call | flops 1000 | bytes 1000 | tf_op jit(solution)/shard_map/attention_backward/pallas_call | solution.py:638
  289.0 5.4 %units_back_near.1 = (bf16[256,1024]{1,0:T(8,128)(2,1)S(1)}, bf16[256,1024]{1,0:T(8,128)(2,1)S(1)}) custom-call(s32[8]{0:T(128)S(1)} %concatenate.41.meta, bf16[256,1024]{1,0:T(8,128)(2,1)S(1)} %rows_before.1.g0.g_ref, bf16[256,1024]{1,0:T(8,128)(2,1)S(1)} %collective-permute-done.51.g1, bf16[256,1024]{1,0:T(8,128)(2,1)S(1)} %copy-done.12, ...), custom_call_target="tpu_custom_call" | custom-call | flops 1000 | bytes 1000 | tf_op jit(solution)/shard_map/units_back_near/pallas_call | solution.py:778
  294.4 7.0 %collective-permute-done.53.g0 = bf16[256,1024]{1,0:T(8,128)(2,1)S(1)} collective-permute-done((bf16[256,1024]{1,0:T(8,128)(2,1)S(1)}, bf16[256,1024]{1,0:T(8,128)(2,1)S(1)}, u32[]{:S(2)}, u32[]{:S(2)}) %collective-permute-start.53) | collective-permute-done | bytes 524320 | tf_op jit(solution)/shard_map/ppermute | solution.py:345
  303.3 5.4 %units_back_far.1 = (bf16[256,1024]{1,0:T(8,128)(2,1)S(1)}, bf16[256,1024]{1,0:T(8,128)(2,1)S(1)}) custom-call(s32[8]{0:T(128)S(1)} %concatenate.41.meta, bf16[256,1024]{1,0:T(8,128)(2,1)S(1)} %collective-permute-done.53.g0, bf16[256,1024]{1,0:T(8,128)(2,1)S(1)} %collective-permute-done.54.g1, bf16[256,1024]{1,0:T(8,128)(2,1)S(1)} %copy-done.8, ...), custom_call_target="tpu_custom_call" | custom-call | flops 1000 | bytes 1000 | tf_op jit(solution)/shard_map/units_back_far/pallas_call | solution.py:778
  330.8 8.2 %collective-permute-done.60.g2 = bf16[256,1024]{1,0:T(8,128)(2,1)S(1)} collective-permute-done((bf16[256,1024]{1,0:T(8,128)(2,1)S(1)}, bf16[256,1024]{1,0:T(8,128)(2,1)S(1)}, u32[]{:S(2)}, u32[]{:S(2)}) %collective-permute-start.60) | collective-permute-done | bytes 524320 | tf_op jit(solution)/shard_map/ppermute | solution.py:345
  344.9 19.5 %attention_backward.3 = (bf16[256,1024]{1,0:T(8,128)(2,1)S(1)}, bf16[256,1024]{1,0:T(8,128)(2,1)S(1)}, bf16[256,1024]{1,0:T(8,128)(2,1)S(1)}, bf16[256,1024]{1,0...) custom-call(s32[8]{0:T(128)S(1)} %concatenate.41.meta, bf16[256,1024]{1,0:T(8,128)(2,1)S(1)} %rows_first.1.n0, ...), custom_call_target="tpu_custom_call" | custom-call | flops 1000 | bytes 1000 | tf_op jit(solution)/shard_map/attention_backward/pallas_call | solution.py:638
  390.4 6.3 %collective-permute-done.70 = bf16[256,1024]{1,0:T(8,128)(2,1)S(1)} collective-permute-done((bf16[256,1024]{1,0:T(8,128)(2,1)S(1)}, bf16[256,1024]{1,0:T(8,128)(2,1)S(1)}, u32[]{:S(2)}, u32[]{:S(2)}) %collective-permute-start.70) | collective-permute-done | bytes 524320 | tf_op jit(solution)/shard_map/ppermute | solution.py:345
  (280 shorter events, 171.8 us)
Async XLA Ops:
  8.1 33.8 %collective-permute-start.8 = (bf16[4,1024,256]{2,1,0:T(8,128)(2,1)}, bf16[4,1024,256]{2,1,0:T(8,128)(2,1)}, u32[]{:S(2)}, u32[]{:S(2)}) collective-permute-start(bf16[4,1024,256]{2,1,0:T(8,128)(2,1)} %collective-permute-done.7.w_other), channel_id=1, source_target_pairs={{16,2},{17,3},{18,16},{19,17},{20,6},{21,7},{22,20},{23,21},{24,10... | collective-permute-start | bytes 6291464 | tf_op jit(solution)/shard_map/ppermute | solution.py:345
  11.0 16.8 %collective-permute-start.1 = (bf16[256,1024]{1,0:T(8,128)(2,1)}, bf16[256,1024]{1,0:T(8,128)(2,1)S(1)}, u32[]{:S(2)}, u32[]{:S(2)}) collective-permute-start(bf16[256,1024]{1,0:T(8,128)(2,1)} %get-tuple-element.253), channel_id=1, source_target_pairs={{0,2},{1,3},{2,18},{3,19},{4,6},{5,7},{6,22},{7,23},{8,10},{9,11},... | collective-permute-start | bytes 1572872 | tf_op jit(solution)/shard_map/ppermute | solution.py:345
  18.8 15.1 %collective-permute-start.6 = (f32[2,16,1024]{2,1,0:T(8,128)}, f32[2,16,1024]{2,1,0:T(8,128)}, u32[]{:S(2)}, u32[]{:S(2)}) collective-permute-start(f32[2,16,1024]{2,1,0:T(8,128)} %maximum_select_fusion.2), channel_id=1, source_target_pairs={{0,2},{1,3},{2,0},{3,1},{16,18},{17,19},{18,16},{19,17},{4,6},{5,7... | collective-permute-start | bytes 393224 | tf_op jit(solution)/shard_map/ppermute | solution.py:345
  41.9 58.5 %collective-permute-start.15 = (bf16[2048,1024]{1,0:T(8,128)(2,1)}, bf16[2048,1024]{1,0:T(8,128)(2,1)}, u32[]{:S(2)}, u32[]{:S(2)}) collective-permute-start(bf16[2048,1024]{1,0:T(8,128)(2,1)} %pad_maximum_fusion.rest_0_), channel_id=1, source_target_pairs={{0,2},{1,3},{2,16},{3,17},{4,6},{5,7},{6,20},{7,21},{8,10},{9,11},... | collective-permute-start | bytes 12582920 | tf_op jit(solution)/shard_map/ppermute | solution.py:345
  49.7 50.8 %collective-permute-start.14 = (bf16[2048,1024]{1,0:T(8,128)(2,1)}, bf16[2048,1024]{1,0:T(8,128)(2,1)}, u32[]{:S(2)}, u32[]{:S(2)}) collective-permute-start(bf16[2048,1024]{1,0:T(8,128)(2,1)} %pad_maximum_fusion.rest_0_), channel_id=1, source_target_pairs={{0,16},{1,17},{2,18},{3,19},{16,0},{17,1},{18,2},{19,3},{4,20},{5,... | collective-permute-start | bytes 12582920 | tf_op jit(solution)/shard_map/ppermute | solution.py:345
  76.8 14.4 %collective-permute-start.12 = (bf16[256,1024]{1,0:T(8,128)(2,1)S(1)}, bf16[256,1024]{1,0:T(8,128)(2,1)S(1)}, u32[]{:S(2)}, u32[]{:S(2)}) collective-permute-start(bf16[256,1024]{1,0:T(8,128)(2,1)S(1)} %add_convert_fusion.7), channel_id=1, source_target_pairs={{0,1},{1,0},{2,3},{3,2},{16,17},{17,16},{18,19},{19,18},{4,5},{5,4... | collective-permute-start | bytes 1572872 | tf_op jit(solution)/shard_map/ppermute | solution.py:345
  92.9 16.6 %collective-permute-start.17 = (bf16[256,1024]{1,0:T(8,128)(2,1)S(1)}, bf16[256,1024]{1,0:T(8,128)(2,1)S(1)}, u32[]{:S(2)}, u32[]{:S(2)}) collective-permute-start(bf16[256,1024]{1,0:T(8,128)(2,1)S(1)} %get-tuple-element.139.n0), channel_id=1, source_target_pairs={{0,1},{1,0},{2,3},{3,2},{16,17},{17,16},{18,19},{19,18},{4,5},{5,4... | collective-permute-start | bytes 1572872 | tf_op jit(solution)/shard_map/ppermute | solution.py:345
  94.6 47.5 %collective-permute-start.23 = (bf16[4,1024,256]{2,1,0:T(8,128)(2,1)}, bf16[4,1024,256]{2,1,0:T(8,128)(2,1)}, u32[]{:S(2)}, u32[]{:S(2)}) collective-permute-start(bf16[4,1024,256]{2,1,0:T(8,128)(2,1)} %collective-permute-done.7.w_other), channel_id=1, source_target_pairs={{0,2},{1,3},{2,16},{3,17},{4,6},{5,7},{6,20},{7,21},{8,10},{9,11},... | collective-permute-start | bytes 6291464 | tf_op jit(solution)/shard_map/ppermute | solution.py:345
  126.1 14.2 %collective-permute-start.20 = (bf16[256,1024]{1,0:T(8,128)(2,1)}, bf16[256,1024]{1,0:T(8,128)(2,1)}, u32[]{:S(2)}, u32[]{:S(2)}) collective-permute-start(bf16[256,1024]{1,0:T(8,128)(2,1)} %add_convert_fusion.6), channel_id=1, source_target_pairs={{0,1},{1,0},{2,3},{3,2},{16,17},{17,16},{18,19},{19,18},{4,5},{5,4... | collective-permute-start | bytes 1572872 | tf_op jit(solution)/shard_map/ppermute | solution.py:345
  142.1 51.6 %collective-permute-start.33 = (bf16[2048,1024]{1,0:T(8,128)(2,1)}, bf16[2048,1024]{1,0:T(8,128)(2,1)}, u32[]{:S(2)}, u32[]{:S(2)}) collective-permute-start(bf16[2048,1024]{1,0:T(8,128)(2,1)} %collective-permute-done.14.rest_1_), channel_id=1, source_target_pairs={{0,2},{1,3},{2,16},{3,17},{4,6},{5,7},{6,20},{7,21},{8,10},{9,11},... | collective-permute-start | bytes 12582920 | tf_op jit(solution)/shard_map/ppermute | solution.py:345
  157.7 17.4 %collective-permute-start.27 = (bf16[256,1024]{1,0:T(8,128)(2,1)S(1)}, bf16[256,1024]{1,0:T(8,128)(2,1)S(1)}, u32[]{:S(2)}, u32[]{:S(2)}) collective-permute-start(bf16[256,1024]{1,0:T(8,128)(2,1)S(1)} %select_select_fusion.g0.g_ref), channel_id=1, source_target_pairs={{0,1},{1,0},{2,3},{3,2},{16,17},{17,16},{18,19},{19,18},{4,5},{5,4... | collective-permute-start | bytes 1572872 | tf_op jit(solution)/shard_map/ppermute | solution.py:345
  177.2 14.0 %collective-permute-start.30 = (bf16[256,1024]{1,0:T(8,128)(2,1)S(1)}, bf16[256,1024]{1,0:T(8,128)(2,1)S(1)}, u32[]{:S(2)}, u32[]{:S(2)}) collective-permute-start(bf16[256,1024]{1,0:T(8,128)(2,1)S(1)} %add_convert_fusion.5), channel_id=1, source_target_pairs={{0,1},{1,0},{2,3},{3,2},{16,17},{17,16},{18,19},{19,18},{4,5},{5,4... | collective-permute-start | bytes 1572872 | tf_op jit(solution)/shard_map/ppermute | solution.py:345
  178.9 14.9 %collective-permute-start.32 = (bf16[256,1024]{1,0:T(8,128)(2,1)S(1)}, bf16[256,1024]{1,0:T(8,128)(2,1)S(1)}, u32[]{:S(2)}, u32[]{:S(2)}) collective-permute-start(bf16[256,1024]{1,0:T(8,128)(2,1)S(1)} %select_select_fusion.g0.g_ref), channel_id=1, source_target_pairs={{0,16},{1,17},{2,18},{3,19},{16,0},{17,1},{18,2},{19,3},{4,20},{5,... | collective-permute-start | bytes 1572872 | tf_op jit(solution)/shard_map/ppermute | solution.py:345
  191.9 14.3 %collective-permute-start.35 = (bf16[256,1024]{1,0:T(8,128)(2,1)S(1)}, bf16[256,1024]{1,0:T(8,128)(2,1)S(1)}, u32[]{:S(2)}, u32[]{:S(2)}) collective-permute-start(bf16[256,1024]{1,0:T(8,128)(2,1)S(1)} %get-tuple-element.166.n0), channel_id=1, source_target_pairs={{0,1},{1,0},{2,3},{3,2},{16,17},{17,16},{18,19},{19,18},{4,5},{5,4... | collective-permute-start | bytes 1572872 | tf_op jit(solution)/shard_map/ppermute | solution.py:345
  217.9 14.0 %collective-permute-start.39 = (bf16[256,1024]{1,0:T(8,128)(2,1)S(1)}, bf16[256,1024]{1,0:T(8,128)(2,1)S(1)}, u32[]{:S(2)}, u32[]{:S(2)}) collective-permute-start(bf16[256,1024]{1,0:T(8,128)(2,1)S(1)} %add_convert_fusion.4), channel_id=1, source_target_pairs={{0,1},{1,0},{2,3},{3,2},{16,17},{17,16},{18,19},{19,18},{4,5},{5,4... | collective-permute-start | bytes 1572872 | tf_op jit(solution)/shard_map/ppermute | solution.py:345
  246.6 23.3 %collective-permute-start.43 = (bf16[256,1024]{1,0:T(8,128)(2,1)S(1)}, bf16[256,1024]{1,0:T(8,128)(2,1)S(1)}, u32[]{:S(2)}, u32[]{:S(2)}) collective-permute-start(bf16[256,1024]{1,0:T(8,128)(2,1)S(1)} %get-tuple-element.189), channel_id=1, source_target_pairs={{0,16},{1,17},{2,18},{3,19},{16,0},{17,1},{18,2},{19,3},{4,20},{5,... | collective-permute-start | bytes 1572872 | tf_op jit(solution)/shard_map/ppermute | solution.py:345
  248.0 21.9 %collective-permute-start.45 = (bf16[256,1024]{1,0:T(8,128)(2,1)S(1)}, bf16[256,1024]{1,0:T(8,128)(2,1)S(1)}, u32[]{:S(2)}, u32[]{:S(2)}) collective-permute-start(bf16[256,1024]{1,0:T(8,128)(2,1)S(1)} %add_convert_fusion.3), channel_id=1, source_target_pairs={{0,1},{1,0},{2,3},{3,2},{16,17},{17,16},{18,19},{19,18},{4,5},{5,4... | collective-permute-start | bytes 1572872 | tf_op jit(solution)/shard_map/ppermute | solution.py:345
  272.1 14.0 %collective-permute-start.48 = (bf16[256,1024]{1,0:T(8,128)(2,1)S(1)}, bf16[256,1024]{1,0:T(8,128)(2,1)S(1)}, u32[]{:S(2)}, u32[]{:S(2)}) collective-permute-start(bf16[256,1024]{1,0:T(8,128)(2,1)S(1)} %add_convert_fusion.2), channel_id=1, source_target_pairs={{0,1},{1,0},{2,3},{3,2},{16,17},{17,16},{18,19},{19,18},{4,5},{5,4... | collective-permute-start | bytes 1572872 | tf_op jit(solution)/shard_map/ppermute | solution.py:345
  287.1 14.3 %collective-permute-start.53 = (bf16[256,1024]{1,0:T(8,128)(2,1)S(1)}, bf16[256,1024]{1,0:T(8,128)(2,1)S(1)}, u32[]{:S(2)}, u32[]{:S(2)}) collective-permute-start(bf16[256,1024]{1,0:T(8,128)(2,1)S(1)} %rows_before.1.g0.g_ref), channel_id=1, source_target_pairs={{0,1},{1,0},{2,3},{3,2},{16,17},{17,16},{18,19},{19,18},{4,5},{5,4... | collective-permute-start | bytes 1572872 | tf_op jit(solution)/shard_map/ppermute | solution.py:345
  310.9 14.0 %collective-permute-start.56 = (bf16[256,1024]{1,0:T(8,128)(2,1)S(1)}, bf16[256,1024]{1,0:T(8,128)(2,1)S(1)}, u32[]{:S(2)}, u32[]{:S(2)}) collective-permute-start(bf16[256,1024]{1,0:T(8,128)(2,1)S(1)} %add_convert_fusion.1), channel_id=1, source_target_pairs={{0,1},{1,0},{2,3},{3,2},{16,17},{17,16},{18,19},{19,18},{4,5},{5,4... | collective-permute-start | bytes 1572872 | tf_op jit(solution)/shard_map/ppermute | solution.py:345
  317.7 21.3 %collective-permute-start.62 = (f32[256,1024]{1,0:T(8,128)S(1)}, f32[256,1024]{1,0:T(8,128)S(1)}, u32[]{:S(2)}, u32[]{:S(2)}) collective-permute-start(f32[256,1024]{1,0:T(8,128)S(1)} %get-tuple-element.222), channel_id=1, source_target_pairs={{0,16},{1,17},{4,20},{5,21},{8,24},{9,25},{12,28},{13,29}} | collective-permute-start | bytes 3145736 | tf_op jit(solution)/shard_map/ppermute | solution.py:345
  340.9 23.4 %collective-permute-start.65 = (f32[8,512]{1,0:T(8,128)S(1)}, f32[8,512]{1,0:T(8,128)S(1)}, u32[]{:S(2)}, u32[]{:S(2)}) collective-permute-start(f32[8,512]{1,0:T(8,128)S(1)} %slice.53), channel_id=1, source_target_pairs={{0,16},{1,17},{4,20},{5,21},{8,24},{9,25},{12,28},{13,29}} | collective-permute-start | bytes 49160 | tf_op jit(solution)/shard_map/ppermute | solution.py:345
  343.1 21.2 %collective-permute-start.64 = (f32[8,1024]{1,0:T(8,128)S(1)}, f32[8,1024]{1,0:T(8,128)S(1)}, u32[]{:S(2)}, u32[]{:S(2)}) collective-permute-start(f32[8,1024]{1,0:T(8,128)S(1)} %slice_add_fusion.1), channel_id=1, source_target_pairs={{0,1},{1,0},{2,3},{3,2},{16,17},{17,16},{18,19},{19,18},{4,5},{5,4... | collective-permute-start | bytes 98312 | tf_op jit(solution)/shard_map/ppermute | solution.py:345
  367.3 14.6 %collective-permute-start.68 = (bf16[256,1024]{1,0:T(8,128)(2,1)S(1)}, bf16[256,1024]{1,0:T(8,128)(2,1)S(1)}, u32[]{:S(2)}, u32[]{:S(2)}) collective-permute-start(bf16[256,1024]{1,0:T(8,128)(2,1)S(1)} %add_convert_fusion), channel_id=1, source_target_pairs={{0,1},{1,0},{2,3},{3,2},{16,17},{17,16},{18,19},{19,18},{4,5},{5,4... | collective-permute-start | bytes 1572872 | tf_op jit(solution)/shard_map/ppermute | solution.py:345
  (89 other events, 848.5 us)

commit v3 on v0

--- a/solution.py
+++ b/solution.py
@@ -1,6 +1,10 @@
+import functools
+
 import jax
 import jax.numpy as jnp
 from jax import lax
+from jax.experimental import pallas as pl
+from jax.experimental.pallas import tpu as pltpu
 from jax.sharding import PartitionSpec as P
 
 HEAD = 64
@@ -95,7 +99,7 @@
     return (lax.psum(part_a, ("dp", "tensor")), lax.psum(second_portion, "dp"))
 
 
-def body(
+def plain_body(
     activations,
     starts,
     attention_weights,
@@ -324,6 +328,827 @@
     return (combined[None], totals_a[None], totals_b[None])
 
 
+LOW = 2 * ADAPTER_RANK
+VMEM_SPACE = pl.BlockSpec(memory_space=pltpu.VMEM)
+SMEM_SPACE = pl.BlockSpec(memory_space=pltpu.SMEM)
+HBM_SPACE = pl.BlockSpec(memory_space=pltpu.HBM)
+BLOCK = 256
+CHUNK = 2 * BLOCK
+
+
+def send(block, route):
+    pairs = []
+    for s in range(2):
+        for t in range(4):
+            to = route(s, t)
+            if to is not None:
+                pairs.append((s * 4 + t, to[0] * 4 + to[1]))
+    return lax.ppermute(block, ("section", "tensor"), pairs)
+
+
+def other_core(block):
+    return send(block, lambda s, t: (1 - s, t))
+
+
+def x_swap(block):
+    return send(block, lambda s, t: (s, t ^ 1))
+
+
+def y_swap(block):
+    return send(block, lambda s, t: (s, t ^ 2))
+
+
+def after(value, *others):
+    return lax.optimization_barrier((value, others))[0]
+
+
+def cross_send(block, source=0):
+    return send(block, lambda s, t: (t >> 1, t ^ 2) if s == source else None)
+
+
+def collect(target, same_chip, cross_chip):
+    return (
+        send(same_chip, lambda s, t: (target, t) if s == t & 1 and s != target else None),
+        send(cross_chip, lambda s, t: (target, t ^ 2) if s == t & 1 else None),
+    )
+
+
+def mm(left, right):
+    return jnp.dot(left, right, preferred_element_type=jnp.float32)
+
+
+def mm_nt(left, right):
+    return contract_axes(left, right, 1, 1)
+
+
+def norm_back(rows, gain, grad):
+    mean = jnp.mean(rows, axis=-1, keepdims=True)
+    centered = rows - mean
+    scale = lax.rsqrt(jnp.mean(centered * centered, axis=-1, keepdims=True) + 1e-05)
+    unit = centered * scale
+    scaled = grad * gain
+    return scale * (
+        scaled
+        - jnp.mean(scaled, axis=-1, keepdims=True)
+        - unit * jnp.mean(scaled * unit, axis=-1, keepdims=True)
+    )
+
+
+def gelu_both(value):
+    square = value * value
+    bent = jnp.tanh(0.7978845608028654 * value * (1.0 + 0.044715 * square))
+    half = 0.5 * (1.0 + bent)
+    slope = half + 0.5 * value * (1.0 - bent * bent) * (
+        0.7978845608028654 * (1.0 + 3.0 * 0.044715 * square)
+    )
+    return value * half, slope
+
+
+def cost(flops, read):
+    return pl.CostEstimate(flops=1000, bytes_accessed=1000, transcendentals=0)
+
+
+def kernel_params(mib):
+    return pltpu.CompilerParams(vmem_limit_bytes=mib * 1024 * 1024)
+
+
+def position_mask(meta, query_block, key_block):
+    shape = (BLOCK, BLOCK)
+    key_pos = key_block * BLOCK + lax.broadcasted_iota(jnp.int32, shape, 0)
+    query_pos = query_block * BLOCK + lax.broadcasted_iota(jnp.int32, (1, BLOCK), 1)
+    low = jnp.zeros((1, BLOCK), jnp.int32)
+    for c in range(4):
+        first = meta[4 + c]
+        low = jnp.where(first <= query_pos, jnp.maximum(low, first), low)
+    valid = key_pos >= low
+    if query_block == key_block:
+        valid = valid & (key_pos <= query_pos)
+    return valid
+
+
+def head_lanes(half):
+    return (lax.broadcasted_iota(jnp.int32, (1, 2 * HEAD), 1) // HEAD) == half
+
+
+def start_pick(choices, target, sem):
+    for condition, source in choices:
+
+        @pl.when(condition)
+        def _(source=source):
+            pltpu.make_async_copy(source, target, sem).start()
+
+
+def load_qkv_weight(layer, meta, pieces, w_buf, sem):
+    own, other, lead, trail = pieces
+    s, y, w = meta[0], meta[2], meta[8]
+    start_pick(
+        (((s == y) & (s == layer), own), ((s == y) & (s != layer), other)), w_buf, sem
+    )
+
+    @pl.when(s != y)
+    def _():
+        for part, side in ((lead, w), (trail, 1 - w)):
+            pltpu.make_async_copy(part, w_buf.at[pl.ds(2 * side, 2)], sem).start()
+
+    return pltpu.make_async_copy(own, w_buf, sem)
+
+
+def half_rows(core):
+    return pl.ds(pl.multiple_of(core * BLOCK, BLOCK), BLOCK)
+
+
+def lay_out(meta, own, near, target):
+    s = meta[0]
+    target[half_rows(s), :] = own[...]
+    target[half_rows(1 - s), :] = near[...]
+
+
+def share_out(meta, source, keep, give):
+    s = meta[0]
+    keep[...] = source[half_rows(s), :]
+    give[...] = source[half_rows(1 - s), :]
+
+
+def attend_kernel(layer, chunk, meta, shared, varied, own, near, *rest):
+    before, rest = rest[: 2 * chunk], rest[2 * chunk :]
+    q_out, k_out, v_out, lse_out, mixed_out, keep, give = rest[4:11]
+    (
+        n_buf, w_buf, score_buf, vt_buf, q_ref, k_ref, v_ref, lse_ref, mixed_ref, sem, out_sems
+    ) = rest[11:]
+    loaded = load_qkv_weight(layer, meta, rest[:4], w_buf, sem)
+    down = shared[layer, 8:16, :].astype(jnp.bfloat16)
+    bias = varied[layer, 1:2, :]
+    up = varied[layer, 8:16, 0:512].astype(jnp.bfloat16)
+    lay_out(meta, own, near, n_buf)
+    keys = [k_ref] if chunk == 0 else [before[0], k_ref]
+    if chunk == 1:
+        for b in range(2):
+            span = slice(b * BLOCK, (b + 1) * BLOCK)
+            vt_buf[:, span] = before[1][span, :].T
+    loaded.wait()
+    normed = n_buf[...]
+    low = mm_nt(normed, down).astype(jnp.bfloat16)
+    lifted = adapter_scale * mm(low, up)
+    q_ref[...] = (mm(normed, w_buf[0]) + bias[:, 0:256] + lifted[:, 0:256]).astype(jnp.bfloat16)
+    k_ref[...] = mm(normed, w_buf[1]).astype(jnp.bfloat16)
+    v_ref[...] = (mm(normed, w_buf[2]) + bias[:, 256:512] + lifted[:, 256:512]).astype(jnp.bfloat16)
+    saved = [
+        pltpu.make_async_copy(source, target, out_sems.at[i])
+        for i, (source, target) in enumerate(
+            (
+                (q_ref, q_out), (k_ref, k_out), (v_ref, v_out), (lse_ref, lse_out),
+                (mixed_ref, mixed_out),
+            )
+        )
+    ]
+    for copy in saved[:3]:
+        copy.start()
+    for b in range(2):
+        span = slice(b * BLOCK, (b + 1) * BLOCK)
+        vt_buf[:, chunk * CHUNK + b * BLOCK : chunk * CHUNK + (b + 1) * BLOCK] = v_ref[span, :].T
+
+    def one_head(head, carry):
+        lanes = pl.ds(pl.multiple_of((head // 2) * 128, 128), 128)
+        chosen = head_lanes(head % 2)
+        deep = pl.ds(pl.multiple_of(head * HEAD, HEAD), HEAD)
+        for i in range(2):
+            span = slice(i * BLOCK, (i + 1) * BLOCK)
+            place = 2 * chunk + i
+            query = jnp.where(chosen, q_ref[span, lanes] * HEAD ** (-0.5), 0.0).astype(jnp.bfloat16)
+            top = jnp.full((1, BLOCK), -1e30, jnp.float32)
+            for j in range(place + 1):
+                rows = slice((j % 2) * BLOCK, (j % 2 + 1) * BLOCK)
+                scores = mm_nt(keys[j // 2][rows, lanes], query)
+                scores = jnp.where(position_mask(meta, place, j), scores, -1e30)
+                score_buf[j] = scores
+                top = jnp.maximum(top, jnp.max(scores, axis=0, keepdims=True))
+            total = jnp.zeros((1, BLOCK), jnp.float32)
+            mixed = jnp.zeros((HEAD, BLOCK), jnp.float32)
+            for j in range(place + 1):
+                weights = jnp.exp(score_buf[j] - top)
+                total = total + jnp.sum(weights, axis=0, keepdims=True)
+                mixed = mixed + mm(
+                    vt_buf[deep, j * BLOCK : (j + 1) * BLOCK], weights.astype(jnp.bfloat16)
+                )
+            mixed_ref[deep, span] = mixed / total
+            lse_ref[pl.ds(head, 1), span] = top + jnp.log(total)
+        return carry
+
+    lax.fori_loop(0, 4, one_head, 0)
+    for copy in saved[3:]:
+        copy.start()
+    for b in range(2):
+        span = slice(b * BLOCK, (b + 1) * BLOCK)
+        n_buf[span, :] = mm_nt(
+            mixed_ref[:, span].T.astype(jnp.bfloat16), w_buf[3]
+        ).astype(jnp.bfloat16)
+    share_out(meta, n_buf, keep, give)
+    for copy in saved:
+        copy.wait()
+
+
+def attend_call(layer, chunk, meta, blocks, before, shared, varied, weight):
+    bf, f32 = jnp.bfloat16, jnp.float32
+    wide = jax.ShapeDtypeStruct((CHUNK, 256), bf)
+    piece = jax.ShapeDtypeStruct((BLOCK, 1024), bf)
+    *saved, keep, give = pl.pallas_call(
+        functools.partial(attend_kernel, layer, chunk),
+        in_specs=[SMEM_SPACE] + [VMEM_SPACE] * (4 + 2 * chunk) + [HBM_SPACE] * 4,
+        out_specs=[HBM_SPACE] * 5 + [VMEM_SPACE] * 2,
+        out_shape=[wide, wide, wide, jax.ShapeDtypeStruct((8, CHUNK), f32),
+                   jax.ShapeDtypeStruct((256, CHUNK), f32), piece, piece],
+        scratch_shapes=[
+            pltpu.VMEM((CHUNK, 1024), bf),
+            pltpu.VMEM((4, 1024, 256), bf),
+            pltpu.VMEM((2 + 2 * chunk, BLOCK, BLOCK), f32),
+            pltpu.VMEM((256, CHUNK * (1 + chunk)), bf),
+            pltpu.VMEM((CHUNK, 256), bf),
+            pltpu.VMEM((CHUNK, 256), bf),
+            pltpu.VMEM((CHUNK, 256), bf),
+            pltpu.VMEM((8, CHUNK), f32),
+            pltpu.VMEM((256, CHUNK), f32),
+            pltpu.SemaphoreType.DMA,
+            pltpu.SemaphoreType.DMA((5,)),
+        ],
+        compiler_params=kernel_params(24),
+        cost_estimate=cost(3.5e9, 8e6),
+        name="attention_forward_%d" % chunk,
+    )(meta, shared, varied, *blocks, *(before if chunk else ()), *weight)
+    return saved, keep, give
+
+
+def attend_back_kernel(layer, chunk, meta, shared, varied, n_own, n_near, g_own, g_near, *rest):
+    q_ref, lse_ref, mixed_ref = rest[:3]
+    keys, values = rest[3 : 4 + chunk], rest[4 + chunk : 5 + 2 * chunk]
+    rest = rest[5 + 2 * chunk :]
+    if chunk == 0:
+        dk_in, dv_in, down_in, up_in = rest[:4]
+        keep, give, down_ref, up_ref = rest[8:12]
+        weight, scratch = rest[4:8], rest[12:]
+    else:
+        keep, give, down_ref, up_ref, dk_out, dv_out = rest[4:10]
+        weight, scratch = rest[:4], rest[10:]
+    (
+        n_buf, g_buf, w_buf, kt_buf, do_buf, delta_buf, dqt_buf, dk_buf, dv_buf, dq_buf, sem
+    ) = scratch
+    loaded = load_qkv_weight(layer, meta, weight, w_buf, sem)
+    lay_out(meta, g_own, g_near, g_buf)
+    lay_out(meta, n_own, n_near, n_buf)
+    for j in range(2 + 2 * chunk):
+        rows = slice((j % 2) * BLOCK, (j % 2 + 1) * BLOCK)
+        kt_buf[:, j * BLOCK : (j + 1) * BLOCK] = keys[j // 2][rows, :].T
+    if chunk == 0:
+        dk_buf[...] = dk_in[...]
+        dv_buf[...] = dv_in[...]
+    else:
+        dk_buf[...] = jnp.zeros_like(dk_buf)
+        dv_buf[...] = jnp.zeros_like(dv_buf)
+    loaded.wait()
+    do_buf[...] = mm(g_buf[...], w_buf[3]).astype(jnp.bfloat16)
+    for b in range(2):
+        span = slice(b * BLOCK, (b + 1) * BLOCK)
+        product = do_buf[span, :].astype(jnp.float32).T * mixed_ref[:, span]
+        for head in range(4):
+            delta_buf[head : head + 1, span] = jnp.sum(
+                product[head * HEAD : (head + 1) * HEAD], axis=0, keepdims=True
+            )
+
+    def one_head(head, carry):
+        lanes = pl.ds(pl.multiple_of((head // 2) * 128, 128), 128)
+        chosen = head_lanes(head % 2)
+        deep = pl.ds(pl.multiple_of(head * HEAD, HEAD), HEAD)
+        for i in range(2):
+            span = slice(i * BLOCK, (i + 1) * BLOCK)
+            place = 2 * chunk + i
+            query = jnp.where(chosen, q_ref[span, lanes] * HEAD ** (-0.5), 0.0).astype(jnp.bfloat16)
+            grad_mixed = jnp.where(chosen, do_buf[span, lanes], 0.0).astype(jnp.bfloat16)
+            lse = lse_ref[pl.ds(head, 1), span]
+            delta = delta_buf[pl.ds(head, 1), span]
+            grad_query = jnp.zeros((HEAD, BLOCK), jnp.float32)
+            for j in range(place + 1):
+                rows = slice((j % 2) * BLOCK, (j % 2 + 1) * BLOCK)
+                all_rows = slice(j * BLOCK, (j + 1) * BLOCK)
+                scores = mm_nt(keys[j // 2][rows, lanes], query)
+                probs = jnp.where(position_mask(meta, place, j), jnp.exp(scores - lse), 0.0)
+                grad_probs = mm_nt(values[j // 2][rows, lanes], grad_mixed)
+                grad_scores = (probs * (grad_probs - delta)).astype(jnp.bfloat16)
+                dv_buf[all_rows, lanes] += mm(probs.astype(jnp.bfloat16), grad_mixed)
+                dk_buf[all_rows, lanes] += mm(grad_scores, query)
+                grad_query = grad_query + mm(kt_buf[deep, all_rows], grad_scores)
+            dqt_buf[deep, span] = grad_query * HEAD ** (-0.5)
+        return carry
+
+    lax.fori_loop(0, 4, one_head, 0)
+    down = shared[layer, 8:16, :].astype(jnp.bfloat16)
+    up = varied[layer, 8:16, 0:512].astype(jnp.bfloat16)
+    for b in range(2):
+        span = slice(b * BLOCK, (b + 1) * BLOCK)
+        dq_buf[span, :] = dqt_buf[:, span].T.astype(jnp.bfloat16)
+    done = slice(chunk * CHUNK, (chunk + 1) * CHUNK)
+    normed = n_buf[...]
+    grad_q = dq_buf[...]
+    grad_k = dk_buf[done, :].astype(jnp.bfloat16)
+    grad_v = dv_buf[done, :].astype(jnp.bfloat16)
+    both = jnp.concatenate([grad_q, grad_v], axis=1)
+    low_grad = (adapter_scale * mm_nt(both, up)).astype(jnp.bfloat16)
+    low_grad_t = (adapter_scale * mm_nt(up, both)).astype(jnp.bfloat16)
+    low_t = mm_nt(down, normed).astype(jnp.bfloat16)
+    g_buf[...] = (
+        mm_nt(grad_q, w_buf[0]) + mm_nt(grad_k, w_buf[1]) + mm_nt(grad_v, w_buf[2])
+        + mm(low_grad, down)
+    ).astype(jnp.bfloat16)
+    share_out(meta, g_buf, keep, give)
+    total_down = mm(low_grad_t, normed)
+    total_up = adapter_scale * mm(low_t, both)
+    if chunk == 0:
+        total_down = total_down + down_in[...]
+        total_up = total_up + up_in[...]
+    else:
+        dk_out[...] = dk_buf[0:CHUNK, :]
+        dv_out[...] = dv_buf[0:CHUNK, :]
+    down_ref[...] = total_down
+    up_ref[...] = total_up
+
+
+def attend_back_call(layer, chunk, meta, blocks, grads, saved, carried, shared, varied, weight):
+    bf, f32 = jnp.bfloat16, jnp.float32
+    piece = jax.ShapeDtypeStruct((BLOCK, 1024), bf)
+    tall = jax.ShapeDtypeStruct((CHUNK, 256), f32)
+    spans = CHUNK * (1 + chunk)
+    q, _, _, lse, mixed = saved[chunk]
+    keys = [one[1] for one in saved[: chunk + 1]]
+    values = [one[2] for one in saved[: chunk + 1]]
+    inputs = (shared, varied, *blocks, *grads, q, lse, mixed, *keys, *values, *carried)
+    return pl.pallas_call(
+        functools.partial(attend_back_kernel, layer, chunk),
+        in_specs=[SMEM_SPACE] + [VMEM_SPACE] * len(inputs) + [HBM_SPACE] * 4,
+        out_specs=[VMEM_SPACE] * (4 + 2 * chunk),
+        out_shape=[piece, piece, jax.ShapeDtypeStruct((LOW, 1024), f32),
+                   jax.ShapeDtypeStruct((LOW, 512), f32)] + [tall] * (2 * chunk),
+        scratch_shapes=[
+            pltpu.VMEM((CHUNK, 1024), bf),
+            pltpu.VMEM((CHUNK, 1024), bf),
+            pltpu.VMEM((4, 1024, 256), bf),
+            pltpu.VMEM((256, spans), bf),
+            pltpu.VMEM((CHUNK, 256), bf),
+            pltpu.VMEM((8, CHUNK), f32),
+            pltpu.VMEM((256, CHUNK), f32),
+            pltpu.VMEM((spans, 256), f32),
+            pltpu.VMEM((spans, 256), f32),
+            pltpu.VMEM((CHUNK, 256), bf),
+            pltpu.SemaphoreType.DMA,
+        ],
+        compiler_params=kernel_params(24),
+        cost_estimate=cost(6e9, 12e6),
+        name="attention_backward_%d" % chunk,
+    )(meta, *inputs, *weight)
+
+
+def summed(passed, far):
+    return passed[...].astype(jnp.float32) + far[...].astype(jnp.float32)
+
+
+def rows_middle_kernel(layer, h_ref, passed, far, shared, middle_ref, normed_ref):
+    middle = h_ref[...].astype(jnp.float32) + summed(passed, far) + shared[layer, 4:5, :]
+    middle_ref[...] = middle
+    normed_ref[...] = layer_norm(middle, shared[layer, 1:2, :], shared[layer, 3:4, :]).astype(
+        jnp.bfloat16
+    )
+
+
+def load_units(layer, meta, pieces, w1, w2, sems):
+    own, other, (lead, trail) = pieces[0:2], pieces[2:4], pieces[4:6]
+    s, y, w = meta[0], meta[2], meta[8]
+    copies = []
+    for m, matrix in enumerate((w1, w2)):
+        start_pick(
+            (
+                ((s == y) & (s == layer), own[m]),
+                ((s == y) & (s != layer), other[m]),
+                ((s != y) & (w == m), lead),
+                ((s != y) & (w != m), trail),
+            ),
+            matrix,
+            sems.at[m],
+        )
+        copies.append(pltpu.make_async_copy(own[m], matrix, sems.at[m]))
+    return copies
+
+
+def stack_rows(blocks, target):
+    for i, block in enumerate(blocks):
+        target[i * BLOCK : (i + 1) * BLOCK, :] = block[...]
+
+
+def halve(total, keep, give):
+    keep[...] = total[:BLOCK].astype(jnp.bfloat16)
+    give[...] = total[BLOCK:].astype(jnp.bfloat16)
+
+
+def units_kernel(layer, meta, n0, n1, bias, *rest):
+    keep, give, slope_out, w1, w2, sems, n_buf, slope_buf, out_sem = rest[6:]
+    waits = load_units(layer, meta, rest[:6], w1, w2, sems)
+    stack_rows((n0, n1), n_buf)
+    waits[0].wait()
+    active, slope = gelu_both(mm(n_buf[...], w1[...]) + bias[layer, 0:1, :])
+    slope_buf[...] = slope.astype(jnp.bfloat16)
+    saving = pltpu.make_async_copy(slope_buf, slope_out, out_sem)
+    saving.start()
+    waits[1].wait()
+    halve(mm(active.astype(jnp.bfloat16), w2[...]), keep, give)
+    saving.wait()
+
+
+def units_turn_kernel(layer, meta, n0, n1, g0, g1, bias, *rest):
+    keep, give, out_keep, out_give, w1, w2, sems, n_buf, g_buf = rest[6:]
+    waits = load_units(layer, meta, rest[:6], w1, w2, sems)
+    stack_rows((n0, n1), n_buf)
+    stack_rows((g0, g1), g_buf)
+    for copy in waits:
+        copy.wait()
+    active, slope = gelu_both(mm(n_buf[...], w1[...]) + bias[layer, 0:1, :])
+    grad_hidden = (mm_nt(g_buf[...], w2[...]) * slope).astype(jnp.bfloat16)
+    halve(mm_nt(grad_hidden, w1[...]), keep, give)
+    halve(mm(active.astype(jnp.bfloat16), w2[...]), out_keep, out_give)
+
+
+def units_back_kernel(layer, meta, g0, g1, slope_in, *rest):
+    keep, give, w1, w2, sems, g_buf, slope_buf, in_sem = rest[6:]
+    waits = load_units(layer, meta, rest[:6], w1, w2, sems)
+    fetch = pltpu.make_async_copy(slope_in, slope_buf, in_sem)
+    fetch.start()
+    stack_rows((g0, g1), g_buf)
+    waits[1].wait()
+    fetch.wait()
+    grad = (mm_nt(g_buf[...], w2[...]) * slope_buf[...].astype(jnp.float32)).astype(jnp.bfloat16)
+    waits[0].wait()
+    halve(mm_nt(grad, w1[...]), keep, give)
+
+
+def rows_first_kernel(meta, mine, crossed, far_mine, far_crossed, shared, *outs):
+    holder = meta[0] == meta[1]
+    upper = meta[2] == 0
+    first = jnp.where(holder, mine[...], far_mine[...])
+    second = jnp.where(holder, crossed[...], far_crossed[...])
+    for c, (one, other) in enumerate(((first, second), (second, first))):
+        rows = jnp.where(upper, one, other)
+        outs[c][...] = rows
+        outs[2 + c][...] = layer_norm(
+            rows.astype(jnp.float32), shared[0, 0:1, :], shared[0, 2:3, :]
+        ).astype(jnp.bfloat16)
+
+
+def rows_next_kernel(middle, passed, far, shared, between_ref, normed_ref):
+    between = (middle[...] + summed(passed, far) + shared[0, 5:6, :]).astype(jnp.bfloat16)
+    between_ref[...] = between
+    normed_ref[...] = layer_norm(
+        between.astype(jnp.float32), shared[1, 0:1, :], shared[1, 2:3, :]
+    ).astype(jnp.bfloat16)
+
+
+def rows_turn_kernel(layer, middle, g_ref, passed, far, shared, grad_ref, sent_ref):
+    grad_middle = g_ref[...].astype(jnp.float32) + norm_back(
+        middle[...], shared[layer, 1:2, :], summed(passed, far)
+    )
+    grad_ref[...] = grad_middle
+    sent_ref[...] = grad_middle.astype(jnp.bfloat16)
+
+
+def rows_before_kernel(gm_ref, passed, far, between_ref, shared, grad_ref):
+    grad_rows = gm_ref[...] + norm_back(
+        between_ref[...].astype(jnp.float32), shared[1, 0:1, :], summed(passed, far)
+    )
+    grad_ref[...] = grad_rows.astype(jnp.bfloat16)
+
+
+def rows_output_kernel(middle, passed, far, shared, wide_ref, narrow_ref):
+    total = middle[...] + summed(passed, far) + shared[1, 5:6, :]
+    wide_ref[...] = total
+    narrow_ref[...] = total.astype(jnp.bfloat16)
+
+
+def rows_final_kernel(gm_ref, passed, far, h_ref, shared, wide_ref, narrow_ref):
+    grad_in = gm_ref[...] + norm_back(
+        h_ref[...].astype(jnp.float32), shared[0, 0:1, :], summed(passed, far)
+    )
+    wide_ref[...] = grad_in
+    narrow_ref[...] = grad_in.astype(jnp.bfloat16)
+
+
+def units_call(kernel, meta, small, saved, weights, outs, saving, scratch, name):
+    return pl.pallas_call(
+        kernel,
+        in_specs=[SMEM_SPACE] + [VMEM_SPACE] * len(small) + [HBM_SPACE] * (len(saved) + len(weights)),
+        out_specs=[VMEM_SPACE] * len(outs) + [HBM_SPACE] * len(saving),
+        out_shape=[*outs, *saving],
+        scratch_shapes=scratch,
+        compiler_params=kernel_params(24),
+        cost_estimate=cost(2e9, 8e6),
+        name=name,
+    )(meta, *small, *saved, *weights)
+
+
+def plain_call(kernel, scalar, small, large, outs, scratch, flops, name):
+    specs = [VMEM_SPACE] * len(small) + [HBM_SPACE] * len(large)
+    operands = (*small, *large)
+    if scalar is not None:
+        specs, operands = [SMEM_SPACE] + specs, (scalar, *operands)
+    return pl.pallas_call(
+        kernel,
+        in_specs=specs,
+        out_specs=[VMEM_SPACE] * len(outs),
+        out_shape=outs,
+        scratch_shapes=scratch,
+        compiler_params=kernel_params(24),
+        cost_estimate=cost(flops, 8e6),
+        name=name,
+    )(*operands)
+
+
+def deal_rows(source, slots, section, y):
+    same = lax.dynamic_index_in_dim(slots, y, 0, keepdims=False)
+    cross = lax.dynamic_index_in_dim(slots, 1 - y, 0, keepdims=False)
+    moved = send(same, lambda s, t: (t & 1, t) if s == source and s != t & 1 else None)
+    crossed = send(cross, lambda s, t: (t & 1, t ^ 2) if s == source else None)
+    mine = jnp.where(section == source, same, moved)
+    return mine, crossed
+
+
+def to_x(block):
+    return send(block, lambda s, t: (s, t ^ 1) if s == t & 1 else None)
+
+
+def from_x(block):
+    return send(block, lambda s, t: (s, t ^ 1) if s != t & 1 else None)
+
+
+def z_swap(block):
+    size = lax.axis_size("dp")
+    pairs = [
+        ((s * size + z) * 4 + t, (s * size + (z ^ 1)) * 4 + t)
+        for s in range(2) for z in range(size) for t in range(4) if s != t >> 1
+    ]
+    return lax.ppermute(block, ("section", "dp", "tensor"), pairs)
+
+
+def chip_sum(keep, give, last, swap=x_swap):
+    take = other_core(after(give, last))
+    passed = (keep.astype(jnp.float32) + take.astype(jnp.float32)).astype(jnp.bfloat16)
+    return passed, swap(passed)
+
+
+def total_over_z(downs, ups):
+    both = jnp.concatenate([jnp.concatenate(downs), jnp.concatenate(ups)], axis=1)
+    size = lax.axis_size("dp")
+    step = 1
+    while step < size:
+        both = both + lax.ppermute(both, "dp", [(i, i ^ step) for i in range(size)])
+        step *= 2
+    return both
+
+
+def total_over_cores(both, section, y):
+    both = both + y_swap(both)
+    moved = other_core(both)
+    down = both[:, :1024] + moved[:, :1024]
+    down = jnp.where(section == 0, down[:LOW], down[LOW:])
+    up = jnp.where(section == y, both[:, 1024:], moved[:, 1024:])
+    return down + x_swap(down), jnp.where(section == 0, up[:LOW], up[LOW:])
+
+
+def relay_body(
+    activations, starts, attention_weights, projection_weight, feedforward_weight, output_weight,
+    norm_gains, norm_biases, output_biases, query_value_bias, feedforward_bias,
+    adapter_down_weight, adapter_up_weight,
+):
+    bf, f32 = jnp.bfloat16, jnp.float32
+    section = lax.axis_index("section")
+    place = lax.axis_index("tensor")
+    y, x = place // 2, place % 2
+    first = section == 0
+
+    mine, crossed = deal_rows(0, activations[0], section, y)
+    down_rows = adapter_down_weight[0].astype(f32).transpose(0, 2, 1).reshape(LOW, 1024)
+    up0 = adapter_up_weight[0, 0].astype(f32)
+    up1 = adapter_up_weight[0, 1].astype(f32)
+    zero = jnp.zeros((ADAPTER_RANK, 256), f32)
+    common = jnp.concatenate(
+        [norm_gains[0], norm_biases[0], output_biases[0], jnp.zeros((2, 1024), f32), down_rows]
+    )
+    own_part = jnp.concatenate(
+        [
+            feedforward_bias,
+            jnp.pad(query_value_bias[0].reshape(1, 512), ((0, 0), (0, 512))),
+            jnp.zeros((6, 1024), f32),
+            jnp.concatenate([up0, zero, jnp.zeros((ADAPTER_RANK, 512), f32)], axis=1),
+            jnp.concatenate([zero, up1, jnp.zeros((ADAPTER_RANK, 512), f32)], axis=1),
+        ]
+    )
+    partner = other_core(common)
+    partner_part = other_core(own_part)
+    parts = jnp.where(
+        first, jnp.stack([own_part, partner_part]), jnp.stack([partner_part, own_part])
+    )
+    near_varied = jnp.where(section == y, parts, y_swap(parts))
+    shared = jnp.where(first, jnp.stack([common, partner]), jnp.stack([partner, common]))
+    meta = jnp.concatenate(
+        [
+            jnp.stack([section, x, y, place]).astype(jnp.int32),
+            lax.dynamic_index_in_dim(starts, y, 0, keepdims=False).reshape(4),
+            (lax.axis_index("dp") % 2).astype(jnp.int32)[None],
+        ]
+    )
+    even = lax.axis_index("dp") % 2 == 0
+    own_a = jnp.concatenate([attention_weights[0], projection_weight[0].T[None]])
+    w1_own, w2_own = feedforward_weight[0], output_weight[0]
+    other_a = other_core(own_a)
+    mine, crossed, shared = lax.optimization_barrier((mine, crossed, shared))
+    lead_a0 = cross_send(after(jnp.where(even, own_a[:2], own_a[2:]), crossed, near_varied))
+    far_mine, far_crossed = to_x(mine), to_x(crossed)
+    g_mine, g_crossed = deal_rows(1, after(activations[0], crossed), section, y)
+    far_crossed, g_mine, g_crossed = lax.optimization_barrier((far_crossed, g_mine, g_crossed))
+    trail_a0 = z_swap(after(lead_a0, far_mine, far_crossed))
+
+    sheet = jax.ShapeDtypeStruct((BLOCK, 1024), f32)
+    thin = jax.ShapeDtypeStruct((BLOCK, 1024), bf)
+    slope_shape = jax.ShapeDtypeStruct((CHUNK, 1024), bf)
+    matrices = [
+        pltpu.VMEM((1024, 1024), bf), pltpu.VMEM((1024, 1024), bf), pltpu.SemaphoreType.DMA((2,))
+    ]
+    group = pltpu.VMEM((CHUNK, 1024), bf)
+
+    def small(kernel, *operands, outs, name):
+        return plain_call(kernel, None, operands, (), outs, [], 1e7, name)
+
+    def attend(layer, chunk, normed, before, weight, near=None):
+        near = other_core(normed) if near is None else near
+        return attend_call(
+            layer, chunk, meta, (normed, near), before, shared, near_varied, weight
+        )
+
+    def units(layer, normed, weight):
+        return units_call(
+            functools.partial(units_kernel, layer), meta, (normed, other_core(normed), near_varied),
+            (), weight, [thin, thin], [slope_shape],
+            [*matrices, group, group, pltpu.SemaphoreType.DMA], "units",
+        )
+
+    def units_turn(layer, normed, grad, near_grad, weight):
+        return units_call(
+            functools.partial(units_turn_kernel, layer), meta,
+            (normed, other_core(normed), grad, near_grad, near_varied), (), weight,
+            [thin] * 4, [], [*matrices, group, group], "units_turn",
+        )
+
+    def units_back(layer, grad, slope, weight):
+        return units_call(
+            functools.partial(units_back_kernel, layer), meta, (grad, other_core(grad)), (slope,),
+            weight, [thin, thin], [], [*matrices, group, group, pltpu.SemaphoreType.DMA],
+            "units_back",
+        )
+
+    def middle(layer, rows, sums):
+        return small(
+            functools.partial(rows_middle_kernel, layer), rows, *sums, shared, outs=[sheet, thin],
+            name="rows_middle",
+        )
+
+    def turn(layer, middle_rows, grad, sums):
+        return small(
+            functools.partial(rows_turn_kernel, layer), middle_rows, grad, *sums, shared,
+            outs=[sheet, thin], name="rows_turn",
+        )
+
+    row0, row1, n0, n1 = plain_call(
+        rows_first_kernel, meta, (mine, crossed, far_mine, far_crossed, shared), (), [thin] * 4,
+        [], 1e7, "rows_first",
+    )
+    g_far = [to_x(one) for one in (g_mine, g_crossed)]
+    weights_a0 = (own_a, other_a, lead_a0, trail_a0)
+    near_n0 = other_core(n0)
+    lead_b0 = cross_send(jnp.where(even, *after((w1_own, w2_own), near_n0)))
+    n00, n01 = n0, n1
+    saved00, keep, give = attend(0, 0, n0, (), weights_a0, near_n0)
+    keep, give, g_far = lax.optimization_barrier((keep, give, g_far))
+    sum0 = chip_sum(keep, give, lead_a0)
+    other_w1, other_w2 = (other_core(after(one, sum0[0])) for one in (w1_own, w2_own))
+    trail_b0 = z_swap(after(lead_b0, sum0[0]))
+    weights_b0 = (w1_own, w2_own, other_w1, other_w2, lead_b0, trail_b0)
+    saved01, keep, give = attend(0, 1, n1, saved00[1:3], weights_a0)
+    sum1 = chip_sum(keep, give, sum0[1])
+    lead_a1 = cross_send(jnp.where(even, *after((other_a[:2], other_a[2:]), sum0[0])))
+    middle00, n0 = middle(0, row0, sum0)
+    keep, give, slope0 = units(0, n0, weights_b0)
+    sum2 = chip_sum(keep, give, sum1[1])
+    sum1, lead_a1 = lax.optimization_barrier((sum1, lead_a1))
+    trail_a1 = z_swap(lead_a1)
+    lead_b1 = cross_send(jnp.where(even, *after((other_w1, other_w2), lead_a1)))
+    middle01, n1 = middle(0, row1, sum1)
+    keep, give, slope1 = units(0, n1, weights_b0)
+    sum3 = chip_sum(keep, give, sum2[1])
+    weights_a1 = (own_a, other_a, lead_a1, trail_a1)
+    between0, n10 = small(rows_next_kernel, middle00, *sum2, shared, outs=[thin, thin], name="rows_next")
+    saved10, keep, give = attend(1, 0, n10, (), weights_a1)
+    sum4 = chip_sum(keep, give, sum3[1])
+    sum3, lead_b1 = lax.optimization_barrier((sum3, lead_b1))
+    trail_b1 = z_swap(lead_b1)
+    weights_b1 = (w1_own, w2_own, other_w1, other_w2, lead_b1, trail_b1)
+    between1, n11 = small(rows_next_kernel, middle01, *sum3, shared, outs=[thin, thin], name="rows_next")
+    saved11, keep, give = attend(1, 1, n11, saved10[1:3], weights_a1)
+    sum5 = chip_sum(keep, give, sum4[1])
+    holder, upper = section == x, y == 0
+    mine, crossed = (
+        jnp.where(holder, one, two) for one, two in zip((g_mine, g_crossed), after(g_far, sum4[0]))
+    )
+    grad_outs = (jnp.where(upper, mine, crossed), jnp.where(upper, crossed, mine))
+    near_outs = [other_core(one) for one in grad_outs]
+    middle10, m0 = middle(1, between0, sum4)
+    keep, give, out_keep0, out_give0 = units_turn(1, m0, grad_outs[0], near_outs[0], weights_b1)
+    sum6 = chip_sum(keep, give, sum5[1])
+    middle11, m1 = middle(1, between1, sum5)
+    keep, give, out_keep1, out_give1 = units_turn(1, m1, grad_outs[1], near_outs[1], weights_b1)
+    sum7 = chip_sum(keep, give, sum6[1])
+    grad_middle10, g0 = turn(1, middle10, grad_outs[0], sum6)
+    grad_middle11, g1 = turn(1, middle11, grad_outs[1], sum7)
+    keep, give, down1, up1, dk, dv = attend_back_call(
+        1, 1, meta, (n11, other_core(n11)), (g1, other_core(g1)), (saved10, saved11), (), shared,
+        near_varied, weights_a1,
+    )
+    out_sums = [
+        chip_sum(*after(one, g1), sum7[1], from_x)
+        for one in ((out_keep0, out_give0), (out_keep1, out_give1))
+    ]
+    keep, give, out_sums = lax.optimization_barrier((keep, give, out_sums))
+    sum8 = chip_sum(keep, give, sum7[1])
+    keep, give, down1, up1 = attend_back_call(
+        1, 0, meta, (n10, other_core(n10)), (g0, other_core(g0)), (saved10, saved11),
+        (dk, dv, down1, up1), shared, near_varied, weights_a1,
+    )
+    sum9 = chip_sum(keep, give, sum8[1])
+    before1 = small(
+        rows_before_kernel, grad_middle11, *sum8, between1, shared, outs=[thin], name="rows_before"
+    )[0]
+    keep, give = units_back(0, before1, slope1, weights_b0)
+    sum10 = chip_sum(keep, give, sum9[1])
+    outs = [
+        small(rows_output_kernel, one, *after(two, keep), shared, outs=[sheet, thin],
+              name="rows_output")
+        for one, two in zip((middle10, middle11), out_sums)
+    ]
+    out_wide = jnp.where(upper, outs[0][0], outs[1][0])
+    out_same, out_cross = collect(1, out_wide, jnp.where(upper, outs[1][1], outs[0][1]))
+    sum9, out_same, out_cross = lax.optimization_barrier((sum9, out_same, out_cross))
+    before0 = small(
+        rows_before_kernel, grad_middle10, *sum9, between0, shared, outs=[thin], name="rows_before"
+    )[0]
+    keep, give = units_back(0, before0, slope0, weights_b0)
+    sum11 = chip_sum(keep, give, sum10[1])
+    grad_middle01, h1 = turn(0, middle01, before1, sum10)
+    keep, give, down0, up0, dk, dv = attend_back_call(
+        0, 1, meta, (n01, other_core(n01)), (h1, other_core(h1)), (saved00, saved01), (), shared,
+        near_varied, weights_a0,
+    )
+    sum12 = chip_sum(keep, give, sum11[1], from_x)
+    grad_middle00, h0 = turn(0, middle00, before0, sum11)
+    keep, give, down0, up0 = attend_back_call(
+        0, 0, meta, (n00, other_core(n00)), (h0, other_core(h0)), (saved00, saved01),
+        (dk, dv, down0, up0), shared, near_varied, weights_a0,
+    )
+    sum13 = chip_sum(keep, give, sum12[1], from_x)
+    totals = total_over_z((down0, down1), after((up0, up1), sum13[0]))
+    sum13, totals = lax.optimization_barrier((sum13, totals))
+    ends = [
+        small(rows_final_kernel, one, *two, three, shared, outs=[sheet, thin], name="rows_final")
+        for one, two, three in ((grad_middle00, sum13, row0), (grad_middle01, sum12, row1))
+    ]
+    wide = jnp.where(upper, ends[0][0], ends[1][0])
+    in_same, in_cross = collect(0, wide, jnp.where(upper, ends[1][1], ends[0][1]))
+    grad_down, grad_up = total_over_cores(totals, section, y)
+    same = jnp.where(
+        first, jnp.where(x == 0, wide, in_same), jnp.where(x == 1, out_wide, out_same)
+    )
+    cross = jnp.where(first, in_cross, out_cross).astype(f32)
+    combined = jnp.where(y == 0, jnp.stack([same, cross]), jnp.stack([cross, same]))
+    return (
+        combined[None],
+        grad_down.reshape(1, 2, ADAPTER_RANK, 1024).transpose(0, 1, 3, 2),
+        jnp.stack([grad_up[:ADAPTER_RANK, :256], grad_up[ADAPTER_RANK:, 256:]])[None],
+    )
+
+
+def body(*arrays):
+    dp = lax.axis_size("dp")
+    known = (
+        arrays[0].shape == (1, 2, BLOCK, 1024)
+        and lax.axis_size("tensor") == 4
+        and lax.axis_size("section") == 2
+        and arrays[3].shape == (1, 256, 1024)
+        and arrays[5].shape == (1, 1024, 1024)
+        and dp & (dp - 1) == 0
+    )
+    return relay_body(*arrays) if known else plain_body(*arrays)
+
+
 def solution(mesh):
     placed = (
         P("section", None, ("dp", "tensor"), None),

time: 1700 us -> 377 us (0.22)
  waiting for transfers between devices: 1060 us -> 113 us
  matrix products: 339 us -> 0 us
  other arithmetic: 139 us -> 15.9 us
  Pallas kernels: 0 us -> 107 us
  starting transfers between devices: 20.4 us -> 111 us
  blocking collectives: 86.2 us -> 0 us
    reduce_scatter x15 -> x0, waiting for transfers between devices: 534 us -> none  [the longest x6 288 us: forward_relay(): lax.psum_scatter(jnp.dot(mixed, projection_weight[0], preferred_element_t...]
    all_gather x18 -> x0, waiting for transfers between devices: 521 us -> none  [the longest x6 174 us: forward_relay(): gathered = lax.all_gather(normalized_rows, 'tensor', axis=0, tiled=True)]
    dot_general x84 -> x0, matrix products: 306 us -> none  [the longest x27 59 us: contract_axes(): lax.dot_general(left, right, (((left_dim,), (right_dim,)), ((), ())), pre...]
    pallas_call x0 -> x31, Pallas kernels: none -> 107 us  [the longest x4 36 us: attend_back_call(): pl.pallas_call(functools.partial(attend_back_kernel, layer, chunk), in_sp...]
    ppermute x4 -> x79, waiting for transfers between devices: 8.18 us -> 113 us  [the longest x73 109 us: send(): return lax.ppermute(block, ('section', 'tensor'), pairs)]
    ppermute x4 -> x79, starting transfers between devices: 6.86 us -> 111 us  [the longest x73 102 us: send(): return lax.ppermute(block, ('section', 'tensor'), pairs)]
    psum x2 -> x0, blocking collectives: 86.2 us -> none  [reduce_adapters(): return (lax.psum(part_a, ('dp', 'tensor')), lax.psum(second_portion, 'dp'))]
    reduce_sum x39 -> x0, other arithmetic: 61.6 us -> none  [the longest x3 24.5 us: attend(): total = jnp.sum(weights, axis=-1, keepdims=True)]
  transfers between devices with their start and end apart: 37 -> 79, of which waited for: 34 -> 36; matrix products, arithmetic and copies ran while one was open for 10% -> 4% of each run, Pallas kernels for 0% -> 29%
where the time goes in v3:
time: 377 us; the launch traced here: 370 us
  waiting for transfers between devices  113 us (30%)
  starting transfers between devices  111 us (29%)
  Pallas kernels  107 us (28%)
  local copies, waits for them, and re-layouts  20.3 us (5%)
  other arithmetic  15.9 us (4%)
    ppermute x73, waiting for transfers between devices, send(): return lax.ppermute(block, ('section', 'tensor'), pairs)  109 us
    ppermute x73, starting transfers between devices, send(): return lax.ppermute(block, ('section', 'tensor'), pairs)  102 us
    pallas_call x4, Pallas kernels, attend_back_call(): pl.pallas_call(functools.partial(attend_back_kernel, layer, chunk), in_sp...  36 us
    pallas_call x4, Pallas kernels, attend_call(): pl.pallas_call(functools.partial(attend_kernel, layer, chunk), in_specs=[...  31.3 us
    pallas_call x6, Pallas kernels, units_call(): pl.pallas_call(kernel, in_specs=[SMEM_SPACE] + [VMEM_SPACE] * len(small)...  28 us
    unnamed x244, local copies, waits for them, and re-layouts  16.3 us
    pallas_call x17, Pallas kernels, plain_call(): pl.pallas_call(kernel, in_specs=specs, out_specs=[VMEM_SPACE] * len(outs)...  11.8 us
  transfers between devices with their start and end apart: 79, of which 36 were waited for; matrix products, arithmetic and copies ran while one was open for 4% of the time, Pallas kernels for 29%

profile of v3, /device:TPU:0, one launch (start us, length us, event | category | flops | bytes accessed | tf_op | source)
XLA Modules:
  0.0 369.8 jit_solution(13407116903368767974)
XLA Ops:
  4.5 4.9 %collective-permute-start.1 = (bf16[256,1024]{1,0:T(8,128)(2,1)}, bf16[256,1024]{1,0:T(8,128)(2,1)S(1)}, u32[]{:S(2)}, u32[]{:S(2)}) collective-permute-start(bf16[256,1024]{1,0:T(8,128)(2,1)} %get-tuple-element.343), channel_id=1, source_target_pairs={{0,2},{1,19},{2,0},{3,17},{4,6},{5,23},{6,4},{7,21},{8,10},{9,27},... | collective-permute-start | bytes 1572872 | tf_op jit(solution)/shard_map/ppermute | solution.py:346
  13.2 4.9 %collective-permute-done.1.crossed = bf16[256,1024]{1,0:T(8,128)(2,1)S(1)} collective-permute-done((bf16[256,1024]{1,0:T(8,128)(2,1)}, bf16[256,1024]{1,0:T(8,128)(2,1)S(1)}, u32[]{:S(2)}, u32[]{:S(2)}) %collective-permute-start.1) | collective-permute-done | bytes 524320 | tf_op jit(solution)/shard_map/ppermute | solution.py:346
  47.8 5.6 %collective-permute-start.13 = (bf16[256,1024]{1,0:T(8,128)(2,1)S(1)}, bf16[256,1024]{1,0:T(8,128)(2,1)S(1)}, u32[]{:S(2)}, u32[]{:S(2)}) collective-permute-start(bf16[256,1024]{1,0:T(8,128)(2,1)S(1)} %broadcast_select_fusion.5), channel_id=1, source_target_pairs={{0,1},{2,3},{17,16},{19,18},{4,5},{6,7},{21,20},{23,22},{8,9},{10,... | collective-permute-start | bytes 1572872 | tf_op jit(solution)/shard_map/ppermute | solution.py:346
  54.7 6.5 %attention_forward_0.2 = (bf16[512,256]{1,0:T(8,128)(2,1)S(1)}, bf16[512,256]{1,0:T(8,128)(2,1)S(1)}, bf16[512,256]{1,0:T(8,128)(2,1)S(1)}, f32[8,512]{1,0:T(8,1...) custom-call(s32[9]{0:T(128)S(1)} %concatenate.41.meta, ...), custom_call_target="tpu_custom_call" | custom-call | flops 1000 | bytes 1000 | tf_op jit(solution)/shard_map/attention_forward_0/pallas_call | solution.py:554
  79.5 8.6 %attention_forward_1.2 = (bf16[512,256]{1,0:T(8,128)(2,1)S(1)}, bf16[512,256]{1,0:T(8,128)(2,1)S(1)}, bf16[512,256]{1,0:T(8,128)(2,1)S(1)}, f32[8,512]{1,0:T(8,1...) custom-call(s32[9]{0:T(128)S(1)} %concatenate.41.meta, ...), custom_call_target="tpu_custom_call" | custom-call | flops 1000 | bytes 1000 | tf_op jit(solution)/shard_map/attention_forward_1/pallas_call | solution.py:554
  113.3 5.5 %collective-permute-start.37 = (bf16[1024,1024]{1,0:T(8,128)(2,1)S(1)}, bf16[1024,1024]{1,0:T(8,128)(2,1)}, u32[]{:S(2)}, u32[]{:S(2)}) collective-permute-start(bf16[1024,1024]{1,0:T(8,128)(2,1)S(1)} %broadcast_select_fusion), channel_id=1, source_target_pairs={{0,2},{1,3},{2,16},{3,17},{4,6},{5,7},{6,20},{7,21},{8,10},{9,11},... | collective-permute-start | bytes 6291464 | tf_op jit(solution)/shard_map/ppermute | solution.py:346
  118.8 4.9 %units.3 = (bf16[256,1024]{1,0:T(8,128)(2,1)S(1)}, bf16[256,1024]{1,0:T(8,128)(2,1)S(1)}, bf16[512,1024]{1,0:T(8,128)(2,1)S(1)}) custom-call(s32[9]{0:T(128)S(1)} %concatenate.41.meta, bf16[256,1024]{1,0:T(8,128)(2,1)S(1)} %get-tuple-element.212.n0, bf16[256,1024]{1,0:T(8,128)(2,1)S(1)} %collective-permute-done.30.n1, ...), custom_call_target="tpu_custom_call" | custom-call | flops 1000 | bytes 1000 | tf_op jit(solution)/shard_map/units/pallas_call | solution.py:839
  130.7 6.5 %attention_forward_0.3 = (bf16[512,256]{1,0:T(8,128)(2,1)S(1)}, bf16[512,256]{1,0:T(8,128)(2,1)S(1)}, bf16[512,256]{1,0:T(8,128)(2,1)S(1)}, f32[8,512]{1,0:T(8,1...) custom-call(s32[9]{0:T(128)S(1)} %concatenate.41.meta, ...), custom_call_target="tpu_custom_call" | custom-call | flops 1000 | bytes 1000 | tf_op jit(solution)/shard_map/attention_forward_0/pallas_call | solution.py:554
  138.0 4.8 %collective-permute-done.32.far = bf16[256,1024]{1,0:T(8,128)(2,1)S(1)} collective-permute-done((bf16[256,1024]{1,0:T(8,128)(2,1)S(1)}, bf16[256,1024]{1,0:T(8,128)(2,1)S(1)}, u32[]{:S(2)}, u32[]{:S(2)}) %collective-permute-start.32) | collective-permute-done | bytes 524320 | tf_op jit(solution)/shard_map/ppermute | solution.py:346
  142.7 6.3 %collective-permute-start.33 = (bf16[256,1024]{1,0:T(8,128)(2,1)S(1)}, bf16[256,1024]{1,0:T(8,128)(2,1)S(1)}, u32[]{:S(2)}, u32[]{:S(2)}) collective-permute-start(bf16[256,1024]{1,0:T(8,128)(2,1)S(1)} %get-tuple-element.216), channel_id=1, source_target_pairs={{0,16},{1,17},{2,18},{3,19},{16,0},{17,1},{18,2},{19,3},{4,20},{5,... | collective-permute-start | bytes 1572872 | tf_op jit(solution)/shard_map/ppermute | solution.py:346
  153.9 9.7 %attention_forward_1.3 = (bf16[512,256]{1,0:T(8,128)(2,1)S(1)}, bf16[512,256]{1,0:T(8,128)(2,1)S(1)}, bf16[512,256]{1,0:T(8,128)(2,1)S(1)}, f32[8,512]{1,0:T(8,1...) custom-call(s32[9]{0:T(128)S(1)} %concatenate.41.meta, ...), custom_call_target="tpu_custom_call" | custom-call | flops 1000 | bytes 1000 | tf_op jit(solution)/shard_map/attention_forward_1/pallas_call | solution.py:554
  178.9 5.6 %units_turn.2 = (bf16[256,1024]{1,0:T(8,128)(2,1)S(1)}, bf16[256,1024]{1,0:T(8,128)(2,1)S(1)}, bf16[256,1024]{1,0:T(8,128)(2,1)S(1)}, bf16[256,1024]{1,0:T(8,128)(2,1)S(1)}) custom-call(s32[9]{0:T(128)S(1)} %concatenate.41.meta, bf16[256,1024]{1,0:T(8,128)(2,1)S(1)} %get-tuple-element.222.n0, bf16[256,1024]{1,0:T(8,128)(2,1)S(1)} %collective-permute-done.35.n1, ...), custom_call_target="tpu_custom_call" | custom-call | flops 1000 | bytes 1000 | tf_op jit(solution)/shard_map/units_turn/pallas_call | solution.py:839
  184.5 5.5 %collective-permute-done.41.far = bf16[256,1024]{1,0:T(8,128)(2,1)S(1)} collective-permute-done((bf16[256,1024]{1,0:T(8,128)(2,1)S(1)}, bf16[256,1024]{1,0:T(8,128)(2,1)S(1)}, u32[]{:S(2)}, u32[]{:S(2)}) %collective-permute-start.41) | collective-permute-done | bytes 524320 | tf_op jit(solution)/shard_map/ppermute | solution.py:346
  193.7 5.8 %units_turn.3 = (bf16[256,1024]{1,0:T(8,128)(2,1)S(1)}, bf16[256,1024]{1,0:T(8,128)(2,1)S(1)}, bf16[256,1024]{1,0:T(8,128)(2,1)S(1)}, bf16[256,1024]{1,0:T(8,128)(2,1)S(1)}) custom-call(s32[9]{0:T(128)S(1)} %concatenate.41.meta, bf16[256,1024]{1,0:T(8,128)(2,1)S(1)} %get-tuple-element.245.n0, bf16[256,1024]{1,0:T(8,128)(2,1)S(1)} %collective-permute-done.45.n1, ...), custom_call_target="tpu_custom_call" | custom-call | flops 1000 | bytes 1000 | tf_op jit(solution)/shard_map/units_turn/pallas_call | solution.py:839
  199.5 6.7 %collective-permute-done.43.far = bf16[256,1024]{1,0:T(8,128)(2,1)S(1)} collective-permute-done((bf16[256,1024]{1,0:T(8,128)(2,1)S(1)}, bf16[256,1024]{1,0:T(8,128)(2,1)S(1)}, u32[]{:S(2)}, u32[]{:S(2)}) %collective-permute-start.43) | collective-permute-done | bytes 524320 | tf_op jit(solution)/shard_map/ppermute | solution.py:346
  209.8 12.4 %collective-permute-done.48.far = bf16[256,1024]{1,0:T(8,128)(2,1)S(1)} collective-permute-done((bf16[256,1024]{1,0:T(8,128)(2,1)S(1)}, bf16[256,1024]{1,0:T(8,128)(2,1)S(1)}, u32[]{:S(2)}, u32[]{:S(2)}) %collective-permute-start.48) | collective-permute-done | bytes 524320 | tf_op jit(solution)/shard_map/ppermute | solution.py:346
  228.2 11.0 %attention_backward_1.2 = (bf16[256,1024]{1,0:T(8,128)(2,1)S(1)}, bf16[256,1024]{1,0:T(8,128)(2,1)S(1)}, f32[8,1024]{1,0:T(8,128)S(1)}, f32[8,512]{1,0:T(8,128)S...) custom-call(s32[9]{0:T(128)S(1)} %concatenate.41.meta, f32[2,16,1024]{2,1,0:T(8,128)S(1)} %maximum_select_fusion.1.shared, ...), custom_call_target="tpu_custom_call" | custom-call | flops 1000 | bytes 1000 | tf_op jit(solution)/shard_map/attention_backward_1/pallas_call | solution.py:682
  245.2 12.9 %collective-permute-done.55.far = bf16[256,1024]{1,0:T(8,128)(2,1)S(1)} collective-permute-done((bf16[256,1024]{1,0:T(8,128)(2,1)S(1)}, bf16[256,1024]{1,0:T(8,128)(2,1)S(1)}, u32[]{:S(2)}, u32[]{:S(2)}) %collective-permute-start.55) | collective-permute-done | bytes 524320 | tf_op jit(solution)/shard_map/ppermute | solution.py:346
  259.0 7.0 %attention_backward_0.2 = (bf16[256,1024]{1,0:T(8,128)(2,1)S(1)}, bf16[256,1024]{1,0:T(8,128)(2,1)S(1)}, f32[8,1024]{1,0:T(8,128)S(1)}, f32[8,512]{1,0:T(8,128)S(1)}) custom-call(s32[9]{0:T(128)S(1)} %concatenate.41.meta, f32[2,16,1024]{2,1,0:T(8,128)S(1)} %maximum_select_fusion.1.shared, f32[2,16,1024]{2,1,0:T(8,128)S(1)} %broadcast_select_fusion.13.varied.bias, ...), custom_call_target="tpu_custom_call" | custom-call | flops 1000 | bytes 1000 | tf_op jit(solution)/shard_map/attention_backward_0/pallas_call | solution.py:682
  273.6 4.9 %collective-permute-start.60 = (bf16[256,1024]{1,0:T(8,128)(2,1)S(1)}, bf16[256,1024]{1,0:T(8,128)(2,1)}, u32[]{:S(2)}, u32[]{:S(2)}) collective-permute-start(bf16[256,1024]{1,0:T(8,128)(2,1)S(1)} %broadcast_select_fusion.8), channel_id=1, source_target_pairs={{0,18},{2,16},{17,19},{19,17},{4,22},{6,20},{21,23},{23,21},{8,26}... | collective-permute-start | bytes 1572872 | tf_op jit(solution)/shard_map/ppermute | solution.py:346
  278.5 8.2 %collective-permute-done.57.far = bf16[256,1024]{1,0:T(8,128)(2,1)S(1)} collective-permute-done((bf16[256,1024]{1,0:T(8,128)(2,1)S(1)}, bf16[256,1024]{1,0:T(8,128)(2,1)S(1)}, u32[]{:S(2)}, u32[]{:S(2)}) %collective-permute-start.57) | collective-permute-done | bytes 524320 | tf_op jit(solution)/shard_map/ppermute | solution.py:346
  294.2 9.0 %collective-permute-done.63.far = bf16[256,1024]{1,0:T(8,128)(2,1)S(1)} collective-permute-done((bf16[256,1024]{1,0:T(8,128)(2,1)S(1)}, bf16[256,1024]{1,0:T(8,128)(2,1)S(1)}, u32[]{:S(2)}, u32[]{:S(2)}) %collective-permute-start.63) | collective-permute-done | bytes 524320 | tf_op jit(solution)/shard_map/ppermute | solution.py:346
  306.3 10.8 %attention_backward_1.3 = (bf16[256,1024]{1,0:T(8,128)(2,1)S(1)}, bf16[256,1024]{1,0:T(8,128)(2,1)S(1)}, f32[8,1024]{1,0:T(8,128)S(1)}, f32[8,512]{1,0:T(8,128)S...) custom-call(s32[9]{0:T(128)S(1)} %concatenate.41.meta, f32[2,16,1024]{2,1,0:T(8,128)S(1)} %maximum_select_fusion.1.shared, ...), custom_call_target="tpu_custom_call" | custom-call | flops 1000 | bytes 1000 | tf_op jit(solution)/shard_map/attention_backward_1/pallas_call | solution.py:682
  323.0 7.3 %attention_backward_0.3 = (bf16[256,1024]{1,0:T(8,128)(2,1)S(1)}, bf16[256,1024]{1,0:T(8,128)(2,1)S(1)}, f32[8,1024]{1,0:T(8,128)S(1)}, f32[8,512]{1,0:T(8,128)S(1)}) custom-call(s32[9]{0:T(128)S(1)} %concatenate.41.meta, f32[2,16,1024]{2,1,0:T(8,128)S(1)} %maximum_select_fusion.1.shared, f32[2,16,1024]{2,1,0:T(8,128)S(1)} %broadcast_select_fusion.13.varied.bias, ...), custom_call_target="tpu_custom_call" | custom-call | flops 1000 | bytes 1000 | tf_op jit(solution)/shard_map/attention_backward_0/pallas_call | solution.py:682
  (472 shorter events, 191.5 us)
Async XLA Ops:
  11.5 16.0 %collective-permute-start.8 = (f32[2,16,1024]{2,1,0:T(8,128)}, f32[2,16,1024]{2,1,0:T(8,128)}, u32[]{:S(2)}, u32[]{:S(2)}) collective-permute-start(f32[2,16,1024]{2,1,0:T(8,128)} %maximum_select_fusion.2), channel_id=1, source_target_pairs={{0,2},{1,3},{2,0},{3,1},{16,18},{17,19},{18,16},{19,17},{4,6},{5,7... | collective-permute-start | bytes 393224 | tf_op jit(solution)/shard_map/ppermute | solution.py:346
  27.6 19.4 %collective-permute-start.11 = (bf16[2,1024,256]{2,1,0:T(8,128)(2,1)}, bf16[2,1024,256]{2,1,0:T(8,128)(2,1)S(1)}, u32[]{:S(2)}, u32[]{:S(2)}) collective-permute-start(bf16[2,1024,256]{2,1,0:T(8,128)(2,1)} %fusion.1), channel_id=1, source_target_pairs={{0,2},{1,3},{2,16},{3,17},{4,6},{5,7},{6,20},{7,21},{8,10},{9,11},... | collective-permute-start | bytes 3145736 | tf_op jit(solution)/shard_map/ppermute | solution.py:346
  42.8 29.2 %collective-permute-start.20 = (bf16[1024,1024]{1,0:T(8,128)(2,1)S(1)}, bf16[1024,1024]{1,0:T(8,128)(2,1)S(1)}, u32[]{:S(2)}, u32[]{:S(2)}) collective-permute-start(bf16[1024,1024]{1,0:T(8,128)(2,1)S(1)} %broadcast_select_fusion.1), channel_id=1, source_target_pairs={{0,2},{1,3},{2,16},{3,17},{4,6},{5,7},{6,20},{7,21},{8,10},{9,11},... | collective-permute-start | bytes 6291464 | tf_op jit(solution)/shard_map/ppermute | solution.py:346
  47.8 14.2 %collective-permute-start.13 = (bf16[256,1024]{1,0:T(8,128)(2,1)S(1)}, bf16[256,1024]{1,0:T(8,128)(2,1)S(1)}, u32[]{:S(2)}, u32[]{:S(2)}) collective-permute-start(bf16[256,1024]{1,0:T(8,128)(2,1)S(1)} %broadcast_select_fusion.5), channel_id=1, source_target_pairs={{0,1},{2,3},{17,16},{19,18},{4,5},{6,7},{21,20},{23,22},{8,9},{10,... | collective-permute-start | bytes 1572872 | tf_op jit(solution)/shard_map/ppermute | solution.py:346
  71.4 28.5 %collective-permute-start.18 = (bf16[1024,1024]{1,0:T(8,128)(2,1)S(1)}, bf16[1024,1024]{1,0:T(8,128)(2,1)S(1)}, u32[]{:S(2)}, u32[]{:S(2)}) collective-permute-start(bf16[1024,1024]{1,0:T(8,128)(2,1)S(1)} %bitcast.59), channel_id=1, source_target_pairs={{0,16},{1,17},{2,18},{3,19},{16,0},{17,1},{18,2},{19,3},{4,20},{5,... | collective-permute-start | bytes 6291464 | tf_op jit(solution)/shard_map/ppermute | solution.py:346
  71.9 28.1 %collective-permute-start.19 = (bf16[1024,1024]{1,0:T(8,128)(2,1)S(1)}, bf16[1024,1024]{1,0:T(8,128)(2,1)S(1)}, u32[]{:S(2)}, u32[]{:S(2)}) collective-permute-start(bf16[1024,1024]{1,0:T(8,128)(2,1)S(1)} %bitcast.67), channel_id=1, source_target_pairs={{0,16},{1,17},{2,18},{3,19},{16,0},{17,1},{18,2},{19,3},{4,20},{5,... | collective-permute-start | bytes 6291464 | tf_op jit(solution)/shard_map/ppermute | solution.py:346
  72.0 28.0 %collective-permute-start.21 = (bf16[1024,1024]{1,0:T(8,128)(2,1)S(1)}, bf16[1024,1024]{1,0:T(8,128)(2,1)S(1)}, u32[]{:S(2)}, u32[]{:S(2)}) collective-permute-start(bf16[1024,1024]{1,0:T(8,128)(2,1)S(1)} %collective-permute-done.20.rest_4_), channel_id=1, source_target_pairs={{2,6},{3,7},{6,2},{7,3},{10,14},{11,15},{14,10},{15,11},{16,20},{1... | collective-permute-start | bytes 6291464 | tf_op jit(solution)/shard_map/ppermute | solution.py:891
  75.6 16.0 %collective-permute-start.16 = (bf16[256,1024]{1,0:T(8,128)(2,1)S(1)}, bf16[256,1024]{1,0:T(8,128)(2,1)S(1)}, u32[]{:S(2)}, u32[]{:S(2)}) collective-permute-start(bf16[256,1024]{1,0:T(8,128)(2,1)S(1)} %add_convert_fusion.15.passed), channel_id=1, source_target_pairs={{0,1},{1,0},{2,3},{3,2},{16,17},{17,16},{18,19},{19,18},{4,5},{5,4... | collective-permute-start | bytes 1572872 | tf_op jit(solution)/shard_map/ppermute | solution.py:346
  93.5 16.6 %collective-permute-start.28 = (bf16[2,1024,256]{2,1,0:T(8,128)(2,1)S(1)}, bf16[2,1024,256]{2,1,0:T(8,128)(2,1)S(1)}, u32[]{:S(2)}, u32[]{:S(2)}) collective-permute-start(bf16[2,1024,256]{2,1,0:T(8,128)(2,1)S(1)} %broadcast_select_fusion.2), channel_id=1, source_target_pairs={{0,2},{1,3},{2,16},{3,17},{4,6},{5,7},{6,20},{7,21},{8,10},{9,11},... | collective-permute-start | bytes 3145736 | tf_op jit(solution)/shard_map/ppermute | solution.py:346
  111.2 14.1 %collective-permute-start.26 = (bf16[256,1024]{1,0:T(8,128)(2,1)S(1)}, bf16[256,1024]{1,0:T(8,128)(2,1)S(1)}, u32[]{:S(2)}, u32[]{:S(2)}) collective-permute-start(bf16[256,1024]{1,0:T(8,128)(2,1)S(1)} %add_convert_fusion.13.passed), channel_id=1, source_target_pairs={{0,1},{1,0},{2,3},{3,2},{16,17},{17,16},{18,19},{19,18},{4,5},{5,4... | collective-permute-start | bytes 1572872 | tf_op jit(solution)/shard_map/ppermute | solution.py:346
  113.3 35.8 %collective-permute-start.37 = (bf16[1024,1024]{1,0:T(8,128)(2,1)S(1)}, bf16[1024,1024]{1,0:T(8,128)(2,1)}, u32[]{:S(2)}, u32[]{:S(2)}) collective-permute-start(bf16[1024,1024]{1,0:T(8,128)(2,1)S(1)} %broadcast_select_fusion), channel_id=1, source_target_pairs={{0,2},{1,3},{2,16},{3,17},{4,6},{5,7},{6,20},{7,21},{8,10},{9,11},... | collective-permute-start | bytes 6291464 | tf_op jit(solution)/shard_map/ppermute | solution.py:346
  128.8 13.9 %collective-permute-start.32 = (bf16[256,1024]{1,0:T(8,128)(2,1)S(1)}, bf16[256,1024]{1,0:T(8,128)(2,1)S(1)}, u32[]{:S(2)}, u32[]{:S(2)}) collective-permute-start(bf16[256,1024]{1,0:T(8,128)(2,1)S(1)} %add_convert_fusion.12.passed), channel_id=1, source_target_pairs={{0,1},{1,0},{2,3},{3,2},{16,17},{17,16},{18,19},{19,18},{4,5},{5,4... | collective-permute-start | bytes 1572872 | tf_op jit(solution)/shard_map/ppermute | solution.py:346
  149.1 28.2 %collective-permute-start.38 = (bf16[1024,1024]{1,0:T(8,128)(2,1)}, bf16[1024,1024]{1,0:T(8,128)(2,1)}, u32[]{:S(2)}, u32[]{:S(2)}) collective-permute-start(bf16[1024,1024]{1,0:T(8,128)(2,1)} %collective-permute-done.37.rest_4_), channel_id=1, source_target_pairs={{2,6},{3,7},{6,2},{7,3},{10,14},{11,15},{14,10},{15,11},{16,20},{1... | collective-permute-start | bytes 6291464 | tf_op jit(solution)/shard_map/ppermute | solution.py:891
  152.1 15.3 %collective-permute-start.34 = (bf16[256,1024]{1,0:T(8,128)(2,1)S(1)}, bf16[256,1024]{1,0:T(8,128)(2,1)S(1)}, u32[]{:S(2)}, u32[]{:S(2)}) collective-permute-start(bf16[256,1024]{1,0:T(8,128)(2,1)S(1)} %add_convert_fusion.11.passed), channel_id=1, source_target_pairs={{0,1},{1,0},{2,3},{3,2},{16,17},{17,16},{18,19},{19,18},{4,5},{5,4... | collective-permute-start | bytes 1572872 | tf_op jit(solution)/shard_map/ppermute | solution.py:346
  175.6 14.4 %collective-permute-start.41 = (bf16[256,1024]{1,0:T(8,128)(2,1)S(1)}, bf16[256,1024]{1,0:T(8,128)(2,1)S(1)}, u32[]{:S(2)}, u32[]{:S(2)}) collective-permute-start(bf16[256,1024]{1,0:T(8,128)(2,1)S(1)} %add_convert_fusion.10.passed), channel_id=1, source_target_pairs={{0,1},{1,0},{2,3},{3,2},{16,17},{17,16},{18,19},{19,18},{4,5},{5,4... | collective-permute-start | bytes 1572872 | tf_op jit(solution)/shard_map/ppermute | solution.py:346
  192.1 14.0 %collective-permute-start.43 = (bf16[256,1024]{1,0:T(8,128)(2,1)S(1)}, bf16[256,1024]{1,0:T(8,128)(2,1)S(1)}, u32[]{:S(2)}, u32[]{:S(2)}) collective-permute-start(bf16[256,1024]{1,0:T(8,128)(2,1)S(1)} %add_convert_fusion.9.passed), channel_id=1, source_target_pairs={{0,1},{1,0},{2,3},{3,2},{16,17},{17,16},{18,19},{19,18},{4,5},{5,4... | collective-permute-start | bytes 1572872 | tf_op jit(solution)/shard_map/ppermute | solution.py:346
  208.2 14.0 %collective-permute-start.48 = (bf16[256,1024]{1,0:T(8,128)(2,1)S(1)}, bf16[256,1024]{1,0:T(8,128)(2,1)S(1)}, u32[]{:S(2)}, u32[]{:S(2)}) collective-permute-start(bf16[256,1024]{1,0:T(8,128)(2,1)S(1)} %add_convert_fusion.8.passed), channel_id=1, source_target_pairs={{0,1},{1,0},{2,3},{3,2},{16,17},{17,16},{18,19},{19,18},{4,5},{5,4... | collective-permute-start | bytes 1572872 | tf_op jit(solution)/shard_map/ppermute | solution.py:346
  225.2 13.9 %collective-permute-start.53 = (bf16[256,1024]{1,0:T(8,128)(2,1)S(1)}, bf16[256,1024]{1,0:T(8,128)(2,1)S(1)}, u32[]{:S(2)}, u32[]{:S(2)}) collective-permute-start(bf16[256,1024]{1,0:T(8,128)(2,1)S(1)} %add_convert_fusion.6.passed), channel_id=1, source_target_pairs={{1,0},{3,2},{16,17},{18,19},{5,4},{7,6},{20,21},{22,23},{9,8},{11,... | collective-permute-start | bytes 1572872 | tf_op jit(solution)/shard_map/ppermute | solution.py:346
  226.7 15.2 %collective-permute-start.51 = (bf16[256,1024]{1,0:T(8,128)(2,1)S(1)}, bf16[256,1024]{1,0:T(8,128)(2,1)S(1)}, u32[]{:S(2)}, u32[]{:S(2)}) collective-permute-start(bf16[256,1024]{1,0:T(8,128)(2,1)S(1)} %add_convert_fusion.7.passed), channel_id=1, source_target_pairs={{1,0},{3,2},{16,17},{18,19},{5,4},{7,6},{20,21},{22,23},{9,8},{11,... | collective-permute-start | bytes 1572872 | tf_op jit(solution)/shard_map/ppermute | solution.py:346
  244.0 14.0 %collective-permute-start.55 = (bf16[256,1024]{1,0:T(8,128)(2,1)S(1)}, bf16[256,1024]{1,0:T(8,128)(2,1)S(1)}, u32[]{:S(2)}, u32[]{:S(2)}) collective-permute-start(bf16[256,1024]{1,0:T(8,128)(2,1)S(1)} %add_convert_fusion.5.passed), channel_id=1, source_target_pairs={{0,1},{1,0},{2,3},{3,2},{16,17},{17,16},{18,19},{19,18},{4,5},{5,4... | collective-permute-start | bytes 1572872 | tf_op jit(solution)/shard_map/ppermute | solution.py:346
  270.9 15.8 %collective-permute-start.59 = (f32[256,1024]{1,0:T(8,128)S(1)}, f32[256,1024]{1,0:T(8,128)S(1)}, u32[]{:S(2)}, u32[]{:S(2)}) collective-permute-start(f32[256,1024]{1,0:T(8,128)S(1)} %broadcast_select_fusion.9), channel_id=1, source_target_pairs={{0,16},{2,18},{4,20},{6,22},{8,24},{10,26},{12,28},{14,30}} | collective-permute-start | bytes 3145736 | tf_op jit(solution)/shard_map/ppermute | solution.py:346
  289.3 13.9 %collective-permute-start.63 = (bf16[256,1024]{1,0:T(8,128)(2,1)S(1)}, bf16[256,1024]{1,0:T(8,128)(2,1)S(1)}, u32[]{:S(2)}, u32[]{:S(2)}) collective-permute-start(bf16[256,1024]{1,0:T(8,128)(2,1)S(1)} %add_convert_fusion.3.passed), channel_id=1, source_target_pairs={{0,1},{1,0},{2,3},{3,2},{16,17},{17,16},{18,19},{19,18},{4,5},{5,4... | collective-permute-start | bytes 1572872 | tf_op jit(solution)/shard_map/ppermute | solution.py:346
  305.4 14.0 %collective-permute-start.65 = (bf16[256,1024]{1,0:T(8,128)(2,1)S(1)}, bf16[256,1024]{1,0:T(8,128)(2,1)S(1)}, u32[]{:S(2)}, u32[]{:S(2)}) collective-permute-start(bf16[256,1024]{1,0:T(8,128)(2,1)S(1)} %add_convert_fusion.2.passed), channel_id=1, source_target_pairs={{0,1},{1,0},{2,3},{3,2},{16,17},{17,16},{18,19},{19,18},{4,5},{5,4... | collective-permute-start | bytes 1572872 | tf_op jit(solution)/shard_map/ppermute | solution.py:346
  351.7 14.3 %collective-permute-start.74 = (f32[256,1024]{1,0:T(8,128)S(1)}, f32[256,1024]{1,0:T(8,128)}, u32[]{:S(2)}, u32[]{:S(2)}) collective-permute-start(f32[256,1024]{1,0:T(8,128)S(1)} %broadcast_select_fusion.7), channel_id=1, source_target_pairs={{17,1},{19,3},{21,5},{23,7},{25,9},{27,11},{29,13},{31,15}} | collective-permute-start | bytes 3145736 | tf_op jit(solution)/shard_map/ppermute | solution.py:346
  (176 other events, 1813.4 us)

commit v4 on v3

--- a/solution.py
+++ b/solution.py
@@ -578,9 +578,18 @@
 
 
 def attend_back_kernel(layer, chunk, meta, shared, varied, n_own, n_near, g_own, g_near, *rest):
-    q_ref, lse_ref, mixed_ref = rest[:3]
-    keys, values = rest[3 : 4 + chunk], rest[4 + chunk : 5 + 2 * chunk]
-    rest = rest[5 + 2 * chunk :]
+    n_saved = 5 + 2 * chunk
+    saved, rest = rest[:n_saved], rest[n_saved:]
+    saved_sems, rest = rest[-1], rest[:-1]
+    bufs, rest = rest[-n_saved:], rest[:-n_saved]
+    fetches = [
+        pltpu.make_async_copy(source, target, saved_sems.at[i])
+        for i, (source, target) in enumerate(zip(saved, bufs))
+    ]
+    for fetch in fetches:
+        fetch.start()
+    q_ref, lse_ref, mixed_ref = bufs[:3]
+    keys, values = bufs[3 : 4 + chunk], bufs[4 + chunk :]
     if chunk == 0:
         dk_in, dv_in, down_in, up_in = rest[:4]
         keep, give, down_ref, up_ref = rest[8:12]
@@ -594,6 +603,8 @@
     loaded = load_qkv_weight(layer, meta, weight, w_buf, sem)
     lay_out(meta, g_own, g_near, g_buf)
     lay_out(meta, n_own, n_near, n_buf)
+    for fetch in fetches:
+        fetch.wait()
     for j in range(2 + 2 * chunk):
         rows = slice((j % 2) * BLOCK, (j % 2 + 1) * BLOCK)
         kt_buf[:, j * BLOCK : (j + 1) * BLOCK] = keys[j // 2][rows, :].T
@@ -678,10 +689,12 @@
     q, _, _, lse, mixed = saved[chunk]
     keys = [one[1] for one in saved[: chunk + 1]]
     values = [one[2] for one in saved[: chunk + 1]]
-    inputs = (shared, varied, *blocks, *grads, q, lse, mixed, *keys, *values, *carried)
+    held = (q, lse, mixed, *keys, *values)
+    inputs = (shared, varied, *blocks, *grads, *held, *carried)
     return pl.pallas_call(
         functools.partial(attend_back_kernel, layer, chunk),
-        in_specs=[SMEM_SPACE] + [VMEM_SPACE] * len(inputs) + [HBM_SPACE] * 4,
+        in_specs=[SMEM_SPACE] + [VMEM_SPACE] * 6 + [HBM_SPACE] * len(held)
+        + [VMEM_SPACE] * len(carried) + [HBM_SPACE] * 4,
         out_specs=[VMEM_SPACE] * (4 + 2 * chunk),
         out_shape=[piece, piece, jax.ShapeDtypeStruct((LOW, 1024), f32),
                    jax.ShapeDtypeStruct((LOW, 512), f32)] + [tall] * (2 * chunk),
@@ -697,6 +710,8 @@
             pltpu.VMEM((spans, 256), f32),
             pltpu.VMEM((CHUNK, 256), bf),
             pltpu.SemaphoreType.DMA,
+            *[pltpu.VMEM(one.shape, one.dtype) for one in held],
+            pltpu.SemaphoreType.DMA((len(held),)),
         ],
         compiler_params=kernel_params(24),
         cost_estimate=cost(6e9, 12e6),
@@ -1046,6 +1061,7 @@
     middle01, n1 = middle(0, row1, sum1)
     keep, give, slope1 = units(0, n1, weights_b0)
     sum3 = chip_sum(keep, give, sum2[1])
+    sum2, trail_a1 = lax.optimization_barrier((sum2, trail_a1))
     weights_a1 = (own_a, other_a, lead_a1, trail_a1)
     between0, n10 = small(rows_next_kernel, middle00, *sum2, shared, outs=[thin, thin], name="rows_next")
     saved10, keep, give = attend(1, 0, n10, (), weights_a1)
@@ -1086,18 +1102,10 @@
     )
     sum9 = chip_sum(keep, give, sum8[1])
     before1 = small(
-        rows_before_kernel, grad_middle11, *sum8, between1, shared, outs=[thin], name="rows_before"
+        rows_before_kernel, grad_middle11, *after(sum8, keep), between1, shared, outs=[thin], name="rows_before"
     )[0]
     keep, give = units_back(0, before1, slope1, weights_b0)
     sum10 = chip_sum(keep, give, sum9[1])
-    outs = [
-        small(rows_output_kernel, one, *after(two, keep), shared, outs=[sheet, thin],
-              name="rows_output")
-        for one, two in zip((middle10, middle11), out_sums)
-    ]
-    out_wide = jnp.where(upper, outs[0][0], outs[1][0])
-    out_same, out_cross = collect(1, out_wide, jnp.where(upper, outs[1][1], outs[0][1]))
-    sum9, out_same, out_cross = lax.optimization_barrier((sum9, out_same, out_cross))
     before0 = small(
         rows_before_kernel, grad_middle10, *sum9, between0, shared, outs=[thin], name="rows_before"
     )[0]
@@ -1115,6 +1123,13 @@
         (dk, dv, down0, up0), shared, near_varied, weights_a0,
     )
     sum13 = chip_sum(keep, give, sum12[1], from_x)
+    outs = [
+        small(rows_output_kernel, one, *after(two, sum13[0]), shared, outs=[sheet, thin],
+              name="rows_output")
+        for one, two in zip((middle10, middle11), out_sums)
+    ]
+    out_wide = jnp.where(upper, outs[0][0], outs[1][0])
+    out_same, out_cross = collect(1, out_wide, jnp.where(upper, outs[1][1], outs[0][1]))
     totals = total_over_z((down0, down1), after((up0, up1), sum13[0]))
     sum13, totals = lax.optimization_barrier((sum13, totals))
     ends = [

time: 377 us -> 368 us (0.976)
  waiting for transfers between devices: 113 us -> 99.8 us
  starting transfers between devices: 111 us -> 107 us
    ppermute x73, waiting for transfers between devices: 109 us -> 98.4 us  [send(): return lax.ppermute(block, ('section', 'tensor'), pairs)]
    unnamed x244 -> x264, local copies, waits for them, and re-layouts: 16.3 us -> 19.2 us
  transfers between devices with their start and end apart: 79 -> 79, of which waited for: 36 -> 38; matrix products, arithmetic and copies ran while one was open for 4% -> 4% of each run, Pallas kernels for 29% -> 30%
where the time goes in v4:
time: 368 us; the launch traced here: 360 us
  Pallas kernels  109 us (30%)
  starting transfers between devices  107 us (29%)
  waiting for transfers between devices  99.8 us (27%)
  local copies, waits for them, and re-layouts  23.2 us (6%)
  other arithmetic  18.8 us (5%)
    ppermute x73, starting transfers between devices, send(): return lax.ppermute(block, ('section', 'tensor'), pairs)  98.6 us
    ppermute x73, waiting for transfers between devices, send(): return lax.ppermute(block, ('section', 'tensor'), pairs)  98.4 us
    pallas_call x4, Pallas kernels, attend_back_call(): pl.pallas_call(functools.partial(attend_back_kernel, layer, chunk), in_sp...  37.6 us
    pallas_call x4, Pallas kernels, attend_call(): pl.pallas_call(functools.partial(attend_kernel, layer, chunk), in_specs=[...  31.3 us
    pallas_call x6, Pallas kernels, units_call(): pl.pallas_call(kernel, in_specs=[SMEM_SPACE] + [VMEM_SPACE] * len(small)...  28 us
    unnamed x264, local copies, waits for them, and re-layouts  19.2 us
    pallas_call x17, Pallas kernels, plain_call(): pl.pallas_call(kernel, in_specs=specs, out_specs=[VMEM_SPACE] * len(outs)...  11.8 us
  transfers between devices with their start and end apart: 79, of which 38 were waited for; matrix products, arithmetic and copies ran while one was open for 4% of the time, Pallas kernels for 30%

profile of v4, /device:TPU:0, one launch (start us, length us, event | category | flops | bytes accessed | tf_op | source)
XLA Modules:
  0.0 360.4 jit_solution(14227080844682234198)
XLA Ops:
  13.2 4.9 %collective-permute-done.1.crossed = bf16[256,1024]{1,0:T(8,128)(2,1)S(1)} collective-permute-done((bf16[256,1024]{1,0:T(8,128)(2,1)}, bf16[256,1024]{1,0:T(8,128)(2,1)S(1)}, u32[]{:S(2)}, u32[]{:S(2)}) %collective-permute-start.1) | collective-permute-done | bytes 524320 | tf_op jit(solution)/shard_map/ppermute | solution.py:346
  42.7 4.9 %collective-permute-start.20 = (bf16[1024,1024]{1,0:T(8,128)(2,1)S(1)}, bf16[1024,1024]{1,0:T(8,128)(2,1)S(1)}, u32[]{:S(2)}, u32[]{:S(2)}) collective-permute-start(bf16[1024,1024]{1,0:T(8,128)(2,1)S(1)} %broadcast_select_fusion.1), channel_id=1, source_target_pairs={{0,2},{1,3},{2,16},{3,17},{4,6},{5,7},{6,20},{7,21},{8,10},{9,11},... | collective-permute-start | bytes 6291464 | tf_op jit(solution)/shard_map/ppermute | solution.py:346
  48.4 7.4 %collective-permute-start.13 = (bf16[256,1024]{1,0:T(8,128)(2,1)S(1)}, bf16[256,1024]{1,0:T(8,128)(2,1)S(1)}, u32[]{:S(2)}, u32[]{:S(2)}) collective-permute-start(bf16[256,1024]{1,0:T(8,128)(2,1)S(1)} %broadcast_select_fusion.5), channel_id=1, source_target_pairs={{0,1},{2,3},{17,16},{19,18},{4,5},{6,7},{21,20},{23,22},{8,9},{10,... | collective-permute-start | bytes 1572872 | tf_op jit(solution)/shard_map/ppermute | solution.py:346
  57.9 6.5 %attention_forward_0.2 = (bf16[512,256]{1,0:T(8,128)(2,1)S(1)}, bf16[512,256]{1,0:T(8,128)(2,1)S(1)}, bf16[512,256]{1,0:T(8,128)(2,1)S(1)}, f32[8,512]{1,0:T(8,1...) custom-call(s32[9]{0:T(128)S(1)} %concatenate.41.meta, ...), custom_call_target="tpu_custom_call" | custom-call | flops 1000 | bytes 1000 | tf_op jit(solution)/shard_map/attention_forward_0/pallas_call | solution.py:554
  80.6 8.6 %attention_forward_1.2 = (bf16[512,256]{1,0:T(8,128)(2,1)S(1)}, bf16[512,256]{1,0:T(8,128)(2,1)S(1)}, bf16[512,256]{1,0:T(8,128)(2,1)S(1)}, f32[8,512]{1,0:T(8,1...) custom-call(s32[9]{0:T(128)S(1)} %concatenate.41.meta, ...), custom_call_target="tpu_custom_call" | custom-call | flops 1000 | bytes 1000 | tf_op jit(solution)/shard_map/attention_forward_1/pallas_call | solution.py:554
  94.7 5.6 %collective-permute-start.27 = (bf16[2,1024,256]{2,1,0:T(8,128)(2,1)S(1)}, bf16[2,1024,256]{2,1,0:T(8,128)(2,1)S(1)}, u32[]{:S(2)}, u32[]{:S(2)}) collective-permute-start(bf16[2,1024,256]{2,1,0:T(8,128)(2,1)S(1)} %broadcast_select_fusion.2), channel_id=1, source_target_pairs={{0,2},{1,3},{2,16},{3,17},{4,6},{5,7},{6,20},{7,21},{8,10},{9,11},... | collective-permute-start | bytes 3145736 | tf_op jit(solution)/shard_map/ppermute | solution.py:346
  116.4 7.1 %collective-permute-start.37 = (bf16[1024,1024]{1,0:T(8,128)(2,1)S(1)}, bf16[1024,1024]{1,0:T(8,128)(2,1)}, u32[]{:S(2)}, u32[]{:S(2)}) collective-permute-start(bf16[1024,1024]{1,0:T(8,128)(2,1)S(1)} %broadcast_select_fusion), channel_id=1, source_target_pairs={{0,2},{1,3},{2,16},{3,17},{4,6},{5,7},{6,20},{7,21},{8,10},{9,11},... | collective-permute-start | bytes 6291464 | tf_op jit(solution)/shard_map/ppermute | solution.py:346
  123.6 4.9 %units.3 = (bf16[256,1024]{1,0:T(8,128)(2,1)S(1)}, bf16[256,1024]{1,0:T(8,128)(2,1)S(1)}, bf16[512,1024]{1,0:T(8,128)(2,1)S(1)}) custom-call(s32[9]{0:T(128)S(1)} %concatenate.41.meta, bf16[256,1024]{1,0:T(8,128)(2,1)S(1)} %get-tuple-element.216.n0, bf16[256,1024]{1,0:T(8,128)(2,1)S(1)} %collective-permute-done.30.n1, ...), custom_call_target="tpu_custom_call" | custom-call | flops 1000 | bytes 1000 | tf_op jit(solution)/shard_map/units/pallas_call | solution.py:854
  132.6 6.5 %attention_forward_0.3 = (bf16[512,256]{1,0:T(8,128)(2,1)S(1)}, bf16[512,256]{1,0:T(8,128)(2,1)S(1)}, bf16[512,256]{1,0:T(8,128)(2,1)S(1)}, f32[8,512]{1,0:T(8,1...) custom-call(s32[9]{0:T(128)S(1)} %concatenate.41.meta, ...), custom_call_target="tpu_custom_call" | custom-call | flops 1000 | bytes 1000 | tf_op jit(solution)/shard_map/attention_forward_0/pallas_call | solution.py:554
  139.9 5.1 %collective-permute-done.32.far = bf16[256,1024]{1,0:T(8,128)(2,1)S(1)} collective-permute-done((bf16[256,1024]{1,0:T(8,128)(2,1)S(1)}, bf16[256,1024]{1,0:T(8,128)(2,1)S(1)}, u32[]{:S(2)}, u32[]{:S(2)}) %collective-permute-start.32) | collective-permute-done | bytes 524320 | tf_op jit(solution)/shard_map/ppermute | solution.py:346
  150.3 9.7 %attention_forward_1.3 = (bf16[512,256]{1,0:T(8,128)(2,1)S(1)}, bf16[512,256]{1,0:T(8,128)(2,1)S(1)}, bf16[512,256]{1,0:T(8,128)(2,1)S(1)}, f32[8,512]{1,0:T(8,1...) custom-call(s32[9]{0:T(128)S(1)} %concatenate.41.meta, ...), custom_call_target="tpu_custom_call" | custom-call | flops 1000 | bytes 1000 | tf_op jit(solution)/shard_map/attention_forward_1/pallas_call | solution.py:554
  175.3 5.6 %units_turn.2 = (bf16[256,1024]{1,0:T(8,128)(2,1)S(1)}, bf16[256,1024]{1,0:T(8,128)(2,1)S(1)}, bf16[256,1024]{1,0:T(8,128)(2,1)S(1)}, bf16[256,1024]{1,0:T(8,128)(2,1)S(1)}) custom-call(s32[9]{0:T(128)S(1)} %concatenate.41.meta, bf16[256,1024]{1,0:T(8,128)(2,1)S(1)} %get-tuple-element.226.n0, bf16[256,1024]{1,0:T(8,128)(2,1)S(1)} %collective-permute-done.35.n1, ...), custom_call_target="tpu_custom_call" | custom-call | flops 1000 | bytes 1000 | tf_op jit(solution)/shard_map/units_turn/pallas_call | solution.py:854
  180.9 5.4 %collective-permute-done.41.far = bf16[256,1024]{1,0:T(8,128)(2,1)S(1)} collective-permute-done((bf16[256,1024]{1,0:T(8,128)(2,1)S(1)}, bf16[256,1024]{1,0:T(8,128)(2,1)S(1)}, u32[]{:S(2)}, u32[]{:S(2)}) %collective-permute-start.41) | collective-permute-done | bytes 524320 | tf_op jit(solution)/shard_map/ppermute | solution.py:346
  190.0 5.8 %units_turn.3 = (bf16[256,1024]{1,0:T(8,128)(2,1)S(1)}, bf16[256,1024]{1,0:T(8,128)(2,1)S(1)}, bf16[256,1024]{1,0:T(8,128)(2,1)S(1)}, bf16[256,1024]{1,0:T(8,128)(2,1)S(1)}) custom-call(s32[9]{0:T(128)S(1)} %concatenate.41.meta, bf16[256,1024]{1,0:T(8,128)(2,1)S(1)} %get-tuple-element.249.n0, bf16[256,1024]{1,0:T(8,128)(2,1)S(1)} %collective-permute-done.45.n1, ...), custom_call_target="tpu_custom_call" | custom-call | flops 1000 | bytes 1000 | tf_op jit(solution)/shard_map/units_turn/pallas_call | solution.py:854
  195.8 6.7 %collective-permute-done.43.far = bf16[256,1024]{1,0:T(8,128)(2,1)S(1)} collective-permute-done((bf16[256,1024]{1,0:T(8,128)(2,1)S(1)}, bf16[256,1024]{1,0:T(8,128)(2,1)S(1)}, u32[]{:S(2)}, u32[]{:S(2)}) %collective-permute-start.43) | collective-permute-done | bytes 524320 | tf_op jit(solution)/shard_map/ppermute | solution.py:346
  206.2 12.4 %collective-permute-done.48.far = bf16[256,1024]{1,0:T(8,128)(2,1)S(1)} collective-permute-done((bf16[256,1024]{1,0:T(8,128)(2,1)S(1)}, bf16[256,1024]{1,0:T(8,128)(2,1)S(1)}, u32[]{:S(2)}, u32[]{:S(2)}) %collective-permute-start.48) | collective-permute-done | bytes 524320 | tf_op jit(solution)/shard_map/ppermute | solution.py:346
  224.6 11.0 %attention_backward_1.2 = (bf16[256,1024]{1,0:T(8,128)(2,1)S(1)}, bf16[256,1024]{1,0:T(8,128)(2,1)S(1)}, f32[8,1024]{1,0:T(8,128)S(1)}, f32[8,512]{1,0:T(8,128)S...) custom-call(s32[9]{0:T(128)S(1)} %concatenate.41.meta, f32[2,16,1024]{2,1,0:T(8,128)S(1)} %maximum_select_fusion.1.shared, ...), custom_call_target="tpu_custom_call" | custom-call | flops 1000 | bytes 1000 | tf_op jit(solution)/shard_map/attention_backward_1/pallas_call | solution.py:694
  241.2 7.4 %attention_backward_0.2 = (bf16[256,1024]{1,0:T(8,128)(2,1)S(1)}, bf16[256,1024]{1,0:T(8,128)(2,1)S(1)}, f32[8,1024]{1,0:T(8,128)S(1)}, f32[8,512]{1,0:T(8,128)S(1)}) custom-call(s32[9]{0:T(128)S(1)} %concatenate.41.meta, f32[2,16,1024]{2,1,0:T(8,128)S(1)} %maximum_select_fusion.1.shared, f32[2,16,1024]{2,1,0:T(8,128)S(1)} %broadcast_select_fusion.13.varied.bias, ...), custom_call_target="tpu_custom_call" | custom-call | flops 1000 | bytes 1000 | tf_op jit(solution)/shard_map/attention_backward_0/pallas_call | solution.py:694
  248.7 5.8 %collective-permute-done.55.far = bf16[256,1024]{1,0:T(8,128)(2,1)S(1)} collective-permute-done((bf16[256,1024]{1,0:T(8,128)(2,1)S(1)}, bf16[256,1024]{1,0:T(8,128)(2,1)S(1)}, u32[]{:S(2)}, u32[]{:S(2)}) %collective-permute-start.55) | collective-permute-done | bytes 524320 | tf_op jit(solution)/shard_map/ppermute | solution.py:346
  261.0 9.6 %collective-permute-done.57.far = bf16[256,1024]{1,0:T(8,128)(2,1)S(1)} collective-permute-done((bf16[256,1024]{1,0:T(8,128)(2,1)S(1)}, bf16[256,1024]{1,0:T(8,128)(2,1)S(1)}, u32[]{:S(2)}, u32[]{:S(2)}) %collective-permute-start.57) | collective-permute-done | bytes 524320 | tf_op jit(solution)/shard_map/ppermute | solution.py:346
  277.1 9.6 %collective-permute-done.61.far = bf16[256,1024]{1,0:T(8,128)(2,1)S(1)} collective-permute-done((bf16[256,1024]{1,0:T(8,128)(2,1)S(1)}, bf16[256,1024]{1,0:T(8,128)(2,1)S(1)}, u32[]{:S(2)}, u32[]{:S(2)}) %collective-permute-start.61) | collective-permute-done | bytes 524320 | tf_op jit(solution)/shard_map/ppermute | solution.py:346
  289.8 11.2 %attention_backward_1.3 = (bf16[256,1024]{1,0:T(8,128)(2,1)S(1)}, bf16[256,1024]{1,0:T(8,128)(2,1)S(1)}, f32[8,1024]{1,0:T(8,128)S(1)}, f32[8,512]{1,0:T(8,128)S...) custom-call(s32[9]{0:T(128)S(1)} %concatenate.41.meta, f32[2,16,1024]{2,1,0:T(8,128)S(1)} %maximum_select_fusion.1.shared, ...), custom_call_target="tpu_custom_call" | custom-call | flops 1000 | bytes 1000 | tf_op jit(solution)/shard_map/attention_backward_1/pallas_call | solution.py:694
  306.6 7.9 %attention_backward_0.3 = (bf16[256,1024]{1,0:T(8,128)(2,1)S(1)}, bf16[256,1024]{1,0:T(8,128)(2,1)}, f32[8,1024]{1,0:T(8,128)S(1)}, f32[8,512]{1,0:T(8,128)S(1)}) custom-call(s32[9]{0:T(128)S(1)} %concatenate.41.meta, f32[2,16,1024]{2,1,0:T(8,128)S(1)} %maximum_select_fusion.1.shared, f32[2,16,1024]{2,1,0:T(8,128)S(1)} %broadcast_select_fusion.13.varied.bias, ...), custom_call_target="tpu_custom_call" | custom-call | flops 1000 | bytes 1000 | tf_op jit(solution)/shard_map/attention_backward_0/pallas_call | solution.py:694
  327.7 7.9 %collective-permute-start.75 = (bf16[256,1024]{1,0:T(8,128)(2,1)}, bf16[256,1024]{1,0:T(8,128)(2,1)}, u32[]{:S(2)}, u32[]{:S(2)}) collective-permute-start(bf16[256,1024]{1,0:T(8,128)(2,1)} %broadcast_select_fusion.6), channel_id=1, source_target_pairs={{0,18},{2,16},{17,19},{19,17},{4,22},{6,20},{21,23},{23,21},{8,26}... | collective-permute-start | bytes 1572872 | tf_op jit(solution)/shard_map/ppermute | solution.py:346
  (492 shorter events, 179.5 us)
Async XLA Ops:
  11.5 15.9 %collective-permute-start.8 = (f32[2,16,1024]{2,1,0:T(8,128)}, f32[2,16,1024]{2,1,0:T(8,128)}, u32[]{:S(2)}, u32[]{:S(2)}) collective-permute-start(f32[2,16,1024]{2,1,0:T(8,128)} %maximum_select_fusion.2), channel_id=1, source_target_pairs={{0,2},{1,3},{2,0},{3,1},{16,18},{17,19},{18,16},{19,17},{4,6},{5,7... | collective-permute-start | bytes 393224 | tf_op jit(solution)/shard_map/ppermute | solution.py:346
  27.5 20.1 %collective-permute-start.11 = (bf16[2,1024,256]{2,1,0:T(8,128)(2,1)}, bf16[2,1024,256]{2,1,0:T(8,128)(2,1)S(1)}, u32[]{:S(2)}, u32[]{:S(2)}) collective-permute-start(bf16[2,1024,256]{2,1,0:T(8,128)(2,1)} %fusion.1), channel_id=1, source_target_pairs={{0,2},{1,3},{2,16},{3,17},{4,6},{5,7},{6,20},{7,21},{8,10},{9,11},... | collective-permute-start | bytes 3145736 | tf_op jit(solution)/shard_map/ppermute | solution.py:346
  41.2 16.7 %collective-permute-start.10 = (bf16[4,1024,256]{2,1,0:T(8,128)(2,1)S(1)}, bf16[4,1024,256]{2,1,0:T(8,128)(2,1)S(1)}, u32[]{:S(2)}, u32[]{:S(2)}) collective-permute-start(bf16[4,1024,256]{2,1,0:T(8,128)(2,1)S(1)} %pad_maximum_fusion.rest_0_.rest_2_.rest_7_.rest_9_), channel_id=1, source_target_pairs={{0,16},{1,17},{2,18},{3,19},{16,0},{17,1},{18,2},{19,3},{4,20},{5,... | collective-permute-start | bytes 6291464 | tf_op jit(solution)/shard_map/ppermute | solution.py:346
  42.7 30.3 %collective-permute-start.20 = (bf16[1024,1024]{1,0:T(8,128)(2,1)S(1)}, bf16[1024,1024]{1,0:T(8,128)(2,1)S(1)}, u32[]{:S(2)}, u32[]{:S(2)}) collective-permute-start(bf16[1024,1024]{1,0:T(8,128)(2,1)S(1)} %broadcast_select_fusion.1), channel_id=1, source_target_pairs={{0,2},{1,3},{2,16},{3,17},{4,6},{5,7},{6,20},{7,21},{8,10},{9,11},... | collective-permute-start | bytes 6291464 | tf_op jit(solution)/shard_map/ppermute | solution.py:346
  48.4 16.8 %collective-permute-start.13 = (bf16[256,1024]{1,0:T(8,128)(2,1)S(1)}, bf16[256,1024]{1,0:T(8,128)(2,1)S(1)}, u32[]{:S(2)}, u32[]{:S(2)}) collective-permute-start(bf16[256,1024]{1,0:T(8,128)(2,1)S(1)} %broadcast_select_fusion.5), channel_id=1, source_target_pairs={{0,1},{2,3},{17,16},{19,18},{4,5},{6,7},{21,20},{23,22},{8,9},{10,... | collective-permute-start | bytes 1572872 | tf_op jit(solution)/shard_map/ppermute | solution.py:346
  72.4 29.9 %collective-permute-start.18 = (bf16[1024,1024]{1,0:T(8,128)(2,1)S(1)}, bf16[1024,1024]{1,0:T(8,128)(2,1)S(1)}, u32[]{:S(2)}, u32[]{:S(2)}) collective-permute-start(bf16[1024,1024]{1,0:T(8,128)(2,1)S(1)} %bitcast.59), channel_id=1, source_target_pairs={{0,16},{1,17},{2,18},{3,19},{16,0},{17,1},{18,2},{19,3},{4,20},{5,... | collective-permute-start | bytes 6291464 | tf_op jit(solution)/shard_map/ppermute | solution.py:346
  72.9 29.5 %collective-permute-start.19 = (bf16[1024,1024]{1,0:T(8,128)(2,1)S(1)}, bf16[1024,1024]{1,0:T(8,128)(2,1)S(1)}, u32[]{:S(2)}, u32[]{:S(2)}) collective-permute-start(bf16[1024,1024]{1,0:T(8,128)(2,1)S(1)} %bitcast.67), channel_id=1, source_target_pairs={{0,16},{1,17},{2,18},{3,19},{16,0},{17,1},{18,2},{19,3},{4,20},{5,... | collective-permute-start | bytes 6291464 | tf_op jit(solution)/shard_map/ppermute | solution.py:346
  73.0 29.3 %collective-permute-start.21 = (bf16[1024,1024]{1,0:T(8,128)(2,1)S(1)}, bf16[1024,1024]{1,0:T(8,128)(2,1)S(1)}, u32[]{:S(2)}, u32[]{:S(2)}) collective-permute-start(bf16[1024,1024]{1,0:T(8,128)(2,1)S(1)} %collective-permute-done.20.rest_4_), channel_id=1, source_target_pairs={{2,6},{3,7},{6,2},{7,3},{10,14},{11,15},{14,10},{15,11},{16,20},{1... | collective-permute-start | bytes 6291464 | tf_op jit(solution)/shard_map/ppermute | solution.py:906
  76.6 16.1 %collective-permute-start.16 = (bf16[256,1024]{1,0:T(8,128)(2,1)S(1)}, bf16[256,1024]{1,0:T(8,128)(2,1)S(1)}, u32[]{:S(2)}, u32[]{:S(2)}) collective-permute-start(bf16[256,1024]{1,0:T(8,128)(2,1)S(1)} %add_convert_fusion.15.passed), channel_id=1, source_target_pairs={{0,1},{1,0},{2,3},{3,2},{16,17},{17,16},{18,19},{19,18},{4,5},{5,4... | collective-permute-start | bytes 1572872 | tf_op jit(solution)/shard_map/ppermute | solution.py:346
  94.7 17.9 %collective-permute-start.27 = (bf16[2,1024,256]{2,1,0:T(8,128)(2,1)S(1)}, bf16[2,1024,256]{2,1,0:T(8,128)(2,1)S(1)}, u32[]{:S(2)}, u32[]{:S(2)}) collective-permute-start(bf16[2,1024,256]{2,1,0:T(8,128)(2,1)S(1)} %broadcast_select_fusion.2), channel_id=1, source_target_pairs={{0,2},{1,3},{2,16},{3,17},{4,6},{5,7},{6,20},{7,21},{8,10},{9,11},... | collective-permute-start | bytes 3145736 | tf_op jit(solution)/shard_map/ppermute | solution.py:346
  113.4 15.6 %collective-permute-start.28 = (bf16[2,1024,256]{2,1,0:T(8,128)(2,1)S(1)}, bf16[2,1024,256]{2,1,0:T(8,128)(2,1)S(1)}, u32[]{:S(2)}, u32[]{:S(2)}) collective-permute-start(bf16[2,1024,256]{2,1,0:T(8,128)(2,1)S(1)} %collective-permute-done.27.rest_2_.rest_4_.rest_9_.rest_11_), channel_id=1, source_target_pairs={{2,6},{3,7},{6,2},{7,3},{10,14},{11,15},{14,10},{15,11},{16,20},{1... | collective-permute-start | bytes 3145736 | tf_op jit(solution)/shard_map/ppermute | solution.py:906
  114.4 14.3 %collective-permute-start.26 = (bf16[256,1024]{1,0:T(8,128)(2,1)S(1)}, bf16[256,1024]{1,0:T(8,128)(2,1)S(1)}, u32[]{:S(2)}, u32[]{:S(2)}) collective-permute-start(bf16[256,1024]{1,0:T(8,128)(2,1)S(1)} %add_convert_fusion.13.passed), channel_id=1, source_target_pairs={{0,1},{1,0},{2,3},{3,2},{16,17},{17,16},{18,19},{19,18},{4,5},{5,4... | collective-permute-start | bytes 1572872 | tf_op jit(solution)/shard_map/ppermute | solution.py:346
  116.4 29.3 %collective-permute-start.37 = (bf16[1024,1024]{1,0:T(8,128)(2,1)S(1)}, bf16[1024,1024]{1,0:T(8,128)(2,1)}, u32[]{:S(2)}, u32[]{:S(2)}) collective-permute-start(bf16[1024,1024]{1,0:T(8,128)(2,1)S(1)} %broadcast_select_fusion), channel_id=1, source_target_pairs={{0,2},{1,3},{2,16},{3,17},{4,6},{5,7},{6,20},{7,21},{8,10},{9,11},... | collective-permute-start | bytes 6291464 | tf_op jit(solution)/shard_map/ppermute | solution.py:346
  130.8 14.3 %collective-permute-start.32 = (bf16[256,1024]{1,0:T(8,128)(2,1)S(1)}, bf16[256,1024]{1,0:T(8,128)(2,1)S(1)}, u32[]{:S(2)}, u32[]{:S(2)}) collective-permute-start(bf16[256,1024]{1,0:T(8,128)(2,1)S(1)} %add_convert_fusion.12.passed), channel_id=1, source_target_pairs={{0,1},{1,0},{2,3},{3,2},{16,17},{17,16},{18,19},{19,18},{4,5},{5,4... | collective-permute-start | bytes 1572872 | tf_op jit(solution)/shard_map/ppermute | solution.py:346
  146.8 27.0 %collective-permute-start.38 = (bf16[1024,1024]{1,0:T(8,128)(2,1)}, bf16[1024,1024]{1,0:T(8,128)(2,1)}, u32[]{:S(2)}, u32[]{:S(2)}) collective-permute-start(bf16[1024,1024]{1,0:T(8,128)(2,1)} %collective-permute-done.37.rest_4_), channel_id=1, source_target_pairs={{2,6},{3,7},{6,2},{7,3},{10,14},{11,15},{14,10},{15,11},{16,20},{1... | collective-permute-start | bytes 6291464 | tf_op jit(solution)/shard_map/ppermute | solution.py:906
  148.9 14.7 %collective-permute-start.34 = (bf16[256,1024]{1,0:T(8,128)(2,1)S(1)}, bf16[256,1024]{1,0:T(8,128)(2,1)S(1)}, u32[]{:S(2)}, u32[]{:S(2)}) collective-permute-start(bf16[256,1024]{1,0:T(8,128)(2,1)S(1)} %add_convert_fusion.11.passed), channel_id=1, source_target_pairs={{0,1},{1,0},{2,3},{3,2},{16,17},{17,16},{18,19},{19,18},{4,5},{5,4... | collective-permute-start | bytes 1572872 | tf_op jit(solution)/shard_map/ppermute | solution.py:346
  172.2 14.1 %collective-permute-start.41 = (bf16[256,1024]{1,0:T(8,128)(2,1)S(1)}, bf16[256,1024]{1,0:T(8,128)(2,1)S(1)}, u32[]{:S(2)}, u32[]{:S(2)}) collective-permute-start(bf16[256,1024]{1,0:T(8,128)(2,1)S(1)} %add_convert_fusion.10.passed), channel_id=1, source_target_pairs={{0,1},{1,0},{2,3},{3,2},{16,17},{17,16},{18,19},{19,18},{4,5},{5,4... | collective-permute-start | bytes 1572872 | tf_op jit(solution)/shard_map/ppermute | solution.py:346
  188.4 14.0 %collective-permute-start.43 = (bf16[256,1024]{1,0:T(8,128)(2,1)S(1)}, bf16[256,1024]{1,0:T(8,128)(2,1)S(1)}, u32[]{:S(2)}, u32[]{:S(2)}) collective-permute-start(bf16[256,1024]{1,0:T(8,128)(2,1)S(1)} %add_convert_fusion.9.passed), channel_id=1, source_target_pairs={{0,1},{1,0},{2,3},{3,2},{16,17},{17,16},{18,19},{19,18},{4,5},{5,4... | collective-permute-start | bytes 1572872 | tf_op jit(solution)/shard_map/ppermute | solution.py:346
  223.1 15.2 %collective-permute-start.53 = (bf16[256,1024]{1,0:T(8,128)(2,1)S(1)}, bf16[256,1024]{1,0:T(8,128)(2,1)S(1)}, u32[]{:S(2)}, u32[]{:S(2)}) collective-permute-start(bf16[256,1024]{1,0:T(8,128)(2,1)S(1)} %add_convert_fusion.6.passed), channel_id=1, source_target_pairs={{1,0},{3,2},{16,17},{18,19},{5,4},{7,6},{20,21},{22,23},{9,8},{11,... | collective-permute-start | bytes 1572872 | tf_op jit(solution)/shard_map/ppermute | solution.py:346
  240.4 14.0 %collective-permute-start.55 = (bf16[256,1024]{1,0:T(8,128)(2,1)S(1)}, bf16[256,1024]{1,0:T(8,128)(2,1)S(1)}, u32[]{:S(2)}, u32[]{:S(2)}) collective-permute-start(bf16[256,1024]{1,0:T(8,128)(2,1)S(1)} %add_convert_fusion.5.passed), channel_id=1, source_target_pairs={{0,1},{1,0},{2,3},{3,2},{16,17},{17,16},{18,19},{19,18},{4,5},{5,4... | collective-permute-start | bytes 1572872 | tf_op jit(solution)/shard_map/ppermute | solution.py:346
  256.6 14.0 %collective-permute-start.57 = (bf16[256,1024]{1,0:T(8,128)(2,1)S(1)}, bf16[256,1024]{1,0:T(8,128)(2,1)S(1)}, u32[]{:S(2)}, u32[]{:S(2)}) collective-permute-start(bf16[256,1024]{1,0:T(8,128)(2,1)S(1)} %add_convert_fusion.4.passed), channel_id=1, source_target_pairs={{0,1},{1,0},{2,3},{3,2},{16,17},{17,16},{18,19},{19,18},{4,5},{5,4... | collective-permute-start | bytes 1572872 | tf_op jit(solution)/shard_map/ppermute | solution.py:346
  323.8 18.4 %collective-permute-start.69 = (bf16[256,1024]{1,0:T(8,128)(2,1)S(1)}, bf16[256,1024]{1,0:T(8,128)(2,1)S(1)}, u32[]{:S(2)}, u32[]{:S(2)}) collective-permute-start(bf16[256,1024]{1,0:T(8,128)(2,1)S(1)} %add_convert_fusion.passed), channel_id=1, source_target_pairs={{1,0},{3,2},{16,17},{18,19},{5,4},{7,6},{20,21},{22,23},{9,8},{11,... | collective-permute-start | bytes 1572872 | tf_op jit(solution)/shard_map/ppermute | solution.py:346
  327.7 26.7 %collective-permute-start.75 = (bf16[256,1024]{1,0:T(8,128)(2,1)}, bf16[256,1024]{1,0:T(8,128)(2,1)}, u32[]{:S(2)}, u32[]{:S(2)}) collective-permute-start(bf16[256,1024]{1,0:T(8,128)(2,1)} %broadcast_select_fusion.6), channel_id=1, source_target_pairs={{0,18},{2,16},{17,19},{19,17},{4,22},{6,20},{21,23},{23,21},{8,26}... | collective-permute-start | bytes 1572872 | tf_op jit(solution)/shard_map/ppermute | solution.py:346
  338.5 18.2 %collective-permute-start.73 = (f32[256,1024]{1,0:T(8,128)S(1)}, f32[256,1024]{1,0:T(8,128)}, u32[]{:S(2)}, u32[]{:S(2)}) collective-permute-start(f32[256,1024]{1,0:T(8,128)S(1)} %broadcast_select_fusion.8), channel_id=1, source_target_pairs={{0,16},{2,18},{4,20},{6,22},{8,24},{10,26},{12,28},{14,30}} | collective-permute-start | bytes 3145736 | tf_op jit(solution)/shard_map/ppermute | solution.py:346
  (186 other events, 1837.2 us)
